TPU v7x, 512 devices: a whole 4x4x16 slice. The times are simulated.
512 devices in a mesh: gx: 2 (over y_hi), gy: 16 (over x, y_lo, core), gz: 16 (over z).
Axes of the slice: x: 4, y: 4 (y_hi: 2, y_lo: 2; y = y_hi * 2 + y_lo), z: 16, core: 2. Of those that a mesh axis runs over, the one named last changes fastest.
Arguments:
- positions: float32 [3, 32768], P(None, ('gx', 'gy', 'gz')), may hold values from 0 to 12, as said below
- species: int32 [32768], P(('gx', 'gy', 'gz')), may hold values from 0 to 88
- neighbors: int32 [32768, 64], P(('gx', 'gy', 'gz')), may hold values from 0 to 511, as said below
- neighbor_counts: int32 [32768], P(('gx', 'gy', 'gz')), may hold values from 1 to 64, as said below
- embedding: float32 [89, 128], replicated, may hold values from -6 to 6
- first_inner: float32 [8, 64], replicated, may hold values from -12 to 12
- first_outer: float32 [64, 256], replicated, may hold values from -0.75 to 0.75
- first_scalar: float32 [128, 128], replicated, may hold values from -0.5 to 0.5
- first_vector: float32 [128, 128], replicated, may hold values from -0.5 to 0.5
- first_square: float32 [128, 128], replicated, may hold values from -0.5 to 0.5
- second_inner: float32 [8, 64], replicated, may hold values from -12 to 12
- second_outer: float32 [64, 256], replicated, may hold values from -0.75 to 0.75
- second_mix: float32 [128, 128], replicated, may hold values from -0.5 to 0.5
- readout_first: float32 [128], replicated, may hold values from -0.5 to 0.5
- readout_second: float32 [128], replicated, may hold values from -0.5 to 0.5
Outputs:
- energies: float32 [32768], P(('gx', 'gy', 'gz'))
- forces: float32 [3, 32768], P(None, ('gx', 'gy', 'gz'))
Inputs may be any that keep to these rules, and one draw needn't show every extreme that they name: `positions`: atom n of a device lies in [6a, 6a + 6) x [6b, 6b + 6) x [6c, 6c + 6) with 4a + 2b + c = n // 8. `neighbors`: entries index the atom's extended set. `neighbor_counts`: every device has an atom with 64 live slots.
All inputs are finite; a program needn't handle non-finite values.
Results may differ from a plain program's by a relative error of at most 0.0003.
Values sent between devices are 32-bit elements; how exact they have to be, the bound alone decides.
No kernel may reach another device: no remote copies, remote signals or barrier semaphores. Data moves between devices by JAX's collectives and lax.ppermute only.
A program may use at most 64 MiB of HBM per device.

v0:
```python
import jax
import jax.numpy as jnp
from jax import lax
from jax.sharding import PartitionSpec as P

cutoff = 6.0
box_edge = 12.0
softening = 0.25
message_scale = 0.25
block_atoms = 16
highest = lax.Precision.HIGHEST


def padded(block, sides, width):
    for axis, dim in sides:
        count = lax.axis_size(axis)
        forward = [(i, i + 1) for i in range(count - 1)]
        forward.append((count - 1, 0))
        backward = [(target, source) for source, target in forward]
        low = lax.ppermute(
            lax.slice_in_dim(block, block.shape[dim] - width, None, axis=dim), axis, forward
        )
        high = lax.ppermute(lax.slice_in_dim(block, 0, width, axis=dim), axis, backward)
        block = jnp.concatenate([low, block, high], axis=dim)
    return block


def envelope(distance):
    scaled = distance / cutoff
    inside = 1.0 - 28.0 * scaled**6 + 48.0 * scaled**7 - 21.0 * scaled**8
    return jnp.where(scaled < 1.0, inside, 0.0)


def radial(distance, inner, outer):
    orders = jnp.arange(1, inner.shape[0] + 1).astype(jnp.float32)
    angles = jnp.pi / cutoff * distance[..., None] * orders
    bessel = jnp.sqrt(2.0 / cutoff) * jnp.sin(angles) / distance[..., None]
    bessel = bessel * envelope(distance)[..., None]
    hidden = jax.nn.silu(jnp.einsum("akn,nh->akh", bessel, inner, precision=highest))
    return jnp.einsum("akh,hc->akc", hidden, outer, precision=highest)


def geometry(ext_pos, own_pos, neighbor_ids):
    neighbor_pos = jnp.take(ext_pos, neighbor_ids, axis=1)
    separation = neighbor_pos - own_pos[:, :, None]
    distance = jnp.sqrt(jnp.sum(separation * separation, axis=0) + softening)
    return (separation / distance, distance)


def layer_one_block(ext_pos, ext_node, own_pos, own_node, neighbor_ids, live_mask, params):
    inner, outer, mix_scalar, mix_vector, mix_square = params
    channels = own_node.shape[1]
    unit_vec, distance = geometry(ext_pos, own_pos, neighbor_ids)
    weights = radial(distance, inner, outer) * live_mask[..., None]
    sender = jnp.take(ext_node, neighbor_ids, axis=0)
    scalar_msg = message_scale * jnp.sum(weights[..., :channels] * sender, axis=1)
    vector_msg = message_scale * jnp.einsum(
        "xak,akc->xac", unit_vec, weights[..., channels:] * sender, precision=highest
    )
    vector_out = jnp.einsum("xac,cd->xad", vector_msg, mix_vector, precision=highest)
    square = jnp.sum(vector_out * vector_out, axis=0)
    scalar_out = jax.nn.silu(
        jnp.dot(scalar_msg + own_node, mix_scalar, precision=highest)
        + jnp.dot(square, mix_square, precision=highest)
    )
    return jnp.concatenate([scalar_out, vector_out[0], vector_out[1], vector_out[2]], axis=1)


def layer_two_block(ext_pos, ext_feat, own_pos, own_feat, neighbor_ids, live_mask, params):
    inner, outer, mix_two, read_one, read_two = params
    channels = own_feat.shape[1] // 4
    unit_vec, distance = geometry(ext_pos, own_pos, neighbor_ids)
    weights = radial(distance, inner, outer) * live_mask[..., None]
    sender = jnp.take(ext_feat, neighbor_ids, axis=0)
    projected = unit_vec[0][..., None] * sender[..., channels : 2 * channels]
    projected = projected + unit_vec[1][..., None] * sender[..., 2 * channels : 3 * channels]
    projected = projected + unit_vec[2][..., None] * sender[..., 3 * channels :]
    message = message_scale * jnp.sum(
        weights[..., :channels] * sender[..., :channels] + weights[..., channels:] * projected,
        axis=1,
    )
    own_scalar = own_feat[:, :channels]
    hidden = jax.nn.silu(jnp.dot(message + own_scalar, mix_two, precision=highest))
    return jnp.dot(hidden, read_two, precision=highest) + jnp.dot(
        own_scalar, read_one, precision=highest
    )


def over_blocks(
    block_fn, ext_first, ext_second, own_pos, own_feat, neighbor_ids, neighbor_counts, params
):
    atom_count, slot_count = neighbor_ids.shape
    block_count = atom_count // block_atoms
    live_mask = (
        jnp.arange(slot_count, dtype=jnp.int32)[None, :] < neighbor_counts[:, None]
    ).astype(jnp.float32)
    checked = jax.checkpoint(block_fn)

    def one_block(block_item):
        pos_block, feat_block, id_block, mask_block = block_item
        return checked(ext_first, ext_second, pos_block, feat_block, id_block, mask_block, params)

    result = lax.map(
        one_block,
        (
            jnp.moveaxis(own_pos.reshape(3, block_count, block_atoms), 1, 0),
            own_feat.reshape(block_count, block_atoms, own_feat.shape[1]),
            neighbor_ids.reshape(block_count, block_atoms, slot_count),
            live_mask.reshape(block_count, block_atoms, slot_count),
        ),
    )
    return result.reshape((atom_count,) + result.shape[2:])


def offsets():
    shift_values = jnp.array([-box_edge, 0.0, 0.0, box_edge], dtype=jnp.float32)
    return jnp.stack(
        jnp.broadcast_arrays(
            shift_values[:, None, None], shift_values[None, :, None], shift_values[None, None, :]
        ),
        axis=-1,
    )


def embed_rows(species_float, species_codes, embedding):
    onehot = (species_float[:, None] == species_codes[None, :]).astype(jnp.float32)
    return jnp.dot(onehot, embedding, precision=highest)


def fold_back(widened, axis_pos):
    lower_sum = lax.index_in_dim(widened, 0, axis_pos, False) + lax.index_in_dim(
        widened, 2, axis_pos, False
    )
    upper_sum = lax.index_in_dim(widened, 3, axis_pos, False) + lax.index_in_dim(
        widened, 5, axis_pos, False
    )
    return jnp.stack([lower_sum, upper_sum], axis=axis_pos)


def across(payload, returning):
    widened = padded(payload, (("gx", 0), ("gy", 1), ("gz", 2)), 1)
    if returning:
        widened = fold_back(fold_back(fold_back(widened, 0), 1), 2)
    return widened


def send_back(grad_ext, octant):
    arranged = jnp.moveaxis(grad_ext.reshape(3, 4, 4, 4, octant), 0, 3)
    folded = across(arranged, True)
    return jnp.moveaxis(folded, 3, 0).reshape(3, 8 * octant)


def shards(
    positions,
    species,
    neighbors,
    neighbor_counts,
    embedding,
    first_inner,
    first_outer,
    first_scalar,
    first_vector,
    first_square,
    second_inner,
    second_outer,
    second_mix,
    readout_first,
    readout_second,
):
    atom_count = positions.shape[1]
    octant = atom_count // 8
    channels = embedding.shape[1]
    ext_count = 64 * octant
    species_codes = jnp.arange(embedding.shape[0]).astype(jnp.float32)
    species_float = species.astype(jnp.float32)
    own_node = embed_rows(species_float, species_codes, embedding)
    payload = jnp.moveaxis(
        jnp.concatenate([positions, species_float[None, :]], axis=0).reshape(4, 2, 2, 2, octant),
        0,
        3,
    )
    widened = across(payload, False)
    ext_pos = jnp.moveaxis(widened[:, :, :, :3, :] + offsets()[:, :, :, :, None], 3, 0).reshape(
        3, ext_count
    )
    ext_node = embed_rows(widened[:, :, :, 3, :].reshape(ext_count), species_codes, embedding)
    params_one = (first_inner, first_outer, first_scalar, first_vector, first_square)
    params_two = (second_inner, second_outer, second_mix, readout_first, readout_second)

    def first_map(ext_position, own_position):
        return over_blocks(
            layer_one_block,
            ext_position,
            ext_node,
            own_position,
            own_node,
            neighbors,
            neighbor_counts,
            params_one,
        )

    features, first_pull = jax.vjp(first_map, ext_pos, positions)
    ext_feat = across(features.reshape(2, 2, 2, octant, 4 * channels), False).reshape(
        ext_count, 4 * channels
    )

    def energy_fn(ext_position, ext_feature, own_position, own_feature):
        return over_blocks(
            layer_two_block,
            ext_position,
            ext_feature,
            own_position,
            own_feature,
            neighbors,
            neighbor_counts,
            params_two,
        )

    energies, pullback = jax.vjp(energy_fn, ext_pos, ext_feat, positions, features)
    grad_ext_pos, grad_ext_feat, grad_own_pos, grad_own_feat = pullback(jnp.ones_like(energies))
    returned = across(grad_ext_feat.reshape(4, 4, 4, octant, 4 * channels), True).reshape(
        atom_count, 4 * channels
    )
    feature_grad = returned + grad_own_feat
    early = send_back(grad_ext_pos, octant)
    grad_ext_first, grad_own_first = first_pull(feature_grad)
    total = grad_own_pos + early + grad_own_first + send_back(grad_ext_first, octant)
    return (energies, -total)


def solution(mesh):
    placed = (
        P(None, ("gx", "gy", "gz")),
        P(("gx", "gy", "gz")),
        P(("gx", "gy", "gz"), None),
        P(("gx", "gy", "gz")),
        P(),
        P(),
        P(),
        P(),
        P(),
        P(),
        P(),
        P(),
        P(),
        P(),
        P(),
    )
    return jax.shard_map(
        shards,
        mesh=mesh,
        in_specs=placed,
        out_specs=(P(("gx", "gy", "gz")), P(None, ("gx", "gy", "gz"))),
        check_vma=False,
    )
```

profile of v0, /device:TPU:16, one launch (start us, length us, event | category | flops | bytes accessed | tf_op | source)
XLA Modules:
  0.0 613.8 jit_solution(11413522588564274188)
XLA Ops:
  2.3 7.6 %collective-permute-start = (f32[1,2,2,4,8]{4,2,1,0,3:T(2,128)S(1)}, f32[1,2,2,4,8]{4,2,1,0,3:T(2,128)S(1)}, u32[]{:S(2)}, u32[]{:S(2)}) collective-permute-start(f32[1,2,2,4,8]{4,2,1,0,3:T(2,128)S(1)} %get-tuple-element.1330), channel_id=1, source_target_pairs={{0,256},{256,0},{1,257},{257,1},{2,258},{258,2},{3,259},{259,3},{4... | collective-permute-start | bytes 1544 | tf_op jit(solution)/shard_map/ppermute | solution.py:20
  12.9 4.1 collective-permute-done.1
  19.0 5.8 collective-permute-start.3
  28.2 6.0 collective-permute-start.5
  39.6 53.4 %while.62 = (s32[]{:T(128)}, f32[4,16,512]{2,1,0:T(8,128)}, s32[4,16,64]{2,1,0:T(8,128)}, f32[3,512]{0,1:T(8,128)S(1)}, f32[4,3,16]{2,1,0:T(4,128)}, /*index=5*/...) while((s32[]{:T(128)}, f32[4,16,512]{2,1,0:T(8,128)}, ...), condition=%wide.region_4.6_spmd.clone, body=%wide.region_0.5_spmd.clone.sunk | while | flops 229380112 | bytes 5458585 | solution.py:103
  53.7 2.8 gather_fusion.4
  61.4 2.8 gather_fusion.5
  80.4 2.8 gather_fusion.4
  88.0 2.8 gather_fusion.5
  93.9 5.1 collective-permute-start.6
  101.6 5.1 collective-permute-done.7
  109.6 5.8 collective-permute-start.9
  120.8 5.3 collective-permute-start.11
  133.2 180.0 %while.60 = (s32[]{:T(128)}, f32[3,512]{0,1:T(8,128)}, f32[512,512]{1,0:T(8,128)S(1)}, f32[4,3,16]{2,1,0:T(4,128)}, f32[4,16,512]{2,1,0:T(8,128)}, /*index=5*/f3...) while((s32[]{:T(128)}, f32[3,512]{0,1:T(8,128)}, ...), condition=%wide.region_22.25_spmd, body=%wide.region_9.24_spmd.sunk | while | flops 428974080 | bytes 43390080 | solution.py:103
  136.7 4.9 gather_fusion
  141.6 3.2 broadcast_select_fusion.4
  144.8 2.8 gather_fusion.1
  157.8 7.6 %scatter_fusion.1 = f32[512,512]{1,0:T(8,128)S(1)} fusion(f32[512,512]{1,0:T(8,128)S(1)} %get-tuple-element.1960, s32[1024]{0:T(1024)} %copy-done.28, f32[1024,512]{1,0:T(8,128)} %bitcast.465), kind=kCustom, calls=%fused_computation.9.clone.1 | custom fusion | flops 524288 | bytes 6295552 | tf_op jit(solution)/shard_map/transpose(jvp())/while/body/eval_jaxpr/checkpoint/jit(_take)/scatter-add | solution.py:74
  170.8 6.1 %scatter_fusion = f32[3,512]{0,1:T(8,128)S(1)} fusion(f32[3,512]{0,1:T(8,128)S(1)} %copy-done.12, s32[1024]{0:T(1024)S(1)} %reshape.679, f32[1024,3]{1,0:T(8,128)S(1)} %bitcast.471), kind=kCustom, calls=%fused_computation.8.clone.1 | custom fusion | flops 3072 | bytes 40960 | tf_op jit(solution)/shard_map/transpose(jvp())/while/body/eval_jaxpr/checkpoint/jit(_take)/scatter-add | solution.py:44
  181.7 4.9 gather_fusion
  186.7 3.2 broadcast_select_fusion.4
  202.9 7.6 %scatter_fusion.1 = f32[512,512]{1,0:T(8,128)S(1)} fusion(f32[512,512]{1,0:T(8,128)S(1)} %get-tuple-element.1960, s32[1024]{0:T(1024)} %copy-done.28, f32[1024,512]{1,0:T(8,128)} %bitcast.465), kind=kCustom, calls=%fused_computation.9.clone.1 | custom fusion | flops 524288 | bytes 6295552 | tf_op jit(solution)/shard_map/transpose(jvp())/while/body/eval_jaxpr/checkpoint/jit(_take)/scatter-add | solution.py:74
  215.8 6.1 %scatter_fusion = f32[3,512]{0,1:T(8,128)S(1)} fusion(f32[3,512]{0,1:T(8,128)S(1)} %copy-done.12, s32[1024]{0:T(1024)S(1)} %reshape.679, f32[1024,3]{1,0:T(8,128)S(1)} %bitcast.471), kind=kCustom, calls=%fused_computation.8.clone.1 | custom fusion | flops 3072 | bytes 40960 | tf_op jit(solution)/shard_map/transpose(jvp())/while/body/eval_jaxpr/checkpoint/jit(_take)/scatter-add | solution.py:44
  226.7 4.9 gather_fusion
  231.7 3.2 broadcast_select_fusion.4
  234.8 2.8 gather_fusion.1
  247.9 7.6 %scatter_fusion.1 = f32[512,512]{1,0:T(8,128)S(1)} fusion(f32[512,512]{1,0:T(8,128)S(1)} %get-tuple-element.1960, s32[1024]{0:T(1024)} %copy-done.28, f32[1024,512]{1,0:T(8,128)} %bitcast.465), kind=kCustom, calls=%fused_computation.9.clone.1 | custom fusion | flops 524288 | bytes 6295552 | tf_op jit(solution)/shard_map/transpose(jvp())/while/body/eval_jaxpr/checkpoint/jit(_take)/scatter-add | solution.py:74
  260.8 6.1 %scatter_fusion = f32[3,512]{0,1:T(8,128)S(1)} fusion(f32[3,512]{0,1:T(8,128)S(1)} %copy-done.12, s32[1024]{0:T(1024)S(1)} %reshape.679, f32[1024,3]{1,0:T(8,128)S(1)} %bitcast.471), kind=kCustom, calls=%fused_computation.8.clone.1 | custom fusion | flops 3072 | bytes 40960 | tf_op jit(solution)/shard_map/transpose(jvp())/while/body/eval_jaxpr/checkpoint/jit(_take)/scatter-add | solution.py:44
  271.7 4.9 gather_fusion
  276.6 3.2 broadcast_select_fusion.4
  292.8 7.6 %scatter_fusion.1 = f32[512,512]{1,0:T(8,128)S(1)} fusion(f32[512,512]{1,0:T(8,128)S(1)} %get-tuple-element.1960, s32[1024]{0:T(1024)} %copy-done.28, f32[1024,512]{1,0:T(8,128)} %bitcast.465), kind=kCustom, calls=%fused_computation.9.clone.1 | custom fusion | flops 524288 | bytes 6295552 | tf_op jit(solution)/shard_map/transpose(jvp())/while/body/eval_jaxpr/checkpoint/jit(_take)/scatter-add | solution.py:74
  305.8 6.1 %scatter_fusion = f32[3,512]{0,1:T(8,128)S(1)} fusion(f32[3,512]{0,1:T(8,128)S(1)} %copy-done.12, s32[1024]{0:T(1024)S(1)} %reshape.679, f32[1024,3]{1,0:T(8,128)S(1)} %bitcast.471), kind=kCustom, calls=%fused_computation.8.clone.1 | custom fusion | flops 3072 | bytes 40960 | tf_op jit(solution)/shard_map/transpose(jvp())/while/body/eval_jaxpr/checkpoint/jit(_take)/scatter-add | solution.py:44
  316.5 5.0 collective-permute-start.19
  322.9 2.9 collective-permute-done.18
  325.9 2.8 collective-permute-done.19
  331.6 5.8 collective-permute-start.21
  337.4 3.4 collective-permute-start.12
  340.8 4.0 collective-permute-start.13
  344.9 3.1 collective-permute-done.13
  350.6 5.8 collective-permute-start.15
  361.8 5.6 collective-permute-start.17
  371.6 5.1 collective-permute-start.23
  376.7 94.2 %while.63 = (s32[]{:T(128)}, f32[4,16]{1,0:T(4,128)}, s32[4,16,64]{2,1,0:T(8,128)}, f32[3,512]{0,1:T(8,128)S(1)}, f32[4,3,16]{2,1,0:T(4,128)}, /*index=5*/f32[8,...) while((s32[]{:T(128)}, f32[4,16]{1,0:T(4,128)}, ...), condition=%wide.region_8.10_spmd.clone, body=%wide.region_5.9_spmd.clone.sunk | while | flops 213133344 | bytes 13591269 | solution.py:103
  389.2 4.9 gather_fusion.6
  401.1 2.8 gather_fusion.7
  412.8 4.9 gather_fusion.6
  436.3 4.9 gather_fusion.6
  448.2 2.8 gather_fusion.7
  459.9 4.9 gather_fusion.6
  480.4 102.2 %while.61 = (s32[]{:T(128)}, f32[3,512]{0,1:T(8,128)S(1)}, f32[4,3,16]{2,1,0:T(4,128)}, f32[4,3,16]{2,1,0:T(4,128)}, f32[4,16,128]{2,1,0:T(8,128)}, /*index=5*/s...) while((s32[]{:T(128)}, f32[3,512]{0,1:T(8,128)S(1)}, ...), condition=%wide.region_33.36_spmd, body=%wide.region_23.35_spmd.sunk | while | flops 464281600 | bytes 11164385 | solution.py:103
  483.3 2.8 gather_fusion.2
  488.8 2.8 gather_fusion.3
  499.2 6.1 %scatter_fusion.2 = f32[3,512]{0,1:T(8,128)S(1)} fusion(f32[3,512]{0,1:T(8,128)S(1)} %get-tuple-element.2014, s32[1024]{0:T(1024)S(1)} %reshape.687, f32[1024,3]{1,0:T(8,128)S(1)} %bitcast.470), kind=kCustom, calls=%fused_computation.10.clone.1 | custom fusion | flops 3072 | bytes 40960 | tf_op jit(solution)/shard_map/transpose(jvp())/while/body/eval_jaxpr/checkpoint/jit(_take)/scatter-add | solution.py:44
  514.4 2.8 gather_fusion.3
  524.7 6.1 %scatter_fusion.2 = f32[3,512]{0,1:T(8,128)S(1)} fusion(f32[3,512]{0,1:T(8,128)S(1)} %get-tuple-element.2014, s32[1024]{0:T(1024)S(1)} %reshape.687, f32[1024,3]{1,0:T(8,128)S(1)} %bitcast.470), kind=kCustom, calls=%fused_computation.10.clone.1 | custom fusion | flops 3072 | bytes 40960 | tf_op jit(solution)/shard_map/transpose(jvp())/while/body/eval_jaxpr/checkpoint/jit(_take)/scatter-add | solution.py:44
  539.9 2.8 gather_fusion.3
  550.3 6.1 %scatter_fusion.2 = f32[3,512]{0,1:T(8,128)S(1)} fusion(f32[3,512]{0,1:T(8,128)S(1)} %get-tuple-element.2014, s32[1024]{0:T(1024)S(1)} %reshape.687, f32[1024,3]{1,0:T(8,128)S(1)} %bitcast.470), kind=kCustom, calls=%fused_computation.10.clone.1 | custom fusion | flops 3072 | bytes 40960 | tf_op jit(solution)/shard_map/transpose(jvp())/while/body/eval_jaxpr/checkpoint/jit(_take)/scatter-add | solution.py:44
  565.5 2.8 gather_fusion.3
  575.8 6.1 %scatter_fusion.2 = f32[3,512]{0,1:T(8,128)S(1)} fusion(f32[3,512]{0,1:T(8,128)S(1)} %get-tuple-element.2014, s32[1024]{0:T(1024)S(1)} %reshape.687, f32[1024,3]{1,0:T(8,128)S(1)} %bitcast.470), kind=kCustom, calls=%fused_computation.10.clone.1 | custom fusion | flops 3072 | bytes 40960 | tf_op jit(solution)/shard_map/transpose(jvp())/while/body/eval_jaxpr/checkpoint/jit(_take)/scatter-add | solution.py:44
  583.1 4.2 collective-permute-start.24
  587.4 3.2 collective-permute-start.25
  591.3 3.3 collective-permute-done.25
  596.5 5.8 collective-permute-start.27
  605.9 5.1 collective-permute-start.29
  (794 shorter events, 331.9 us)
Async XLA Ops:
  0.6 11.3 %copy-start = (f32[89,128]{1,0:T(8,128)S(1)}, f32[89,128]{1,0:T(8,128)}, u32[]{:S(2)}) copy-start(f32[89,128]{1,0:T(8,128)} %param.32) | copy-start | bytes 136708
  0.6 38.9 %copy-start.40 = (f32[8,64]{1,0:T(8,128)S(1)}, f32[8,64]{1,0:T(8,128)}, u32[]{:S(2)}) copy-start(f32[8,64]{1,0:T(8,128)} %param.33) | copy-start | bytes 6148
  0.7 38.9 %copy-start.29 = (f32[64,256]{1,0:T(8,128)S(1)}, f32[64,256]{1,0:T(8,128)}, u32[]{:S(2)}) copy-start(f32[64,256]{1,0:T(8,128)} %param.34) | copy-start | bytes 196612
  0.7 38.9 %copy-start.5 = (f32[128,128]{1,0:T(8,128)S(1)}, f32[128,128]{1,0:T(8,128)}, u32[]{:S(2)}) copy-start(f32[128,128]{1,0:T(8,128)} %param.35) | copy-start | bytes 196612
  0.7 38.9 %copy-start.9 = (f32[128,128]{1,0:T(8,128)S(1)}, f32[128,128]{1,0:T(8,128)}, u32[]{:S(2)}) copy-start(f32[128,128]{1,0:T(8,128)} %param.36) | copy-start | bytes 196612
  0.7 38.9 %copy-start.7 = (f32[128,128]{1,0:T(8,128)S(1)}, f32[128,128]{1,0:T(8,128)}, u32[]{:S(2)}) copy-start(f32[128,128]{1,0:T(8,128)} %param.37) | copy-start | bytes 196612
  2.3 10.5 %collective-permute-start = (f32[1,2,2,4,8]{4,2,1,0,3:T(2,128)S(1)}, f32[1,2,2,4,8]{4,2,1,0,3:T(2,128)S(1)}, u32[]{:S(2)}, u32[]{:S(2)}) collective-permute-start(f32[1,2,2,4,8]{4,2,1,0,3:T(2,128)S(1)} %get-tuple-element.1330), channel_id=1, source_target_pairs={{0,256},{256,0},{1,257},{257,1},{2,258},{258,2},{3,259},{259,3},{4... | collective-permute-start | bytes 1544 | tf_op jit(solution)/shard_map/ppermute | solution.py:20
  10.0 7.0 %collective-permute-start.1 = (f32[1,2,2,4,8]{4,2,1,0,3:T(2,128)S(1)}, f32[1,2,2,4,8]{4,2,1,0,3:T(2,128)S(1)}, u32[]{:S(2)}, u32[]{:S(2)}) collective-permute-start(f32[1,2,2,4,8]{4,2,1,0,3:T(2,128)S(1)} %get-tuple-element.1331), channel_id=1, source_target_pairs={{256,0},{0,256},{257,1},{1,257},{258,2},{2,258},{259,3},{3,259},{2... | collective-permute-start | bytes 1544 | tf_op jit(solution)/shard_map/ppermute | solution.py:23
  17.1 8.4 %collective-permute-start.2 = (f32[4,1,2,4,8]{4,2,1,0,3:T(2,128)S(1)}, f32[4,1,2,4,8]{4,2,1,0,3:T(2,128)S(1)}, u32[]{:S(2)}, u32[]{:S(2)}) collective-permute-start(f32[4,1,2,4,8]{4,2,1,0,3:T(2,128)S(1)} %get-tuple-element.1328), channel_id=1, source_target_pairs={{0,16},{16,32},{32,48},{48,64},{64,80},{80,96},{96,112},{112,128},... | collective-permute-start | bytes 3080 | tf_op jit(solution)/shard_map/ppermute | solution.py:20
  19.0 7.2 %collective-permute-start.3 = (f32[4,1,2,4,8]{4,2,1,0,3:T(2,128)S(1)}, f32[4,1,2,4,8]{4,2,1,0,3:T(2,128)S(1)}, u32[]{:S(2)}, u32[]{:S(2)}) collective-permute-start(f32[4,1,2,4,8]{4,2,1,0,3:T(2,128)S(1)} %get-tuple-element.1329), channel_id=1, source_target_pairs={{16,0},{32,16},{48,32},{64,48},{80,64},{96,80},{112,96},{128,112},... | collective-permute-start | bytes 3080 | tf_op jit(solution)/shard_map/ppermute | solution.py:23
  26.3 11.5 %collective-permute-start.4 = (f32[4,4,1,4,8]{4,2,1,0,3:T(1,128)S(1)}, f32[4,4,1,4,8]{4,2,1,0,3:T(1,128)S(1)}, u32[]{:S(2)}, u32[]{:S(2)}) collective-permute-start(f32[4,4,1,4,8]{4,2,1,0,3:T(1,128)S(1)} %get-tuple-element.1322), channel_id=1, source_target_pairs={{0,1},{1,2},{2,3},{3,4},{4,5},{5,6},{6,7},{7,8},{8,9},{9,10},{10,1... | collective-permute-start | bytes 6152 | tf_op jit(solution)/shard_map/ppermute | solution.py:20
  28.2 9.5 %collective-permute-start.5 = (f32[4,4,1,4,8]{4,2,1,0,3:T(1,128)S(1)}, f32[4,4,1,4,8]{4,2,1,0,3:T(1,128)S(1)}, u32[]{:S(2)}, u32[]{:S(2)}) collective-permute-start(f32[4,4,1,4,8]{4,2,1,0,3:T(1,128)S(1)} %get-tuple-element.1323), channel_id=1, source_target_pairs={{1,0},{2,1},{3,2},{4,3},{5,4},{6,5},{7,6},{8,7},{9,8},{10,9},{11,1... | collective-permute-start | bytes 6152 | tf_op jit(solution)/shard_map/ppermute | solution.py:23
  92.9 16.7 %copy-start.42 = (f32[4,16,128]{2,1,0:T(8,128)}, f32[4,16,128]{2,1,0:T(8,128)S(1)}, u32[]{:S(2)}) copy-start(f32[4,16,128]{2,1,0:T(8,128)S(1)} %get-tuple-element.2065) | copy-start | bytes 98308
  92.9 35.9 %copy-start.1 = (f32[512,128]{1,0:T(8,128)}, f32[512,128]{1,0:T(8,128)S(1)}, u32[]{:S(2)}) copy-start(f32[512,128]{1,0:T(8,128)S(1)} %get-tuple-element.2048) | copy-start | bytes 786436
  93.9 7.7 %collective-permute-start.6 = (f32[1,2,2,8,512]{4,3,2,1,0:T(8,128)S(1)}, f32[1,2,2,8,512]{4,3,2,1,0:T(8,128)S(1)}, u32[]{:S(2)}, u32[]{:S(2)}) collective-permute-start(f32[1,2,2,8,512]{4,3,2,1,0:T(8,128)S(1)} %get-tuple-element.1316), channel_id=1, source_target_pairs={{0,256},{256,0},{1,257},{257,1},{2,258},{258,2},{3,259},{259,3},{4... | collective-permute-start | bytes 196616 | tf_op jit(solution)/shard_map/ppermute | solution.py:20
  99.0 7.7 %collective-permute-start.7 = (f32[1,2,2,8,512]{4,3,2,1,0:T(8,128)S(1)}, f32[1,2,2,8,512]{4,3,2,1,0:T(8,128)S(1)}, u32[]{:S(2)}, u32[]{:S(2)}) collective-permute-start(f32[1,2,2,8,512]{4,3,2,1,0:T(8,128)S(1)} %get-tuple-element.1317), channel_id=1, source_target_pairs={{256,0},{0,256},{257,1},{1,257},{258,2},{2,258},{259,3},{3,259},{2... | collective-permute-start | bytes 196616 | tf_op jit(solution)/shard_map/ppermute | solution.py:23
  107.7 8.5 %collective-permute-start.8 = (f32[4,1,2,8,512]{4,3,2,1,0:T(8,128)S(1)}, f32[4,1,2,8,512]{4,3,2,1,0:T(8,128)S(1)}, u32[]{:S(2)}, u32[]{:S(2)}) collective-permute-start(f32[4,1,2,8,512]{4,3,2,1,0:T(8,128)S(1)} %get-tuple-element.1302), channel_id=1, source_target_pairs={{0,16},{16,32},{32,48},{48,64},{64,80},{80,96},{96,112},{112,128},... | collective-permute-start | bytes 393224 | tf_op jit(solution)/shard_map/ppermute | solution.py:20
  109.6 8.3 %collective-permute-start.9 = (f32[4,1,2,8,512]{4,3,2,1,0:T(8,128)S(1)}, f32[4,1,2,8,512]{4,3,2,1,0:T(8,128)S(1)}, u32[]{:S(2)}, u32[]{:S(2)}) collective-permute-start(f32[4,1,2,8,512]{4,3,2,1,0:T(8,128)S(1)} %get-tuple-element.1303), channel_id=1, source_target_pairs={{16,0},{32,16},{48,32},{64,48},{80,64},{96,80},{112,96},{128,112},... | collective-permute-start | bytes 393224 | tf_op jit(solution)/shard_map/ppermute | solution.py:23
  118.8 14.4 %copy-start.4 = (f32[128,128]{1,0:T(8,128)S(1)}, f32[128,128]{1,0:T(8,128)}, u32[]{:S(2)}) copy-start(f32[128,128]{1,0:T(8,128)} %param.40) | copy-start | bytes 196612
  118.8 10.0 %collective-permute-start.10 = (f32[4,4,1,8,512]{4,3,2,1,0:T(8,128)S(1)}, f32[4,4,1,8,512]{4,3,2,1,0:T(8,128)S(1)}, u32[]{:S(2)}, u32[]{:S(2)}) collective-permute-start(f32[4,4,1,8,512]{4,3,2,1,0:T(8,128)S(1)} %get-tuple-element.1298), channel_id=1, source_target_pairs={{0,1},{1,2},{2,3},{3,4},{4,5},{5,6},{6,7},{7,8},{8,9},{9,10},{10,1... | collective-permute-start | bytes 786440 | tf_op jit(solution)/shard_map/ppermute | solution.py:20
  120.8 9.3 %collective-permute-start.11 = (f32[4,4,1,8,512]{4,3,2,1,0:T(8,128)S(1)}, f32[4,4,1,8,512]{4,3,2,1,0:T(8,128)S(1)}, u32[]{:S(2)}, u32[]{:S(2)}) collective-permute-start(f32[4,4,1,8,512]{4,3,2,1,0:T(8,128)S(1)} %get-tuple-element.1299), channel_id=1, source_target_pairs={{1,0},{2,1},{3,2},{4,3},{5,4},{6,5},{7,6},{8,7},{9,8},{10,9},{11,1... | collective-permute-start | bytes 786440 | tf_op jit(solution)/shard_map/ppermute | solution.py:23
  135.3 15.1 %copy-start.35 = (f32[16,64]{1,0:T(8,128)}, f32[16,64]{1,0:T(8,128)S(1)}, u32[]{:S(2)}) copy-start(f32[16,64]{1,0:T(8,128)S(1)} %dynamic-slice_bitcast_fusion.31) | copy-start | bytes 12292 | tf_op jit(solution)/shard_map/transpose(jvp())/while
  136.0 16.4 %copy-start.31 = (f32[3,16]{1,0:T(4,128)}, f32[3,16]{1,0:T(4,128)S(1)}, u32[]{:S(2)}) copy-start(f32[3,16]{1,0:T(4,128)S(1)} %dynamic-slice_bitcast_fusion.28) | copy-start | bytes 580 | tf_op jit(solution)/shard_map/transpose(jvp())/while
  141.6 10.8 %copy-start.24 = (pred[16,64]{1,0:T(8,128)(4,1)}, pred[16,64]{1,0:T(8,128)(4,1)S(1)}, u32[]{:S(2)}) copy-start(pred[16,64]{1,0:T(8,128)(4,1)S(1)} %compare_and_fusion.8) | copy-start | bytes 3076 | tf_op jit(solution)/shard_map/transpose(jvp())/while
  147.9 5.1 copy-start.26
  167.5 10.1 %copy-start.38 = (f32[16,128]{1,0:T(8,128)S(1)}, f32[16,128]{1,0:T(8,128)}, u32[]{:S(2)}) copy-start(f32[16,128]{1,0:T(8,128)} %get-tuple-element.1762) | copy-start | bytes 24580 | tf_op jit(solution)/shard_map/transpose(jvp())/while
  180.4 15.1 %copy-start.35 = (f32[16,64]{1,0:T(8,128)}, f32[16,64]{1,0:T(8,128)S(1)}, u32[]{:S(2)}) copy-start(f32[16,64]{1,0:T(8,128)S(1)} %dynamic-slice_bitcast_fusion.31) | copy-start | bytes 12292 | tf_op jit(solution)/shard_map/transpose(jvp())/while
  181.0 16.4 %copy-start.31 = (f32[3,16]{1,0:T(4,128)}, f32[3,16]{1,0:T(4,128)S(1)}, u32[]{:S(2)}) copy-start(f32[3,16]{1,0:T(4,128)S(1)} %dynamic-slice_bitcast_fusion.28) | copy-start | bytes 580 | tf_op jit(solution)/shard_map/transpose(jvp())/while
  186.6 10.8 %copy-start.24 = (pred[16,64]{1,0:T(8,128)(4,1)}, pred[16,64]{1,0:T(8,128)(4,1)S(1)}, u32[]{:S(2)}) copy-start(pred[16,64]{1,0:T(8,128)(4,1)S(1)} %compare_and_fusion.8) | copy-start | bytes 3076 | tf_op jit(solution)/shard_map/transpose(jvp())/while
  192.9 5.1 copy-start.26
  212.5 10.1 %copy-start.38 = (f32[16,128]{1,0:T(8,128)S(1)}, f32[16,128]{1,0:T(8,128)}, u32[]{:S(2)}) copy-start(f32[16,128]{1,0:T(8,128)} %get-tuple-element.1762) | copy-start | bytes 24580 | tf_op jit(solution)/shard_map/transpose(jvp())/while
  225.4 15.1 %copy-start.35 = (f32[16,64]{1,0:T(8,128)}, f32[16,64]{1,0:T(8,128)S(1)}, u32[]{:S(2)}) copy-start(f32[16,64]{1,0:T(8,128)S(1)} %dynamic-slice_bitcast_fusion.31) | copy-start | bytes 12292 | tf_op jit(solution)/shard_map/transpose(jvp())/while
  226.1 16.4 %copy-start.31 = (f32[3,16]{1,0:T(4,128)}, f32[3,16]{1,0:T(4,128)S(1)}, u32[]{:S(2)}) copy-start(f32[3,16]{1,0:T(4,128)S(1)} %dynamic-slice_bitcast_fusion.28) | copy-start | bytes 580 | tf_op jit(solution)/shard_map/transpose(jvp())/while
  231.7 10.8 %copy-start.24 = (pred[16,64]{1,0:T(8,128)(4,1)}, pred[16,64]{1,0:T(8,128)(4,1)S(1)}, u32[]{:S(2)}) copy-start(pred[16,64]{1,0:T(8,128)(4,1)S(1)} %compare_and_fusion.8) | copy-start | bytes 3076 | tf_op jit(solution)/shard_map/transpose(jvp())/while
  257.5 10.1 %copy-start.38 = (f32[16,128]{1,0:T(8,128)S(1)}, f32[16,128]{1,0:T(8,128)}, u32[]{:S(2)}) copy-start(f32[16,128]{1,0:T(8,128)} %get-tuple-element.1762) | copy-start | bytes 24580 | tf_op jit(solution)/shard_map/transpose(jvp())/while
  270.4 15.1 %copy-start.35 = (f32[16,64]{1,0:T(8,128)}, f32[16,64]{1,0:T(8,128)S(1)}, u32[]{:S(2)}) copy-start(f32[16,64]{1,0:T(8,128)S(1)} %dynamic-slice_bitcast_fusion.31) | copy-start | bytes 12292 | tf_op jit(solution)/shard_map/transpose(jvp())/while
  271.0 16.4 %copy-start.31 = (f32[3,16]{1,0:T(4,128)}, f32[3,16]{1,0:T(4,128)S(1)}, u32[]{:S(2)}) copy-start(f32[3,16]{1,0:T(4,128)S(1)} %dynamic-slice_bitcast_fusion.28) | copy-start | bytes 580 | tf_op jit(solution)/shard_map/transpose(jvp())/while
  276.6 10.8 %copy-start.24 = (pred[16,64]{1,0:T(8,128)(4,1)}, pred[16,64]{1,0:T(8,128)(4,1)S(1)}, u32[]{:S(2)}) copy-start(pred[16,64]{1,0:T(8,128)(4,1)S(1)} %compare_and_fusion.8) | copy-start | bytes 3076 | tf_op jit(solution)/shard_map/transpose(jvp())/while
  302.5 10.1 %copy-start.38 = (f32[16,128]{1,0:T(8,128)S(1)}, f32[16,128]{1,0:T(8,128)}, u32[]{:S(2)}) copy-start(f32[16,128]{1,0:T(8,128)} %get-tuple-element.1762) | copy-start | bytes 24580 | tf_op jit(solution)/shard_map/transpose(jvp())/while
  313.9 12.0 %collective-permute-start.18 = (f32[1,4,4,8,512]{4,3,2,1,0:T(8,128)}, f32[1,4,4,8,512]{4,3,2,1,0:T(8,128)S(1)}, u32[]{:S(2)}, u32[]{:S(2)}) collective-permute-start(f32[1,4,4,8,512]{4,3,2,1,0:T(8,128)} %bitcast.57), channel_id=1, source_target_pairs={{0,256},{256,0},{1,257},{257,1},{2,258},{258,2},{3,259},{259,3},{4... | collective-permute-start | bytes 786440 | tf_op jit(solution)/shard_map/ppermute | solution.py:20
  316.5 12.2 %collective-permute-start.19 = (f32[1,4,4,8,512]{4,3,2,1,0:T(8,128)S(1)}, f32[1,4,4,8,512]{4,3,2,1,0:T(8,128)S(1)}, u32[]{:S(2)}, u32[]{:S(2)}) collective-permute-start(f32[1,4,4,8,512]{4,3,2,1,0:T(8,128)S(1)} %bitcast.498), channel_id=1, source_target_pairs={{256,0},{0,256},{257,1},{1,257},{258,2},{2,258},{259,3},{3,259},{2... | collective-permute-start | bytes 786440 | tf_op jit(solution)/shard_map/ppermute | solution.py:23
  322.9 46.7 %copy-start.20 = (f32[3,4,4,4,8]{4,3,2,1,0:T(4,128)}, f32[3,4,4,4,8]{4,3,2,1,0:T(4,128)S(1)}, u32[]{:S(2)}) copy-start(f32[3,4,4,4,8]{4,3,2,1,0:T(4,128)S(1)} %copy.93) | copy-start | bytes 18436
  325.9 43.7 %copy-start.14 = (f32[1,4,4,8,512]{4,3,2,1,0:T(8,128)}, f32[1,4,4,8,512]{4,3,2,1,0:T(8,128)S(1)}, u32[]{:S(2)}) copy-start(f32[1,4,4,8,512]{4,3,2,1,0:T(8,128)S(1)} %collective-permute-done.18) | copy-start | bytes 786436
  328.7 40.9 %copy-start.16 = (f32[1,4,4,8,512]{4,3,2,1,0:T(8,128)}, f32[1,4,4,8,512]{4,3,2,1,0:T(8,128)S(1)}, u32[]{:S(2)}) copy-start(f32[1,4,4,8,512]{4,3,2,1,0:T(8,128)S(1)} %collective-permute-done.19) | copy-start | bytes 786436
  329.7 37.7 %collective-permute-start.20 = (f32[6,1,4,8,512]{4,3,2,1,0:T(8,128)}, f32[6,1,4,8,512]{4,3,2,1,0:T(8,128)S(1)}, u32[]{:S(2)}, u32[]{:S(2)}) collective-permute-start(f32[6,1,4,8,512]{4,3,2,1,0:T(8,128)} %get-tuple-element.1292), channel_id=1, source_target_pairs={{0,16},{16,32},{32,48},{48,64},{64,80},{80,96},{96,112},{112,128},... | collective-permute-start | bytes 1179656 | tf_op jit(solution)/shard_map/ppermute | solution.py:20
  331.6 35.8 %collective-permute-start.21 = (f32[6,1,4,8,512]{4,3,2,1,0:T(8,128)}, f32[6,1,4,8,512]{4,3,2,1,0:T(8,128)}, u32[]{:S(2)}, u32[]{:S(2)}) collective-permute-start(f32[6,1,4,8,512]{4,3,2,1,0:T(8,128)} %get-tuple-element.1293), channel_id=1, source_target_pairs={{16,0},{32,16},{48,32},{64,48},{80,64},{96,80},{112,96},{128,112},... | collective-permute-start | bytes 1179656 | tf_op jit(solution)/shard_map/ppermute | solution.py:23
  337.4 7.6 %collective-permute-start.12 = (f32[1,4,4,3,8]{4,2,1,0,3:T(4,128)S(1)}, f32[1,4,4,3,8]{4,2,1,0,3:T(4,128)S(1)}, u32[]{:S(2)}, u32[]{:S(2)}) collective-permute-start(f32[1,4,4,3,8]{4,2,1,0,3:T(4,128)S(1)} %get-tuple-element.1318), channel_id=1, source_target_pairs={{0,256},{256,0},{1,257},{257,1},{2,258},{258,2},{3,259},{259,3},{4... | collective-permute-start | bytes 4616 | tf_op jit(solution)/shard_map/ppermute | solution.py:20
  340.8 7.2 %collective-permute-start.13 = (f32[1,4,4,3,8]{4,2,1,0,3:T(4,128)S(1)}, f32[1,4,4,3,8]{4,2,1,0,3:T(4,128)S(1)}, u32[]{:S(2)}, u32[]{:S(2)}) collective-permute-start(f32[1,4,4,3,8]{4,2,1,0,3:T(4,128)S(1)} %get-tuple-element.1319), channel_id=1, source_target_pairs={{256,0},{0,256},{257,1},{1,257},{258,2},{2,258},{259,3},{3,259},{2... | collective-permute-start | bytes 4616 | tf_op jit(solution)/shard_map/ppermute | solution.py:23
  344.9 31.8 %copy-start.43 = (f32[1,4,4,3,8]{4,2,1,0,3:T(4,128)}, f32[1,4,4,3,8]{4,2,1,0,3:T(4,128)S(1)}, u32[]{:S(2)}) copy-start(f32[1,4,4,3,8]{4,2,1,0,3:T(4,128)S(1)} %collective-permute-done.12) | copy-start | bytes 4612
  348.0 28.7 %copy-start.44 = (f32[1,4,4,3,8]{4,2,1,0,3:T(4,128)}, f32[1,4,4,3,8]{4,2,1,0,3:T(4,128)S(1)}, u32[]{:S(2)}) copy-start(f32[1,4,4,3,8]{4,2,1,0,3:T(4,128)S(1)} %collective-permute-done.13) | copy-start | bytes 4612
  348.6 7.7 %collective-permute-start.14 = (f32[6,1,4,3,8]{4,2,1,0,3:T(4,128)}, f32[6,1,4,3,8]{4,2,1,0,3:T(4,128)}, u32[]{:S(2)}, u32[]{:S(2)}) collective-permute-start(f32[6,1,4,3,8]{4,2,1,0,3:T(4,128)} %get-tuple-element.1310), channel_id=1, source_target_pairs={{0,16},{16,32},{32,48},{48,64},{64,80},{80,96},{96,112},{112,128},... | collective-permute-start | bytes 6920 | tf_op jit(solution)/shard_map/ppermute | solution.py:20
  350.6 7.7 %collective-permute-start.15 = (f32[6,1,4,3,8]{4,2,1,0,3:T(4,128)}, f32[6,1,4,3,8]{4,2,1,0,3:T(4,128)}, u32[]{:S(2)}, u32[]{:S(2)}) collective-permute-start(f32[6,1,4,3,8]{4,2,1,0,3:T(4,128)} %get-tuple-element.1311), channel_id=1, source_target_pairs={{16,0},{32,16},{48,32},{64,48},{80,64},{96,80},{112,96},{128,112},... | collective-permute-start | bytes 6920 | tf_op jit(solution)/shard_map/ppermute | solution.py:23
  359.9 113.8 %collective-permute-start.16 = (f32[6,6,1,3,8]{4,2,1,0,3:T(1,128)}, f32[6,6,1,3,8]{4,2,1,0,3:T(1,128)}, u32[]{:S(2)}, u32[]{:S(2)}) collective-permute-start(f32[6,6,1,3,8]{4,2,1,0,3:T(1,128)} %get-tuple-element.1304), channel_id=1, source_target_pairs={{0,1},{1,2},{2,3},{3,4},{4,5},{5,6},{6,7},{7,8},{8,9},{9,10},{10,1... | collective-permute-start | bytes 10376 | tf_op jit(solution)/shard_map/ppermute | solution.py:20
  361.8 111.8 %collective-permute-start.17 = (f32[6,6,1,3,8]{4,2,1,0,3:T(1,128)}, f32[6,6,1,3,8]{4,2,1,0,3:T(1,128)}, u32[]{:S(2)}, u32[]{:S(2)}) collective-permute-start(f32[6,6,1,3,8]{4,2,1,0,3:T(1,128)} %get-tuple-element.1305), channel_id=1, source_target_pairs={{1,0},{2,1},{3,2},{4,3},{5,4},{6,5},{7,6},{8,7},{9,8},{10,9},{11,1... | collective-permute-start | bytes 10376 | tf_op jit(solution)/shard_map/ppermute | solution.py:23
  367.4 9.3 %copy-start.18 = (f32[6,1,4,8,512]{4,3,2,1,0:T(8,128)}, f32[6,1,4,8,512]{4,3,2,1,0:T(8,128)S(1)}, u32[]{:S(2)}) copy-start(f32[6,1,4,8,512]{4,3,2,1,0:T(8,128)S(1)} %collective-permute-done.20) | copy-start | bytes 1179652
  369.6 106.6 %collective-permute-start.22 = (f32[6,6,1,8,512]{4,3,2,1,0:T(8,128)}, f32[6,6,1,8,512]{4,3,2,1,0:T(8,128)}, u32[]{:S(2)}, u32[]{:S(2)}) collective-permute-start(f32[6,6,1,8,512]{4,3,2,1,0:T(8,128)} %get-tuple-element.1290), channel_id=1, source_target_pairs={{0,1},{1,2},{2,3},{3,4},{4,5},{5,6},{6,7},{7,8},{8,9},{9,10},{10,1... | collective-permute-start | bytes 1769480 | tf_op jit(solution)/shard_map/ppermute | solution.py:20
  371.6 104.6 %collective-permute-start.23 = (f32[6,6,1,8,512]{4,3,2,1,0:T(8,128)}, f32[6,6,1,8,512]{4,3,2,1,0:T(8,128)}, u32[]{:S(2)}, u32[]{:S(2)}) collective-permute-start(f32[6,6,1,8,512]{4,3,2,1,0:T(8,128)} %get-tuple-element.1291), channel_id=1, source_target_pairs={{1,0},{2,1},{3,2},{4,3},{5,4},{6,5},{7,6},{8,7},{9,8},{10,9},{11,1... | collective-permute-start | bytes 1769480 | tf_op jit(solution)/shard_map/ppermute | solution.py:23
  582.7 30.5 %copy-start.46 = (f32[3,64]{1,0:T(4,128)S(1)}, f32[3,64]{1,0:T(4,128)}, u32[]{:S(2)}) copy-start(f32[3,64]{1,0:T(4,128)} %reshape.489) | copy-start | bytes 2308
  583.1 8.1 %collective-permute-start.24 = (f32[1,4,4,3,8]{4,2,1,0,3:T(4,128)S(1)}, f32[1,4,4,3,8]{4,2,1,0,3:T(4,128)S(1)}, u32[]{:S(2)}, u32[]{:S(2)}) collective-permute-start(f32[1,4,4,3,8]{4,2,1,0,3:T(4,128)S(1)} %get-tuple-element.1320), channel_id=1, source_target_pairs={{0,256},{256,0},{1,257},{257,1},{2,258},{258,2},{3,259},{259,3},{4... | collective-permute-start | bytes 4616 | tf_op jit(solution)/shard_map/ppermute | solution.py:20
  587.4 7.2 %collective-permute-start.25 = (f32[1,4,4,3,8]{4,2,1,0,3:T(4,128)S(1)}, f32[1,4,4,3,8]{4,2,1,0,3:T(4,128)S(1)}, u32[]{:S(2)}, u32[]{:S(2)}) collective-permute-start(f32[1,4,4,3,8]{4,2,1,0,3:T(4,128)S(1)} %get-tuple-element.1321), channel_id=1, source_target_pairs={{256,0},{0,256},{257,1},{1,257},{258,2},{2,258},{259,3},{3,259},{2... | collective-permute-start | bytes 4616 | tf_op jit(solution)/shard_map/ppermute | solution.py:23
  594.6 7.7 %collective-permute-start.26 = (f32[6,1,4,3,8]{4,2,1,0,3:T(4,128)S(1)}, f32[6,1,4,3,8]{4,2,1,0,3:T(4,128)S(1)}, u32[]{:S(2)}, u32[]{:S(2)}) collective-permute-start(f32[6,1,4,3,8]{4,2,1,0,3:T(4,128)S(1)} %get-tuple-element.1314), channel_id=1, source_target_pairs={{0,16},{16,32},{32,48},{48,64},{64,80},{80,96},{96,112},{112,128},... | collective-permute-start | bytes 6920 | tf_op jit(solution)/shard_map/ppermute | solution.py:20
  596.5 7.4 %collective-permute-start.27 = (f32[6,1,4,3,8]{4,2,1,0,3:T(4,128)S(1)}, f32[6,1,4,3,8]{4,2,1,0,3:T(4,128)S(1)}, u32[]{:S(2)}, u32[]{:S(2)}) collective-permute-start(f32[6,1,4,3,8]{4,2,1,0,3:T(4,128)S(1)} %get-tuple-element.1315), channel_id=1, source_target_pairs={{16,0},{32,16},{48,32},{64,48},{80,64},{96,80},{112,96},{128,112},... | collective-permute-start | bytes 6920 | tf_op jit(solution)/shard_map/ppermute | solution.py:23
  604.0 8.0 %collective-permute-start.28 = (f32[6,6,1,3,8]{4,2,1,0,3:T(1,128)S(1)}, f32[6,6,1,3,8]{4,2,1,0,3:T(1,128)S(1)}, u32[]{:S(2)}, u32[]{:S(2)}) collective-permute-start(f32[6,6,1,3,8]{4,2,1,0,3:T(1,128)S(1)} %get-tuple-element.1306), channel_id=1, source_target_pairs={{0,1},{1,2},{2,3},{3,4},{4,5},{5,6},{6,7},{7,8},{8,9},{9,10},{10,1... | collective-permute-start | bytes 10376 | tf_op jit(solution)/shard_map/ppermute | solution.py:20
  605.9 6.9 %collective-permute-start.29 = (f32[6,6,1,3,8]{4,2,1,0,3:T(1,128)S(1)}, f32[6,6,1,3,8]{4,2,1,0,3:T(1,128)S(1)}, u32[]{:S(2)}, u32[]{:S(2)}) collective-permute-start(f32[6,6,1,3,8]{4,2,1,0,3:T(1,128)S(1)} %get-tuple-element.1307), channel_id=1, source_target_pairs={{1,0},{2,1},{3,2},{4,3},{5,4},{6,5},{7,6},{8,7},{9,8},{10,9},{11,1... | collective-permute-start | bytes 10376 | tf_op jit(solution)/shard_map/ppermute | solution.py:23
  (76 other events, 233.4 us)
where the time goes:
time: 621 us; the launch traced here: 614 us
  local copies, waits for them, and re-layouts  185 us (30%)
  other arithmetic  167 us (27%)
  starting transfers between devices  114 us (18%)
  matrix products  111 us (18%)
  waiting for transfers between devices  33.4 us (5%)
    ppermute x15, starting transfers between devices, padded(): lax.ppermute(lax.slice_in_dim(block, 0, width, axis=dim), axis, backward)  72.3 us
    scatter-add x8, other arithmetic, geometry(): neighbor_pos = jnp.take(ext_pos, neighbor_ids, axis=1)  49.1 us
    gather x32, local copies, waits for them, and re-layouts, geometry(): neighbor_pos = jnp.take(ext_pos, neighbor_ids, axis=1)  48.2 us
    ppermute x15, starting transfers between devices, padded(): lax.ppermute(lax.slice_in_dim(block, block.shape[dim] - width, None, axis...  42 us
    dot_general x24, matrix products, radial(): jnp.einsum('akn,nh->akh', bessel, inner, precision=highest)  41.9 us
    gather x8, local copies, waits for them, and re-layouts, layer_two_block(): sender = jnp.take(ext_feat, neighbor_ids, axis=0)  39.3 us
    dot_general x24, matrix products, radial(): return jnp.einsum('akh,hc->akc', hidden, outer, precision=highest)  34.2 us
    scatter-add x4, other arithmetic, layer_two_block(): sender = jnp.take(ext_feat, neighbor_ids, axis=0)  30.6 us
  transfers between devices with their start and end apart: 30, of which 16 were waited for; matrix products, arithmetic and copies ran while one was open for 18% of the time, Pallas kernels for 0%

commit v1 on v0

v1 whole, which is shorter than its diff:
```python
import jax
import jax.numpy as jnp
from jax import lax
from jax.experimental import pallas as pl
from jax.experimental.pallas import tpu as pltpu
from jax.sharding import PartitionSpec as P

F32 = jnp.float32
BF16 = jnp.bfloat16
I32 = jnp.int32
TILE = 256
MAX_TILES = 128
MAX_CORE_TILES = 32
WINDOW = 64
INTERPRET = False

COLUMNS = [(2, 2), (2, 3), (3, 2), (3, 3)] + [
    (y, z) for y in range(1, 5) for z in range(1, 5) if not (y in (2, 3) and z in (2, 3))
]
LIST_BASE = {1: 0, 2: 6, 3: 8, 4: 16}
LIST_STEP = {1: 3, 2: 5, 3: 5, 4: 3}
COORD_BASE = {-1: 2, 0: 10, 1: 18}
COORD_STEP = {-1: 3, 0: 5, 1: 3}


def split(x):
    high = x.astype(BF16)
    return high, (x - high.astype(F32)).astype(BF16)


def three(x, axis):
    high, low = split(x)
    return jnp.concatenate([high, low, high], axis=axis)


def three_weights(w, axis):
    high, low = split(w)
    return jnp.concatenate([high, high, low], axis=axis)


def dot(a, b):
    return lax.dot_general(a, b, (((1,), (0,)), ((), ())), preferred_element_type=F32)


def dot_t(a, b):
    return lax.dot_general(a, b, (((1,), (1,)), ((), ())), preferred_element_type=F32)


def lanes_of(table, index):
    return jnp.take_along_axis(table, index, axis=1, mode="promise_in_bounds")


def silu_pair(x):
    gate = 1.0 / (1.0 + jnp.exp(-x))
    value = x * gate
    return value, gate + value * (1.0 - gate)


def pack_kernel(pos_ref, species_ref, counts_ref, neighbors_ref, out_ref):
    ids = neighbors_ref[...].astype(F32)
    joined = jnp.concatenate([ids[:32], ids[32:]], axis=1)
    for part in range(4):
        out_ref[part] = joined[part * 8 : part * 8 + 8]
    rows = jnp.concatenate(
        [
            pos_ref[...],
            species_ref[...].astype(F32),
            counts_ref[...].astype(F32),
            jnp.zeros((3, 64), F32),
        ],
        axis=0,
    )
    out_ref[4] = jnp.concatenate([rows, rows], axis=1)


def iota(shape, axis):
    return lax.broadcasted_iota(I32, shape, axis)


def main_kernel(
    own_ref,
    low_ref,
    high_ref,
    emb_ref,
    fi_ref,
    fo_ref,
    fs_ref,
    fv_ref,
    fq_ref,
    si_ref,
    so_ref,
    sm_ref,
    rf_ref,
    rs_ref,
    energy_ref,
    up_ref,
    mid_ref,
    down_ref,
    table,
    mask_buf,
    raw,
    rowbuf,
    buf,
    bes_buf,
    dbes_buf,
    pair_buf,
    offs_vmem,
    offs,
    last_row,
    sem,
    acc,
    vec_t,
    slope_t,
    feat_t,
    feat_grad,
    w_acc,
    grad_lhs,
    expand,
    saved_rg,
    saved_slope,
    saved_feat,
    saved_pair_grad,
    box_acc,
    emb_pad,
):
    lane8 = iota((8, 128), 1)
    sub8 = iota((8, 128), 0)
    upper = lane8 >= 64
    layer_refs = {-1: low_ref, 0: own_ref, 1: high_ref}

    for dy in (-1, 0, 1):
        for dz in (-1, 0, 1):
            ref = layer_refs[dz]
            base = COORD_BASE[dy]
            joined = jnp.where(upper, ref[base + COORD_STEP[dy]], ref[base])
            shift_x = jnp.where(upper, 12.0, 0.0)
            shift = jnp.where(
                sub8 == 0, shift_x, jnp.where(sub8 == 1, 12.0 * dy, jnp.where(sub8 == 2, 12.0 * dz, 0.0))
            )
            joined = joined + shift
            row = (dy + 1) * 3 + dz + 1
            for comp in range(5):
                table[comp, row] = jnp.broadcast_to(joined[comp : comp + 1], (8, 128))

    for col, (y, z) in enumerate(COLUMNS):
        dy, b = {1: (-1, 1), 2: (0, 0), 3: (0, 1), 4: (1, 0)}[y]
        dz, c = {1: (-1, 1), 2: (0, 0), 3: (0, 1), 4: (1, 0)}[z]
        y_low = -1 if y <= 2 else 0
        z_low = -1 if z <= 2 else 0
        row_l = (dy + 1) * 3 + dz + 1
        for xd in range(2):
            tile = layer_refs[dz][LIST_BASE[y] + xd * LIST_STEP[y] + c].astype(I32)
            g = tile & 7
            r1 = ((tile >> 3) & 3) + 1
            q1 = ((tile >> 5) & 3) + 1
            p1 = ((tile >> 7) & 3) + 1
            x_side = (1 - ((p1 >> 1) & 1)) ^ xd
            y_index = (q1 >> 1) + (dy - 1 - y_low)
            z_index = (r1 >> 1) + (dz - 1 - z_low)
            lane = x_side * 64 + (p1 & 1) * 32 + (q1 & 1) * 16 + (r1 & 1) * 8 + g
            lane_l = jnp.where(upper, 32, 0) + sub8 + (xd * 64 + b * 16 + c * 8)
            row0 = (y_low + 1) * 3 + z_low + 1
            y_zero = y_index == 0
            z_zero = z_index == 0

            def fetch(comp):
                low = jnp.where(
                    z_zero, lanes_of(table[comp, row0], lane), lanes_of(table[comp, row0 + 1], lane)
                )
                top = jnp.where(
                    z_zero, lanes_of(table[comp, row0 + 3], lane), lanes_of(table[comp, row0 + 4], lane)
                )
                return jnp.where(y_zero, low, top)

            d = [fetch(comp) - lanes_of(table[comp, row_l], lane_l) for comp in range(3)]
            d[0] = jnp.where(d[0] > 12.0, d[0] - 24.0, jnp.where(d[0] < -12.0, d[0] + 24.0, d[0]))
            species = fetch(3)
            count = lanes_of(table[4, row_l], lane_l)
            square = d[0] * d[0] + d[1] * d[1] + d[2] * d[2] + 0.25
            slot = (lane8 & 63).astype(F32)
            reach = (square < 36.0) & (slot < count)
            inside = ((y_index >> 1) == 0) & ((z_index >> 1) == 0)
            live = jnp.where(reach & inside, 1.0, 0.0)
            code = (row0 + y_index * 3 + z_index) * 128 + lane
            at = (col * 2 + xd) * 8
            mask_buf[at : at + 8, :] = live
            raw[0, at : at + 8, :] = d[0]
            raw[1, at : at + 8, :] = d[1]
            raw[2, at : at + 8, :] = d[2]
            raw[3, at : at + 8, :] = species
            raw[4, at : at + 8, :] = code.astype(F32)

    mask = mask_buf[...].astype(BF16)
    upto = jnp.where(iota((128, 128), 0) <= iota((128, 128), 1), 1.0, 0.0).astype(BF16)
    within = dot(mask, upto)
    totals = dot_t(jnp.ones((8, 128), BF16), mask)
    before = jnp.where(iota((256, 256), 0) < iota((256, 256), 1), 1.0, 0.0).astype(BF16)
    starts = dot(totals.astype(BF16), before)
    offs_vmem[:, 0:256] = starts.astype(I32)
    offs_vmem[:, 256:512] = totals.astype(I32)
    copy = pltpu.make_async_copy(offs_vmem, offs, sem)
    copy.start()

    for col, (y, z) in enumerate(COLUMNS):
        dy, b = {1: (-1, 1), 2: (0, 0), 3: (0, 1), 4: (1, 0)}[y]
        dz, c = {1: (-1, 1), 2: (0, 0), 3: (0, 1), 4: (1, 0)}[z]
        row_l = (dy + 1) * 3 + dz + 1
        for xd in range(2):
            at = (col * 2 + xd) * 8
            counted = within[at : at + 8, :]
            wanted = (lane8 + 1).astype(F32)
            place = jnp.zeros((8, 128), I32)
            for step in (64, 32, 16, 8, 4, 2, 1):
                probe = lanes_of(counted, place + (step - 1))
                place = jnp.where(probe < wanted, place + step, place)
            half = jnp.where(place >= 64, 1, 0)
            atom = (at + sub8) * 2 + half
            code_l = row_l * 128 + xd * 64 + b * 16 + c * 8 + sub8 + half * 32
            fields = [lanes_of(raw[k, at : at + 8, :], place) for k in range(5)]
            fields += [atom.astype(F32), code_l.astype(F32)]
            for k, field in enumerate(fields):
                rowbuf[pl.ds(at * 8 + k, 8, stride=8), :] = field

    copy.wait()

    def join_row(r, current):
        start = offs[0, r]
        length = offs[0, 256 + r]
        shift = start & 127
        rolled = pltpu.roll(rowbuf[pl.ds(r * 8, 8), :], shift, 1)
        current = jnp.where(lane8 >= shift, rolled, current)
        buf[pl.ds((start >> 7) * 8, 8), :] = current
        last_row[start >> 8] = r
        return jnp.where(shift + length >= 128, rolled, current)

    current = lax.fori_loop(0, 256, join_row, jnp.zeros((8, 128), F32), unroll=8)
    total = offs[0, 255] + offs[0, 511]
    core_total = offs[0, 64]
    buf[pl.ds((total >> 7) * 8, 8), :] = current
    last_row[jnp.maximum(total - 1, 0) >> 8] = 255
    tiles = (total + (TILE - 1)) // TILE
    core_tiles = (core_total + (TILE - 1)) // TILE

    column_of = jnp.zeros((8, 128), I32)
    for col, (y, z) in enumerate(COLUMNS):
        column_of = jnp.where(lane8 == (y - 1) * 4 + z - 1, col, column_of)

    def basis(chunk, carry):
        at = chunk * 64
        field = [buf[pl.ds(at + k, 8, stride=8), :] for k in range(7)]
        valid = (chunk * 1024 + sub8 * 128 + lane8) < total
        d = [jnp.where(valid, field[k], 100.0) for k in range(3)]
        species = jnp.where(valid, field[3], 0.0)
        code = jnp.where(valid, field[4], 0.0).astype(I32)
        atom = jnp.where(valid, field[5], -1.0)
        code_l = jnp.where(valid, field[6], 0.0)
        square = d[0] * d[0] + d[1] * d[1] + d[2] * d[2] + 0.25
        rho = jnp.sqrt(square)
        inv = 1.0 / rho
        t = jnp.where(rho < 6.0, rho * (1.0 / 6.0), 1.0)
        inside = valid & (rho < 6.0)
        angle = t * 3.14159265358979 - 1.5707963267948966
        a2 = angle * angle
        sin_a = angle * (
            1.0
            + a2
            * (
                -1.0 / 6
                + a2
                * (
                    1.0 / 120
                    + a2 * (-1.0 / 5040 + a2 * (1.0 / 362880 + a2 * (-1.0 / 39916800 + a2 / 6227020800.0)))
                )
            )
        )
        cos_a = 1.0 + a2 * (
            -0.5
            + a2
            * (
                1.0 / 24
                + a2
                * (
                    -1.0 / 720
                    + a2
                    * (1.0 / 40320 + a2 * (-1.0 / 3628800 + a2 * (1.0 / 479001600 - a2 / 87178291200.0)))
                )
            )
        )
        sine, cosine = cos_a, -sin_a
        t2 = t * t
        t5 = t2 * t2 * t
        f = 1.0 + t5 * t * (-28.0 + t * (48.0 - 21.0 * t))
        f = jnp.where(inside, f, 0.0)
        one = 1.0 - t
        df = jnp.where(inside, -28.0 * t5 * one * one, 0.0)
        scale = 0.5773502691896258
        amount = scale * inv * f
        slope = scale * inv * (df - inv * f)
        s_prev, c_prev = jnp.zeros((8, 128), F32), jnp.ones((8, 128), F32)
        s_now, c_now = sine, cosine
        for n in range(8):
            bes_buf[pl.ds(at + n, 8, stride=8), :] = s_now * amount
            dbes_buf[pl.ds(at + n, 8, stride=8), :] = (
                c_now * amount * ((n + 1) * 0.5235987755982988) + s_now * slope
            )
            s_now, s_prev = 2.0 * cosine * s_now - s_prev, s_now
            c_now, c_prev = 2.0 * cosine * c_now - c_prev, c_now
        row = code >> 7
        lane = code & 127
        row_y = jnp.where(row >= 6, 2, jnp.where(row >= 3, 1, 0))
        row_z = row - 3 * row_y
        y = row_y * 2 + ((lane >> 4) & 1) - 1
        z = row_z * 2 + ((lane >> 3) & 1) - 1
        near = (y >= 0) & (y < 4) & (z >= 0) & (z < 4)
        column = lanes_of(column_of, jnp.where(near, y * 4 + z, 0))
        source = column * 32 + ((lane >> 6) & 1) * 16 + (lane & 7) * 2 + ((lane >> 5) & 1)
        source = jnp.where(near, source, -1)
        both = code.astype(F32) * 2048.0 + code_l
        kept = [d[0] * inv, d[1] * inv, d[2] * inv, inv, species, source.astype(F32), atom, both]
        for k, value in enumerate(kept):
            pair_buf[pl.ds(at + k, 8, stride=8), :] = value
        return carry

    lax.fori_loop(0, (total + 1023) // 1024, basis, 0)

    fi3 = jnp.concatenate([fi_ref[...], jnp.zeros((24, 64), F32)], axis=0)
    si3 = jnp.concatenate([si_ref[...], jnp.zeros((24, 64), F32)], axis=0)

    def inner_weights(padded):
        w = padded.T[:, 0:8]
        high = w.astype(BF16).astype(F32)
        low = w - high
        return jnp.concatenate([high, high, low, jnp.zeros((64, 8), F32)], axis=1).astype(BF16)

    def inner_back(ref):
        w = jnp.concatenate([ref[...], jnp.zeros((8, 64), F32)], axis=0)
        return three_weights(w, 1)

    fi_t3 = inner_weights(fi3)
    si_t3 = inner_weights(si3)
    fi_b3 = inner_back(fi_ref)
    si_b3 = inner_back(si_ref)
    fo_t3 = three_weights(fo_ref[...].T, 1)
    so_t3 = three_weights(so_ref[...].T, 1)
    fo_b3 = three_weights(fo_ref[...], 1)
    so_b3 = three_weights(so_ref[...], 1)
    emb_pad[...] = jnp.zeros((128, 128), F32)
    emb_pad[0:89, :] = emb_ref[...]
    emb_t2 = jnp.concatenate(split(emb_pad[...].T), axis=1)

    def tile_rows(ref, t):
        at = t * 16
        return jnp.concatenate([ref[pl.ds(at, 8), :], ref[pl.ds(at + 8, 8), :]], axis=1)

    def hidden_of(t, weights):
        bes = tile_rows(bes_buf, t)
        high = bes.astype(BF16).astype(F32)
        stack = jnp.concatenate([high, bes - high, high, jnp.zeros((8, TILE), F32)], axis=0)
        return silu_pair(dot(weights, stack.astype(BF16)))

    def onehot(index_row, rows):
        hit = iota((rows, index_row.shape[1]), 0) == index_row.astype(I32)
        return jnp.where(hit, 1.0, 0.0).astype(BF16)

    def sender_of(species_row):
        hot = onehot(species_row, 128)
        return dot(emb_t2, jnp.concatenate([hot, hot], axis=0))

    def first_of(t):
        return jnp.where(t == 0, 0, last_row[jnp.maximum(t - 1, 0)]) * 2

    acc[...] = jnp.zeros(acc.shape, F32)

    def layer_one(t, carry):
        hidden, slope = hidden_of(t, fi_t3)
        saved_slope[t] = slope
        weights = dot(fo_t3, three(hidden, 0))
        pair = tile_rows(pair_buf, t)
        sender = sender_of(pair[4:5])
        m_high, m_low = split(weights[0:128] * sender)
        rg = weights[128:256] * sender
        saved_rg[t] = rg
        v_high, v_low = split(rg)
        saved_pair_grad[t] = jnp.zeros((8, TILE), F32)
        unit = [split(pair[k : k + 1]) for k in range(3)]
        base = first_of(t) & -8
        windows = (last_row[t] * 2 + 1 - base) // WINDOW + 1

        def window(w, carry):
            at = base + w * WINDOW
            hot = onehot(pair[6:7] - at.astype(F32), WINDOW)
            u_high = jnp.concatenate([hot * high for high, _ in unit], axis=0)
            u_low = jnp.concatenate([hot * low for _, low in unit], axis=0)
            m = dot_t(hot, m_high) + dot_t(hot, m_low)
            v = dot_t(u_high, v_high) + dot_t(u_high, v_low) + dot_t(u_low, v_high)
            rows = pl.ds(pl.multiple_of(at, 8), WINDOW)
            acc[0, rows, :] += m
            for x in range(3):
                acc[1 + x, rows, :] += v[x * WINDOW : (x + 1) * WINDOW]
            return carry

        return lax.fori_loop(0, windows, window, carry)

    lax.fori_loop(0, tiles, layer_one, 0)

    parts = []
    for group in range(4):
        merged = None
        for sub in range(4):
            col = group * 4 + sub
            y, z = COLUMNS[col]
            dy, b = {1: (-1, 1), 2: (0, 0), 3: (0, 1), 4: (1, 0)}[y]
            dz, c = {1: (-1, 1), 2: (0, 0), 3: (0, 1), 4: (1, 0)}[z]
            local = lane8 & 31
            index = ((local >> 4) & 1) * 64 + (local & 1) * 32 + ((local >> 1) & 7) + b * 16 + c * 8
            got = lanes_of(table[3, (dy + 1) * 3 + dz + 1], index)
            merged = got if merged is None else jnp.where((lane8 >> 5) == sub, got, merged)
        parts.append(merged)
    species_row = jnp.concatenate(parts, axis=1)[0:1]
    node_t = sender_of(species_row)
    fv_t3 = three_weights(fv_ref[...].T, 1)
    square_t = jnp.zeros((128, 512), F32)
    for x in range(3):
        v3 = three(acc[1 + x, 0:512, :] * 0.25, 1)
        value = dot_t(fv_t3, v3)
        vec_t[x] = value
        square_t = square_t + value * value
        high, low = split(value)
        feat_t[0, 128 + x * 128 : 256 + x * 128, :] = high
        feat_t[1, 128 + x * 128 : 256 + x * 128, :] = low
    fs_t3 = three_weights(fs_ref[...].T, 1)
    fq_t3 = three_weights(fq_ref[...].T, 1)
    pre = dot_t(fs_t3, three(acc[0, 0:512, :] * 0.25, 1))
    pre = pre + dot(fs_t3, three(node_t, 0)) + dot(fq_t3, three(square_t, 0))
    scal_t, slope = silu_pair(pre)
    slope_t[...] = slope
    high, low = split(scal_t)
    feat_t[0, 0:128, :] = high
    feat_t[1, 0:128, :] = low
    scal_core = scal_t[:, 0:128]

    w_acc[...] = jnp.zeros((128, 128), F32)

    def layer_two(t, carry):
        hidden, _ = hidden_of(t, si_t3)
        weights = dot(so_t3, three(hidden, 0))
        pair = tile_rows(pair_buf, t)
        hot = onehot(pair[5:6], 512)
        feat = dot(feat_t[0], hot) + dot(feat_t[1], hot)
        saved_feat[t] = feat
        proj = pair[0:1] * feat[128:256] + pair[1:2] * feat[256:384] + pair[2:3] * feat[384:512]
        high, low = split(weights[0:128] * feat[0:128] + weights[128:256] * proj)
        member = onehot(pair[6:7], 128)
        w_acc[...] += dot_t(high, member) + dot_t(low, member)
        return carry

    lax.fori_loop(0, core_tiles, layer_two, 0)

    mixed = w_acc[...] * 0.25 + scal_core
    rs_col = jnp.broadcast_to(rs_ref[...], (128, 128)).T
    rf_col = jnp.broadcast_to(rf_ref[...], (128, 128)).T
    out, out_slope = silu_pair(dot(three_weights(sm_ref[...].T, 1), three(mixed, 0)))
    energy = jnp.sum(out * rs_col + scal_core * rf_col, axis=0, keepdims=True)
    index = (((lane8 >> 3) & 3) * 16 + (lane8 & 7)) * 2 + ((lane8 >> 5) & 1)
    index = jnp.where(lane8 < 64, ((lane8 >> 3) & 3) * 32 + (lane8 & 7) * 2 + ((lane8 >> 5) & 1), 0)
    energy_ref[...] = lanes_of(jnp.broadcast_to(energy, (8, 128)), index)[0:1, 0:64]

    mixed_grad = dot(three_weights(sm_ref[...], 1), three(rs_col * out_slope, 0))
    w_grad2 = jnp.concatenate(split(mixed_grad * 0.25), axis=1)
    feat_grad[...] = jnp.zeros((512, 512), F32)
    feat_grad[0:128, 0:128] = mixed_grad + rf_col

    def radial_back(t, slope, grad, outer3, inner3):
        hidden_grad = dot(outer3, three(grad, 0)) * slope
        bes_grad = dot(inner3, three(hidden_grad, 0))[0:8]
        return jnp.sum(bes_grad * tile_rows(dbes_buf, t), axis=0, keepdims=True)

    def layer_two_back(t, carry):
        hidden, slope = hidden_of(t, si_t3)
        weights = dot(so_t3, three(hidden, 0))
        pair = tile_rows(pair_buf, t)
        feat = saved_feat[t]
        member = onehot(pair[6:7], 128)
        w_grad = dot(w_grad2, jnp.concatenate([member, member], axis=0))
        proj = pair[0:1] * feat[128:256] + pair[1:2] * feat[256:384] + pair[2:3] * feat[384:512]
        radial_grad = jnp.concatenate([w_grad * feat[0:128], w_grad * proj], axis=0)
        rho_grad = radial_back(t, slope, radial_grad, so_b3, si_b3)
        proj_grad = w_grad * weights[128:256]
        grads = [rho_grad]
        sends = [w_grad * weights[0:128]]
        for x in range(3):
            part = feat[128 + x * 128 : 256 + x * 128]
            grads.append(jnp.sum(proj_grad * part, axis=0, keepdims=True))
            sends.append(proj_grad * pair[x : x + 1])
        saved_pair_grad[t] = jnp.concatenate(grads + [jnp.zeros((4, TILE), F32)], axis=0)
        high, low = split(jnp.concatenate(sends, axis=0))
        hot = onehot(pair[5:6], 512)
        feat_grad[...] += dot_t(high, hot) + dot_t(low, hot)
        return carry

    lax.fori_loop(0, core_tiles, layer_two_back, 0)

    pre_grad3 = three(feat_grad[0:128, :] * slope_t[...], 0)
    m_grad = dot(three_weights(fs_ref[...], 1), pre_grad3)
    square_grad = dot(three_weights(fq_ref[...], 1), pre_grad3)
    fv_b3 = three_weights(fv_ref[...], 1)
    message_grads = [m_grad]
    for x in range(3):
        part = feat_grad[128 + x * 128 : 256 + x * 128, :] + 2.0 * vec_t[x] * square_grad
        message_grads.append(dot(fv_b3, three(part, 0)))
    for kind in range(4):
        high, low = split(message_grads[kind] * 0.25)
        for w in range(4):
            grad_lhs[w, kind * 128 : (kind + 1) * 128, 0:128] = high[:, w * 128 : (w + 1) * 128]
            grad_lhs[w, kind * 128 : (kind + 1) * 128, 128:256] = low[:, w * 128 : (w + 1) * 128]

    box_acc[...] = jnp.zeros((96, 128), F32)

    def layer_one_back(t, carry):
        pair = tile_rows(pair_buf, t)
        first = first_of(t) >> 7
        last = (last_row[t] * 2 + 1) >> 7

        def expanded(w):
            member = onehot(pair[6:7] - (w * 128).astype(F32), 128)
            return dot(grad_lhs[w], jnp.concatenate([member, member], axis=0))

        expand[...] = expanded(first)

        def more(w, carry):
            expand[...] += expanded(w)
            return carry

        lax.fori_loop(first + 1, last + 1, more, 0)
        sender = sender_of(pair[4:5])
        rg = saved_rg[t]
        v_grad = [expand[128 + x * 128 : 256 + x * 128, :] for x in range(3)]
        along = pair[0:1] * v_grad[0] + pair[1:2] * v_grad[1] + pair[2:3] * v_grad[2]
        radial_grad = jnp.concatenate([expand[0:128, :] * sender, along * sender], axis=0)
        earlier = saved_pair_grad[t]
        rho_grad = radial_back(t, saved_slope[t], radial_grad, fo_b3, fi_b3) + earlier[0:1]
        unit_grad = [
            jnp.sum(rg * v_grad[x], axis=0, keepdims=True) + earlier[1 + x : 2 + x] for x in range(3)
        ]
        unit = [pair[x : x + 1] for x in range(3)]
        inner = unit[0] * unit_grad[0] + unit[1] * unit_grad[1] + unit[2] * unit_grad[2]
        inv = pair[3:4]
        values = []
        for x in range(3):
            value = (unit_grad[x] - unit[x] * inner) * inv + rho_grad * unit[x]
            high = value.astype(BF16).astype(F32)
            values += [high, value - high]
        both = pair[7:8].astype(I32)

        def spread(code, sign):
            row = jnp.broadcast_to(code >> 7, (16, TILE)) == iota((16, TILE), 0)
            stack = [jnp.where(row, sign * value, 0.0) for value in values]
            lane = jnp.where(iota((128, TILE), 0) == (code & 127), 1.0, 0.0).astype(BF16)
            return dot_t(jnp.concatenate(stack, axis=0).astype(BF16), lane)

        box_acc[...] += spread(both >> 11, 1.0) + spread(both & 2047, -1.0)
        return carry

    lax.fori_loop(0, tiles, layer_one_back, 0)

    for comp in range(3):
        grid = box_acc[comp * 32 : comp * 32 + 16, :] + box_acc[comp * 32 + 16 : comp * 32 + 32, :]
        for dz, ref in ((-1, down_ref), (0, mid_ref), (1, up_ref)):
            for dy in range(3):
                row = dy * 3 + dz + 1
                ref[dy, comp : comp + 1, :] = grid[row : row + 1, :]
    for ref in (down_ref, mid_ref, up_ref):
        for dy in range(3):
            ref[dy, 3:8, :] = jnp.zeros((5, 128), F32)


def pair_program(own, low, high, weights):
    vm = pltpu.VMEM
    pair_rows = (MAX_TILES * 2 + 8) * 8
    scratch = [
        vm((5, 9, 8, 128), F32),
        vm((256, 128), F32),
        vm((5, 256, 128), F32),
        vm((2048, 128), F32),
        vm((pair_rows, 128), F32),
        vm((pair_rows, 128), F32),
        vm((pair_rows, 128), F32),
        vm((pair_rows, 128), F32),
        vm((8, 512), I32),
        pltpu.SMEM((8, 512), I32),
        pltpu.SMEM((256,), I32),
        pltpu.SemaphoreType.DMA,
        vm((4, 512 + WINDOW, 128), F32),
        vm((3, 128, 512), F32),
        vm((128, 512), F32),
        vm((2, 512, 512), BF16),
        vm((512, 512), F32),
        vm((128, 128), F32),
        vm((4, 512, 256), BF16),
        vm((512, TILE), F32),
        vm((MAX_TILES, 128, TILE), F32),
        vm((MAX_TILES, 64, TILE), F32),
        vm((MAX_CORE_TILES, 512, TILE), F32),
        vm((MAX_TILES, 8, TILE), F32),
        vm((96, 128), F32),
        vm((128, 128), F32),
    ]
    whole = pl.BlockSpec(memory_space=pltpu.VMEM)
    piece = jax.ShapeDtypeStruct((3, 8, 128), F32)
    return pl.pallas_call(
        main_kernel,
        out_shape=(jax.ShapeDtypeStruct((1, 64), F32), piece, piece, piece),
        in_specs=[whole] * (3 + len(weights)),
        out_specs=(whole,) * 4,
        scratch_shapes=scratch,
        compiler_params=pltpu.CompilerParams(vmem_limit_bytes=60 * 1024 * 1024),
        interpret=INTERPRET,
    )(own, low, high, *weights)


def pack(positions, species, counts, neighbors):
    whole = pl.BlockSpec(memory_space=pltpu.VMEM)
    return pl.pallas_call(
        pack_kernel,
        out_shape=jax.ShapeDtypeStruct((5, 8, 128), F32),
        in_specs=[whole] * 4,
        out_specs=whole,
        interpret=INTERPRET,
    )(positions, species.reshape(1, 64), counts.reshape(1, 64), neighbors)


def join_y(own, below, above):
    return jnp.concatenate(
        [below[2:5], below[7:10], own, above[0:2], above[4:7], above[9:10]], axis=0
    )


def ring(axis, step):
    count = lax.axis_size(axis)
    return [(i, (i + step) % count) for i in range(count)]


def shards(
    positions,
    species,
    neighbors,
    neighbor_counts,
    embedding,
    first_inner,
    first_outer,
    first_scalar,
    first_vector,
    first_square,
    second_inner,
    second_outer,
    second_mix,
    readout_first,
    readout_second,
):
    packed = pack(positions, species, neighbor_counts, neighbors)
    partner = lax.ppermute(packed, "gx", ring("gx", 1))
    both = jnp.concatenate([packed, partner], axis=0)
    below = lax.ppermute(both, "gy", ring("gy", 1))
    above = lax.ppermute(both, "gy", ring("gy", -1))
    layer = join_y(both, below, above)
    low = lax.ppermute(layer, "gz", ring("gz", 1))
    high = lax.ppermute(layer, "gz", ring("gz", -1))
    weights = (
        embedding,
        first_inner,
        first_outer,
        first_scalar,
        first_vector,
        first_square,
        second_inner,
        second_outer,
        second_mix,
        readout_first.reshape(1, 128),
        readout_second.reshape(1, 128),
    )
    energy, up, mid, down = pair_program(layer, low, high, weights)
    folded = mid + lax.ppermute(up, "gz", ring("gz", 1)) + lax.ppermute(down, "gz", ring("gz", -1))
    total = folded[1] + lax.ppermute(folded[2], "gy", ring("gy", 1))
    total = total + lax.ppermute(folded[0], "gy", ring("gy", -1))
    return (energy.reshape(64), -total[0:3, 0:64])


def solution(mesh):
    spread = ("gx", "gy", "gz")
    placed = (P(None, spread), P(spread), P(spread, None), P(spread)) + (P(),) * 11
    return jax.shard_map(
        shards,
        mesh=mesh,
        in_specs=placed,
        out_specs=(P(spread), P(None, spread)),
        check_vma=False,
    )
```

time: 621 us -> 115 us (0.19)
  the two profiles are of different devices: /device:TPU:16 before, /device:TPU:25 now
where the time goes in v1:
time: 115 us
  Pallas kernels  56.5 us (49%)
  starting transfers between devices  37.5 us (33%)
  waiting for transfers between devices  17 us (15%)
  other arithmetic  2.03 us (2%)
    pallas_call x1, Pallas kernels, pair_program(): pl.pallas_call(main_kernel, out_shape=(jax.ShapeDtypeStruct((1, 64), F32)...  55 us
    ppermute x1, starting transfers between devices, shards(): high = lax.ppermute(layer, 'gz', ring('gz', -1))  11.1 us
    ppermute x1, starting transfers between devices, shards(): total = folded[1] + lax.ppermute(folded[2], 'gy', ring('gy', 1))  6.16 us
    ppermute x1, starting transfers between devices, shards(): below = lax.ppermute(both, 'gy', ring('gy', 1))  5.13 us
    ppermute x1, starting transfers between devices, shards(): lax.ppermute(down, 'gz', ring('gz', -1))  4.57 us
    ppermute x1, waiting for transfers between devices, shards(): low = lax.ppermute(layer, 'gz', ring('gz', 1))  4.53 us
    ppermute x1, waiting for transfers between devices, shards(): above = lax.ppermute(both, 'gy', ring('gy', -1))  4.22 us
    ppermute x1, waiting for transfers between devices, shards(): total = total + lax.ppermute(folded[0], 'gy', ring('gy', -1))  3.89 us
  transfers between devices with their start and end apart: 9, of which 5 were waited for; matrix products, arithmetic and copies ran while one was open for 0% of the time, Pallas kernels for 0%

profile of v1, /device:TPU:25, one launch (start us, length us, event | category | flops | bytes accessed | tf_op | source)
XLA Modules:
  0.0 114.6 jit_solution(12345744152978700671)
XLA Ops:
  0.6 1.5 %shard_map.158 = f32[5,8,128]{2,1,0:T(8,128)} custom-call(f32[3,64]{1,0:T(4,128)} %pos_ref.1, s32[1,64]{1,0:T(1,128)} %bitcast.15, s32[1,64]{1,0:T(1,128)} %bitcast.16, s32[64,64]{1,0:T(8,128)} %neighbors_ref.1), custom_call_target="tpu_custom_call" | custom-call | tf_op jit(solution)/shard_map/pallas_call | solution.py:623
  2.1 2.9 %collective-permute-start = (f32[5,8,128]{2,1,0:T(8,128)}, f32[5,8,128]{2,1,0:T(8,128)S(1)}, u32[]{:S(2)}, u32[]{:S(2)}) collective-permute-start(f32[5,8,128]{2,1,0:T(8,128)} %shard_map.158), channel_id=1, source_target_pairs={{0,256},{256,0},{1,257},{257,1},{2,258},{258,2},{3,259},{259,3},{4... | collective-permute-start | bytes 61448 | tf_op jit(solution)/shard_map/ppermute | solution.py:661
  5.0 3.4 %collective-permute-done = f32[5,8,128]{2,1,0:T(8,128)S(1)} collective-permute-done((f32[5,8,128]{2,1,0:T(8,128)}, f32[5,8,128]{2,1,0:T(8,128)S(1)}, u32[]{:S(2)}, u32[]{:S(2)}) %collective-permute-start) | collective-permute-done | bytes 20512 | tf_op jit(solution)/shard_map/ppermute | solution.py:661
  8.4 0.7 pad_maximum_fusion
  9.1 0.0 copy-start
  9.1 5.1 %collective-permute-start.1 = (f32[10,8,128]{2,1,0:T(8,128)S(1)}, f32[10,8,128]{2,1,0:T(8,128)S(1)}, u32[]{:S(2)}, u32[]{:S(2)}) collective-permute-start(f32[10,8,128]{2,1,0:T(8,128)S(1)} %pad_maximum_fusion), channel_id=1, source_target_pairs={{0,16},{16,32},{32,48},{48,64},{64,80},{80,96},{96,112},{112,128},... | collective-permute-start | bytes 122888 | tf_op jit(solution)/shard_map/ppermute | solution.py:663
  14.2 1.9 %collective-permute-start.2 = (f32[10,8,128]{2,1,0:T(8,128)S(1)}, f32[10,8,128]{2,1,0:T(8,128)S(1)}, u32[]{:S(2)}, u32[]{:S(2)}) collective-permute-start(f32[10,8,128]{2,1,0:T(8,128)S(1)} %pad_maximum_fusion), channel_id=1, source_target_pairs={{0,240},{16,0},{32,16},{48,32},{64,48},{80,64},{96,80},{112,96},{1... | collective-permute-start | bytes 122888 | tf_op jit(solution)/shard_map/ppermute | solution.py:664
  16.2 0.0 collective-permute-done.1
  16.2 0.0 copy-done
  16.2 4.2 %collective-permute-done.2 = f32[10,8,128]{2,1,0:T(8,128)S(1)} collective-permute-done((f32[10,8,128]{2,1,0:T(8,128)S(1)}, f32[10,8,128]{2,1,0:T(8,128)S(1)}, u32[]{:S(2)}, u32[]{:S(2)}) %collective-permute-start.2) | collective-permute-done | bytes 40992 | tf_op jit(solution)/shard_map/ppermute | solution.py:664
  20.4 0.0 copy-start.1
  20.5 11.1 %collective-permute-start.4 = (f32[22,8,128]{2,1,0:T(8,128)S(1)}, f32[22,8,128]{2,1,0:T(8,128)S(1)}, u32[]{:S(2)}, u32[]{:S(2)}) collective-permute-start(f32[22,8,128]{2,1,0:T(8,128)S(1)} %constant_dynamic-update-slice_fusion.own_ref), channel_id=1, source_target_pairs={{0,15},{1,0},{2,1},{3,2},{4,3},{5,4},{6,5},{7,6},{8,7},{9,8},{10,9... | collective-permute-start | bytes 270344 | tf_op jit(solution)/shard_map/ppermute | solution.py:667
  31.6 1.9 %collective-permute-start.3 = (f32[22,8,128]{2,1,0:T(8,128)S(1)}, f32[22,8,128]{2,1,0:T(8,128)S(1)}, u32[]{:S(2)}, u32[]{:S(2)}) collective-permute-start(f32[22,8,128]{2,1,0:T(8,128)S(1)} %constant_dynamic-update-slice_fusion.own_ref), channel_id=1, source_target_pairs={{0,1},{1,2},{2,3},{3,4},{4,5},{5,6},{6,7},{7,8},{8,9},{9,10},{10,1... | collective-permute-start | bytes 270344 | tf_op jit(solution)/shard_map/ppermute | solution.py:666
  33.5 0.0 collective-permute-done.4.high_ref
  33.5 0.0 copy-start.2
  33.5 4.5 %collective-permute-done.3.low_ref = f32[22,8,128]{2,1,0:T(8,128)S(1)} collective-permute-done((f32[22,8,128]{2,1,0:T(8,128)S(1)}, f32[22,8,128]{2,1,0:T(8,128)S(1)}, u32[]{:S(2)}, u32[]{:S(2)}) %collective-permute-start.3) | collective-permute-done | bytes 90144 | tf_op jit(solution)/shard_map/ppermute | solution.py:666
  38.1 0.0 copy-start.3
  38.1 0.0 copy-done.1
  38.1 0.0 copy-done.2
  38.1 0.6 copy-done.3
  38.7 55.0 %shard_map.159 = (f32[1,64]{1,0:T(1,128)}, f32[3,8,128]{2,1,0:T(8,128)}, f32[3,8,128]{2,1,0:T(8,128)}, f32[3,8,128]{2,1,0:T(8,128)}) custom-call(f32[22,8,128]{2,1,0:T(8,128)} %copy-done.1, f32[22,8,128]{2,1,0:T(8,128)} %copy-done.3, f32[22,8,128]{2,1,0:T(8,128)} %copy-done.2, f32[89,128]{1,0:T(8,128)} %emb_ref.1, f32[8,64]{1,0:T(8,128)} %fi_ref.1, ...), custom_call_target="tpu_custom_call" | custom-call | tf_op jit(solution)/shard_map/pallas_call | solution.py:610
  93.7 1.9 %collective-permute-start.5 = (f32[3,8,128]{2,1,0:T(8,128)}, f32[3,8,128]{2,1,0:T(8,128)S(1)}, u32[]{:S(2)}, u32[]{:S(2)}) collective-permute-start(f32[3,8,128]{2,1,0:T(8,128)} %get-tuple-element.8), channel_id=1, source_target_pairs={{0,1},{1,2},{2,3},{3,4},{4,5},{5,6},{6,7},{7,8},{8,9},{9,10},{10,1... | collective-permute-start | bytes 36872 | tf_op jit(solution)/shard_map/ppermute | solution.py:682
  95.7 4.6 %collective-permute-start.6 = (f32[3,8,128]{2,1,0:T(8,128)}, f32[3,8,128]{2,1,0:T(8,128)S(1)}, u32[]{:S(2)}, u32[]{:S(2)}) collective-permute-start(f32[3,8,128]{2,1,0:T(8,128)} %get-tuple-element.9), channel_id=1, source_target_pairs={{0,15},{1,0},{2,1},{3,2},{4,3},{5,4},{6,5},{7,6},{8,7},{9,8},{10,9... | collective-permute-start | bytes 36872 | tf_op jit(solution)/shard_map/ppermute | solution.py:682
  100.2 0.0 collective-permute-done.5
  100.3 1.0 collective-permute-done.6
  101.3 0.7 add_add_fusion
  102.0 6.2 %collective-permute-start.7 = (f32[8,128]{1,0:T(8,128)S(1)}, f32[8,128]{1,0:T(8,128)S(1)}, u32[]{:S(2)}, u32[]{:S(2)}) collective-permute-start(f32[8,128]{1,0:T(8,128)S(1)} %get-tuple-element.10), channel_id=1, source_target_pairs={{0,16},{16,32},{32,48},{48,64},{64,80},{80,96},{96,112},{112,128},... | collective-permute-start | bytes 12296 | tf_op jit(solution)/shard_map/ppermute | solution.py:683
  108.2 1.9 %collective-permute-start.8 = (f32[8,128]{1,0:T(8,128)S(1)}, f32[8,128]{1,0:T(8,128)S(1)}, u32[]{:S(2)}, u32[]{:S(2)}) collective-permute-start(f32[8,128]{1,0:T(8,128)S(1)} %get-tuple-element.11), channel_id=1, source_target_pairs={{0,240},{16,0},{32,16},{48,32},{64,48},{80,64},{96,80},{112,96},{1... | collective-permute-start | bytes 12296 | tf_op jit(solution)/shard_map/ppermute | solution.py:684
  110.1 0.0 collective-permute-done.7
  110.1 3.9 %collective-permute-done.8 = f32[8,128]{1,0:T(8,128)S(1)} collective-permute-done((f32[8,128]{1,0:T(8,128)S(1)}, f32[8,128]{1,0:T(8,128)S(1)}, u32[]{:S(2)}, u32[]{:S(2)}) %collective-permute-start.8) | collective-permute-done | bytes 4128 | tf_op jit(solution)/shard_map/ppermute | solution.py:684
  114.0 0.6 slice_negate_fusion
  (9 shorter events, 0.0 us)
Async XLA Ops:
  2.1 6.2 %collective-permute-start = (f32[5,8,128]{2,1,0:T(8,128)}, f32[5,8,128]{2,1,0:T(8,128)S(1)}, u32[]{:S(2)}, u32[]{:S(2)}) collective-permute-start(f32[5,8,128]{2,1,0:T(8,128)} %shard_map.158), channel_id=1, source_target_pairs={{0,256},{256,0},{1,257},{257,1},{2,258},{258,2},{3,259},{259,3},{4... | collective-permute-start | bytes 61448 | tf_op jit(solution)/shard_map/ppermute | solution.py:661
  9.1 7.1 %copy-start = (f32[5,8,128]{2,1,0:T(8,128)S(1)}, f32[5,8,128]{2,1,0:T(8,128)}, u32[]{:S(2)}) copy-start(f32[5,8,128]{2,1,0:T(8,128)} %shard_map.158) | copy-start | bytes 61444
  9.1 7.1 %collective-permute-start.1 = (f32[10,8,128]{2,1,0:T(8,128)S(1)}, f32[10,8,128]{2,1,0:T(8,128)S(1)}, u32[]{:S(2)}, u32[]{:S(2)}) collective-permute-start(f32[10,8,128]{2,1,0:T(8,128)S(1)} %pad_maximum_fusion), channel_id=1, source_target_pairs={{0,16},{16,32},{32,48},{48,64},{64,80},{80,96},{96,112},{112,128},... | collective-permute-start | bytes 122888 | tf_op jit(solution)/shard_map/ppermute | solution.py:663
  14.2 6.2 %collective-permute-start.2 = (f32[10,8,128]{2,1,0:T(8,128)S(1)}, f32[10,8,128]{2,1,0:T(8,128)S(1)}, u32[]{:S(2)}, u32[]{:S(2)}) collective-permute-start(f32[10,8,128]{2,1,0:T(8,128)S(1)} %pad_maximum_fusion), channel_id=1, source_target_pairs={{0,240},{16,0},{32,16},{48,32},{64,48},{80,64},{96,80},{112,96},{1... | collective-permute-start | bytes 122888 | tf_op jit(solution)/shard_map/ppermute | solution.py:664
  20.4 17.6 %copy-start.1 = (f32[22,8,128]{2,1,0:T(8,128)}, f32[22,8,128]{2,1,0:T(8,128)S(1)}, u32[]{:S(2)}) copy-start(f32[22,8,128]{2,1,0:T(8,128)S(1)} %constant_dynamic-update-slice_fusion.own_ref) | copy-start | bytes 270340
  20.5 13.1 %collective-permute-start.4 = (f32[22,8,128]{2,1,0:T(8,128)S(1)}, f32[22,8,128]{2,1,0:T(8,128)S(1)}, u32[]{:S(2)}, u32[]{:S(2)}) collective-permute-start(f32[22,8,128]{2,1,0:T(8,128)S(1)} %constant_dynamic-update-slice_fusion.own_ref), channel_id=1, source_target_pairs={{0,15},{1,0},{2,1},{3,2},{4,3},{5,4},{6,5},{7,6},{8,7},{9,8},{10,9... | collective-permute-start | bytes 270344 | tf_op jit(solution)/shard_map/ppermute | solution.py:667
  31.6 6.5 %collective-permute-start.3 = (f32[22,8,128]{2,1,0:T(8,128)S(1)}, f32[22,8,128]{2,1,0:T(8,128)S(1)}, u32[]{:S(2)}, u32[]{:S(2)}) collective-permute-start(f32[22,8,128]{2,1,0:T(8,128)S(1)} %constant_dynamic-update-slice_fusion.own_ref), channel_id=1, source_target_pairs={{0,1},{1,2},{2,3},{3,4},{4,5},{5,6},{6,7},{7,8},{8,9},{9,10},{10,1... | collective-permute-start | bytes 270344 | tf_op jit(solution)/shard_map/ppermute | solution.py:666
  33.5 4.6 %copy-start.2 = (f32[22,8,128]{2,1,0:T(8,128)}, f32[22,8,128]{2,1,0:T(8,128)S(1)}, u32[]{:S(2)}) copy-start(f32[22,8,128]{2,1,0:T(8,128)S(1)} %collective-permute-done.4.high_ref) | copy-start | bytes 270340
  38.1 0.6 copy-start.3
  93.7 6.5 %collective-permute-start.5 = (f32[3,8,128]{2,1,0:T(8,128)}, f32[3,8,128]{2,1,0:T(8,128)S(1)}, u32[]{:S(2)}, u32[]{:S(2)}) collective-permute-start(f32[3,8,128]{2,1,0:T(8,128)} %get-tuple-element.8), channel_id=1, source_target_pairs={{0,1},{1,2},{2,3},{3,4},{4,5},{5,6},{6,7},{7,8},{8,9},{9,10},{10,1... | collective-permute-start | bytes 36872 | tf_op jit(solution)/shard_map/ppermute | solution.py:682
  95.7 5.6 %collective-permute-start.6 = (f32[3,8,128]{2,1,0:T(8,128)}, f32[3,8,128]{2,1,0:T(8,128)S(1)}, u32[]{:S(2)}, u32[]{:S(2)}) collective-permute-start(f32[3,8,128]{2,1,0:T(8,128)} %get-tuple-element.9), channel_id=1, source_target_pairs={{0,15},{1,0},{2,1},{3,2},{4,3},{5,4},{6,5},{7,6},{8,7},{9,8},{10,9... | collective-permute-start | bytes 36872 | tf_op jit(solution)/shard_map/ppermute | solution.py:682
  102.0 8.1 %collective-permute-start.7 = (f32[8,128]{1,0:T(8,128)S(1)}, f32[8,128]{1,0:T(8,128)S(1)}, u32[]{:S(2)}, u32[]{:S(2)}) collective-permute-start(f32[8,128]{1,0:T(8,128)S(1)} %get-tuple-element.10), channel_id=1, source_target_pairs={{0,16},{16,32},{32,48},{48,64},{64,80},{80,96},{96,112},{112,128},... | collective-permute-start | bytes 12296 | tf_op jit(solution)/shard_map/ppermute | solution.py:683
  108.2 5.8 %collective-permute-start.8 = (f32[8,128]{1,0:T(8,128)S(1)}, f32[8,128]{1,0:T(8,128)S(1)}, u32[]{:S(2)}, u32[]{:S(2)}) collective-permute-start(f32[8,128]{1,0:T(8,128)S(1)} %get-tuple-element.11), channel_id=1, source_target_pairs={{0,240},{16,0},{32,16},{48,32},{64,48},{80,64},{96,80},{112,96},{1... | collective-permute-start | bytes 12296 | tf_op jit(solution)/shard_map/ppermute | solution.py:684

commit v2 on v1

--- a/solution.py
+++ b/solution.py
@@ -9,13 +9,15 @@
 BF16 = jnp.bfloat16
 I32 = jnp.int32
 TILE = 256
-MAX_TILES = 128
+MAX_TILES = 129
 MAX_CORE_TILES = 32
 WINDOW = 64
+UNROLL = 3
 INTERPRET = False
 
-COLUMNS = [(2, 2), (2, 3), (3, 2), (3, 3)] + [
-    (y, z) for y in range(1, 5) for z in range(1, 5) if not (y in (2, 3) and z in (2, 3))
+COLUMNS = [
+    (1 + ((col >> 3) * 2 + ((col >> 1) & 1) + 1) % 4, 1 + (((col >> 2) & 1) * 2 + (col & 1) + 1) % 4)
+    for col in range(16)
 ]
 LIST_BASE = {1: 0, 2: 6, 3: 8, 4: 16}
 LIST_STEP = {1: 3, 2: 5, 3: 5, 4: 3}
@@ -98,7 +100,9 @@
     down_ref,
     table,
     mask_buf,
+    lists,
     raw,
+    counted_buf,
     rowbuf,
     buf,
     bes_buf,
@@ -143,52 +147,63 @@
                 table[comp, row] = jnp.broadcast_to(joined[comp : comp + 1], (8, 128))
 
     for col, (y, z) in enumerate(COLUMNS):
-        dy, b = {1: (-1, 1), 2: (0, 0), 3: (0, 1), 4: (1, 0)}[y]
-        dz, c = {1: (-1, 1), 2: (0, 0), 3: (0, 1), 4: (1, 0)}[z]
-        y_low = -1 if y <= 2 else 0
-        z_low = -1 if z <= 2 else 0
-        row_l = (dy + 1) * 3 + dz + 1
+        layer = layer_refs[(z >> 1) - 1]
         for xd in range(2):
-            tile = layer_refs[dz][LIST_BASE[y] + xd * LIST_STEP[y] + c].astype(I32)
-            g = tile & 7
-            r1 = ((tile >> 3) & 3) + 1
-            q1 = ((tile >> 5) & 3) + 1
-            p1 = ((tile >> 7) & 3) + 1
-            x_side = (1 - ((p1 >> 1) & 1)) ^ xd
-            y_index = (q1 >> 1) + (dy - 1 - y_low)
-            z_index = (r1 >> 1) + (dz - 1 - z_low)
-            lane = x_side * 64 + (p1 & 1) * 32 + (q1 & 1) * 16 + (r1 & 1) * 8 + g
-            lane_l = jnp.where(upper, 32, 0) + sub8 + (xd * 64 + b * 16 + c * 8)
-            row0 = (y_low + 1) * 3 + z_low + 1
-            y_zero = y_index == 0
-            z_zero = z_index == 0
-
-            def fetch(comp):
-                low = jnp.where(
-                    z_zero, lanes_of(table[comp, row0], lane), lanes_of(table[comp, row0 + 1], lane)
-                )
-                top = jnp.where(
-                    z_zero, lanes_of(table[comp, row0 + 3], lane), lanes_of(table[comp, row0 + 4], lane)
-                )
-                return jnp.where(y_zero, low, top)
-
-            d = [fetch(comp) - lanes_of(table[comp, row_l], lane_l) for comp in range(3)]
-            d[0] = jnp.where(d[0] > 12.0, d[0] - 24.0, jnp.where(d[0] < -12.0, d[0] + 24.0, d[0]))
-            species = fetch(3)
-            count = lanes_of(table[4, row_l], lane_l)
-            square = d[0] * d[0] + d[1] * d[1] + d[2] * d[2] + 0.25
-            slot = (lane8 & 63).astype(F32)
-            reach = (square < 36.0) & (slot < count)
-            inside = ((y_index >> 1) == 0) & ((z_index >> 1) == 0)
-            live = jnp.where(reach & inside, 1.0, 0.0)
-            code = (row0 + y_index * 3 + z_index) * 128 + lane
-            at = (col * 2 + xd) * 8
-            mask_buf[at : at + 8, :] = live
-            raw[0, at : at + 8, :] = d[0]
-            raw[1, at : at + 8, :] = d[1]
-            raw[2, at : at + 8, :] = d[2]
-            raw[3, at : at + 8, :] = species
-            raw[4, at : at + 8, :] = code.astype(F32)
+            lists[col * 2 + xd] = layer[LIST_BASE[y] + xd * LIST_STEP[y] + (z & 1)]
+
+    def place_of(part):
+        col, xd = part >> 1, part & 1
+        y = 1 + (((col >> 3) * 2 + ((col >> 1) & 1) + 1) & 3)
+        z = 1 + ((((col >> 2) & 1) * 2 + (col & 1) + 1) & 3)
+        lane = xd * 64 + (y & 1) * 16 + (z & 1) * 8
+        return y, z, xd, (y >> 1) * 3 + (z >> 1), lane
+
+    def distances(part, carry):
+        y, z, xd, row_l, base_l = place_of(part)
+        y_low = jnp.where(y >= 3, 1, 0)
+        z_low = jnp.where(z >= 3, 1, 0)
+        row0 = y_low * 3 + z_low
+        tile = lists[part].astype(I32)
+        r1 = ((tile >> 3) & 3) + 1
+        q1 = ((tile >> 5) & 3) + 1
+        p1 = ((tile >> 7) & 3) + 1
+        x_side = (1 - ((p1 >> 1) & 1)) ^ xd
+        y_index = (q1 >> 1) + ((y >> 1) - 1 - y_low)
+        z_index = (r1 >> 1) + ((z >> 1) - 1 - z_low)
+        lane = x_side * 64 + (p1 & 1) * 32 + (q1 & 1) * 16 + (r1 & 1) * 8 + (tile & 7)
+        lane_l = jnp.where(upper, 32, 0) + sub8 + base_l
+        y_zero = y_index == 0
+        z_zero = z_index == 0
+
+        def fetch(comp):
+            low = jnp.where(
+                z_zero, lanes_of(table[comp, row0], lane), lanes_of(table[comp, row0 + 1], lane)
+            )
+            top = jnp.where(
+                z_zero, lanes_of(table[comp, row0 + 3], lane), lanes_of(table[comp, row0 + 4], lane)
+            )
+            return jnp.where(y_zero, low, top)
+
+        d = [fetch(comp) - lanes_of(table[comp, row_l], lane_l) for comp in range(3)]
+        d[0] = jnp.where(d[0] > 12.0, d[0] - 24.0, jnp.where(d[0] < -12.0, d[0] + 24.0, d[0]))
+        species = fetch(3)
+        count = lanes_of(table[4, row_l], lane_l)
+        square = d[0] * d[0] + d[1] * d[1] + d[2] * d[2] + 0.25
+        slot = (lane8 & 63).astype(F32)
+        reach = (square < 36.0) & (slot < count)
+        inside = ((y_index >> 1) == 0) & ((z_index >> 1) == 0)
+        live = jnp.where(reach & inside, 1.0, 0.0)
+        code = (row0 + y_index * 3 + z_index) * 128 + lane
+        rows = pl.ds(pl.multiple_of(part * 8, 8), 8)
+        mask_buf[rows, :] = live
+        raw[0, rows, :] = d[0]
+        raw[1, rows, :] = d[1]
+        raw[2, rows, :] = d[2]
+        raw[3, rows, :] = species
+        raw[4, rows, :] = code.astype(F32)
+        return carry
+
+    lax.fori_loop(0, 32, distances, 0, unroll=4)
 
     mask = mask_buf[...].astype(BF16)
     upto = jnp.where(iota((128, 128), 0) <= iota((128, 128), 1), 1.0, 0.0).astype(BF16)
@@ -201,25 +216,28 @@
     copy = pltpu.make_async_copy(offs_vmem, offs, sem)
     copy.start()
 
-    for col, (y, z) in enumerate(COLUMNS):
-        dy, b = {1: (-1, 1), 2: (0, 0), 3: (0, 1), 4: (1, 0)}[y]
-        dz, c = {1: (-1, 1), 2: (0, 0), 3: (0, 1), 4: (1, 0)}[z]
-        row_l = (dy + 1) * 3 + dz + 1
-        for xd in range(2):
-            at = (col * 2 + xd) * 8
-            counted = within[at : at + 8, :]
-            wanted = (lane8 + 1).astype(F32)
-            place = jnp.zeros((8, 128), I32)
-            for step in (64, 32, 16, 8, 4, 2, 1):
-                probe = lanes_of(counted, place + (step - 1))
-                place = jnp.where(probe < wanted, place + step, place)
-            half = jnp.where(place >= 64, 1, 0)
-            atom = (at + sub8) * 2 + half
-            code_l = row_l * 128 + xd * 64 + b * 16 + c * 8 + sub8 + half * 32
-            fields = [lanes_of(raw[k, at : at + 8, :], place) for k in range(5)]
-            fields += [atom.astype(F32), code_l.astype(F32)]
-            for k, field in enumerate(fields):
-                rowbuf[pl.ds(at * 8 + k, 8, stride=8), :] = field
+    counted_buf[...] = within
+
+    def to_front(part, carry):
+        _, _, _, row_l, base_l = place_of(part)
+        at = pl.multiple_of(part * 8, 8)
+        rows = pl.ds(at, 8)
+        counted = counted_buf[rows, :]
+        wanted = (lane8 + 1).astype(F32)
+        place = jnp.zeros((8, 128), I32)
+        for step in (64, 32, 16, 8, 4, 2, 1):
+            probe = lanes_of(counted, place + (step - 1))
+            place = jnp.where(probe < wanted, place + step, place)
+        half = jnp.where(place >= 64, 1, 0)
+        atom = (at + sub8) * 2 + half
+        code_l = row_l * 128 + base_l + sub8 + half * 32
+        fields = [lanes_of(raw[k, rows, :], place) for k in range(5)]
+        fields += [atom.astype(F32), code_l.astype(F32)]
+        for k, field in enumerate(fields):
+            rowbuf[pl.ds(at * 8 + k, 8, stride=8), :] = field
+        return carry
+
+    lax.fori_loop(0, 32, to_front, 0, unroll=16)
 
     copy.wait()
 
@@ -233,17 +251,14 @@
         last_row[start >> 8] = r
         return jnp.where(shift + length >= 128, rolled, current)
 
-    current = lax.fori_loop(0, 256, join_row, jnp.zeros((8, 128), F32), unroll=8)
+    current = lax.fori_loop(0, 256, join_row, jnp.zeros((8, 128), F32), unroll=16)
     total = offs[0, 255] + offs[0, 511]
     core_total = offs[0, 64]
     buf[pl.ds((total >> 7) * 8, 8), :] = current
     last_row[jnp.maximum(total - 1, 0) >> 8] = 255
     tiles = (total + (TILE - 1)) // TILE
     core_tiles = (core_total + (TILE - 1)) // TILE
-
-    column_of = jnp.zeros((8, 128), I32)
-    for col, (y, z) in enumerate(COLUMNS):
-        column_of = jnp.where(lane8 == (y - 1) * 4 + z - 1, col, column_of)
+    steps = (tiles + UNROLL - 1) // UNROLL
 
     def basis(chunk, carry):
         at = chunk * 64
@@ -312,7 +327,9 @@
         y = row_y * 2 + ((lane >> 4) & 1) - 1
         z = row_z * 2 + ((lane >> 3) & 1) - 1
         near = (y >= 0) & (y < 4) & (z >= 0) & (z < 4)
-        column = lanes_of(column_of, jnp.where(near, y * 4 + z, 0))
+        y = (y + 3) & 3
+        z = (z + 3) & 3
+        column = (y >> 1) * 8 + (z >> 1) * 4 + (y & 1) * 2 + (z & 1)
         source = column * 32 + ((lane >> 6) & 1) * 16 + (lane & 7) * 2 + ((lane >> 5) & 1)
         source = jnp.where(near, source, -1)
         both = code.astype(F32) * 2048.0 + code_l
@@ -321,7 +338,7 @@
             pair_buf[pl.ds(at + k, 8, stride=8), :] = value
         return carry
 
-    lax.fori_loop(0, (total + 1023) // 1024, basis, 0)
+    lax.fori_loop(0, (steps * UNROLL * TILE + 1023) // 1024, basis, 0)
 
     fi3 = jnp.concatenate([fi_ref[...], jnp.zeros((24, 64), F32)], axis=0)
     si3 = jnp.concatenate([si_ref[...], jnp.zeros((24, 64), F32)], axis=0)
@@ -342,8 +359,8 @@
     si_b3 = inner_back(si_ref)
     fo_t3 = three_weights(fo_ref[...].T, 1)
     so_t3 = three_weights(so_ref[...].T, 1)
-    fo_b3 = three_weights(fo_ref[...], 1)
-    so_b3 = three_weights(so_ref[...], 1)
+    fo_b3 = jnp.concatenate(split(fo_ref[...]), axis=0)
+    so_b3 = jnp.concatenate(split(so_ref[...]), axis=0)
     emb_pad[...] = jnp.zeros((128, 128), F32)
     emb_pad[0:89, :] = emb_ref[...]
     emb_t2 = jnp.concatenate(split(emb_pad[...].T), axis=1)
@@ -367,41 +384,65 @@
         return dot(emb_t2, jnp.concatenate([hot, hot], axis=0))
 
     def first_of(t):
-        return jnp.where(t == 0, 0, last_row[jnp.maximum(t - 1, 0)]) * 2
+        before = jnp.clip(t - 1, 0, jnp.maximum(tiles - 1, 0))
+        return jnp.where(t == 0, 0, last_row[before]) * 2
 
     acc[...] = jnp.zeros(acc.shape, F32)
 
-    def layer_one(t, carry):
-        hidden, slope = hidden_of(t, fi_t3)
-        saved_slope[t] = slope
-        weights = dot(fo_t3, three(hidden, 0))
-        pair = tile_rows(pair_buf, t)
-        sender = sender_of(pair[4:5])
-        m_high, m_low = split(weights[0:128] * sender)
-        rg = weights[128:256] * sender
-        saved_rg[t] = rg
-        v_high, v_low = split(rg)
-        saved_pair_grad[t] = jnp.zeros((8, TILE), F32)
-        unit = [split(pair[k : k + 1]) for k in range(3)]
-        base = first_of(t) & -8
-        windows = (last_row[t] * 2 + 1 - base) // WINDOW + 1
-
-        def window(w, carry):
+    def layer_one(step, carry):
+        done = []
+        for part in range(UNROLL):
+            t = step * UNROLL + part
+            hidden, slope = hidden_of(t, fi_t3)
+            saved_slope[t] = slope
+            weights = dot(fo_t3, three(hidden, 0))
+            pair = tile_rows(pair_buf, t)
+            sender = sender_of(pair[4:5])
+            message = split(weights[0:128] * sender)
+            rg = weights[128:256] * sender
+            saved_rg[t] = rg
+            saved_pair_grad[t] = jnp.zeros((8, TILE), F32)
+            done.append((t, first_of(t) & -8, pair, message, split(rg)))
+
+        def window(entry, w):
+            _, base, pair, (m_high, m_low), (v_high, v_low) = entry
             at = base + w * WINDOW
+            unit = [split(pair[k : k + 1]) for k in range(3)]
             hot = onehot(pair[6:7] - at.astype(F32), WINDOW)
             u_high = jnp.concatenate([hot * high for high, _ in unit], axis=0)
             u_low = jnp.concatenate([hot * low for _, low in unit], axis=0)
             m = dot_t(hot, m_high) + dot_t(hot, m_low)
             v = dot_t(u_high, v_high) + dot_t(u_high, v_low) + dot_t(u_low, v_high)
-            rows = pl.ds(pl.multiple_of(at, 8), WINDOW)
+            return pl.ds(pl.multiple_of(at, 8), WINDOW), m, v
+
+        def add(rows, m, v):
             acc[0, rows, :] += m
             for x in range(3):
                 acc[1 + x, rows, :] += v[x * WINDOW : (x + 1) * WINDOW]
-            return carry
-
-        return lax.fori_loop(0, windows, window, carry)
-
-    lax.fori_loop(0, tiles, layer_one, 0)
+
+        for sums in [window(entry, 0) for entry in done]:
+            add(*sums)
+        counts = [
+            jnp.where(t < tiles, (last_row[t] * 2 + 1 - base) // WINDOW + 1, 1)
+            for t, base, _, _, _ in done
+        ]
+        most = counts[0]
+        for count in counts[1:]:
+            most = jnp.maximum(most, count)
+
+        @pl.when(most > 1)
+        def _():
+            for count, entry in zip(counts, done):
+
+                def more(w, carry, entry=entry):
+                    add(*window(entry, w))
+                    return carry
+
+                lax.fori_loop(1, count, more, 0)
+
+        return carry
+
+    lax.fori_loop(0, steps, layer_one, 0)
 
     parts = []
     for group in range(4):
@@ -409,11 +450,10 @@
         for sub in range(4):
             col = group * 4 + sub
             y, z = COLUMNS[col]
-            dy, b = {1: (-1, 1), 2: (0, 0), 3: (0, 1), 4: (1, 0)}[y]
-            dz, c = {1: (-1, 1), 2: (0, 0), 3: (0, 1), 4: (1, 0)}[z]
+            row, b, c = (y >> 1) * 3 + (z >> 1), y & 1, z & 1
             local = lane8 & 31
             index = ((local >> 4) & 1) * 64 + (local & 1) * 32 + ((local >> 1) & 7) + b * 16 + c * 8
-            got = lanes_of(table[3, (dy + 1) * 3 + dz + 1], index)
+            got = lanes_of(table[3, row], index)
             merged = got if merged is None else jnp.where((lane8 >> 5) == sub, got, merged)
         parts.append(merged)
     species_row = jnp.concatenate(parts, axis=1)[0:1]
@@ -471,7 +511,9 @@
     feat_grad[0:128, 0:128] = mixed_grad + rf_col
 
     def radial_back(t, slope, grad, outer3, inner3):
-        hidden_grad = dot(outer3, three(grad, 0)) * slope
+        high, low = split(grad)
+        both = dot(outer3, high)
+        hidden_grad = (both[0:64] + both[64:128] + dot(outer3[0:64], low)) * slope
         bes_grad = dot(inner3, three(hidden_grad, 0))[0:8]
         return jnp.sum(bes_grad * tile_rows(dbes_buf, t), axis=0, keepdims=True)
 
@@ -516,52 +558,69 @@
 
     box_acc[...] = jnp.zeros((96, 128), F32)
 
-    def layer_one_back(t, carry):
-        pair = tile_rows(pair_buf, t)
-        first = first_of(t) >> 7
-        last = (last_row[t] * 2 + 1) >> 7
-
-        def expanded(w):
+    def layer_one_back(step, carry):
+        group = []
+        for part in range(UNROLL):
+            t = step * UNROLL + part
+            group.append((part, t, tile_rows(pair_buf, t), first_of(t) >> 7))
+
+        def expanded(pair, w):
             member = onehot(pair[6:7] - (w * 128).astype(F32), 128)
             return dot(grad_lhs[w], jnp.concatenate([member, member], axis=0))
 
-        expand[...] = expanded(first)
-
-        def more(w, carry):
-            expand[...] += expanded(w)
-            return carry
-
-        lax.fori_loop(first + 1, last + 1, more, 0)
-        sender = sender_of(pair[4:5])
-        rg = saved_rg[t]
-        v_grad = [expand[128 + x * 128 : 256 + x * 128, :] for x in range(3)]
-        along = pair[0:1] * v_grad[0] + pair[1:2] * v_grad[1] + pair[2:3] * v_grad[2]
-        radial_grad = jnp.concatenate([expand[0:128, :] * sender, along * sender], axis=0)
-        earlier = saved_pair_grad[t]
-        rho_grad = radial_back(t, saved_slope[t], radial_grad, fo_b3, fi_b3) + earlier[0:1]
-        unit_grad = [
-            jnp.sum(rg * v_grad[x], axis=0, keepdims=True) + earlier[1 + x : 2 + x] for x in range(3)
+        for part, t, pair, first in group:
+            expand[part] = expanded(pair, first)
+        lasts = [
+            jnp.where(t < tiles, (last_row[t] * 2 + 1) >> 7, 0)
+            for _, t, _, _ in group
         ]
-        unit = [pair[x : x + 1] for x in range(3)]
-        inner = unit[0] * unit_grad[0] + unit[1] * unit_grad[1] + unit[2] * unit_grad[2]
-        inv = pair[3:4]
-        values = []
-        for x in range(3):
-            value = (unit_grad[x] - unit[x] * inner) * inv + rho_grad * unit[x]
-            high = value.astype(BF16).astype(F32)
-            values += [high, value - high]
-        both = pair[7:8].astype(I32)
-
-        def spread(code, sign):
-            row = jnp.broadcast_to(code >> 7, (16, TILE)) == iota((16, TILE), 0)
-            stack = [jnp.where(row, sign * value, 0.0) for value in values]
-            lane = jnp.where(iota((128, TILE), 0) == (code & 127), 1.0, 0.0).astype(BF16)
-            return dot_t(jnp.concatenate(stack, axis=0).astype(BF16), lane)
-
-        box_acc[...] += spread(both >> 11, 1.0) + spread(both & 2047, -1.0)
+        crossing = lasts[0] > group[0][3]
+        for last, entry in zip(lasts[1:], group[1:]):
+            crossing = crossing | (last > entry[3])
+
+        @pl.when(crossing)
+        def _():
+            for last, (part, t, pair, first) in zip(lasts, group):
+
+                def more(w, carry, part=part, pair=pair):
+                    expand[part] += expanded(pair, w)
+                    return carry
+
+                lax.fori_loop(first + 1, last + 1, more, 0)
+
+        spreads = []
+        for part, t, pair, first in group:
+            sender = sender_of(pair[4:5])
+            rg = saved_rg[t]
+            v_grad = [expand[part, 128 + x * 128 : 256 + x * 128, :] for x in range(3)]
+            along = pair[0:1] * v_grad[0] + pair[1:2] * v_grad[1] + pair[2:3] * v_grad[2]
+            radial_grad = jnp.concatenate(
+                [expand[part, 0:128, :] * sender, along * sender], axis=0
+            )
+            earlier = saved_pair_grad[t]
+            rho_grad = radial_back(t, saved_slope[t], radial_grad, fo_b3, fi_b3) + earlier[0:1]
+            unit_grad = [
+                jnp.sum(rg * v_grad[x], axis=0, keepdims=True) + earlier[1 + x : 2 + x]
+                for x in range(3)
+            ]
+            unit = [pair[x : x + 1] for x in range(3)]
+            inner = unit[0] * unit_grad[0] + unit[1] * unit_grad[1] + unit[2] * unit_grad[2]
+            inv = pair[3:4]
+            values = []
+            for x in range(3):
+                value = (unit_grad[x] - unit[x] * inner) * inv + rho_grad * unit[x]
+                high = value.astype(BF16).astype(F32)
+                values += [high, value - high]
+            both = pair[7:8].astype(I32)
+            for code, sign in ((both >> 11, 1.0), (both & 2047, -1.0)):
+                row = jnp.broadcast_to(code >> 7, (16, TILE)) == iota((16, TILE), 0)
+                stack = [jnp.where(row, sign * value, 0.0) for value in values]
+                lane = jnp.where(iota((128, TILE), 0) == (code & 127), 1.0, 0.0).astype(BF16)
+                spreads.append(dot_t(jnp.concatenate(stack, axis=0).astype(BF16), lane))
+        box_acc[...] += sum(spreads[1:], spreads[0])
         return carry
 
-    lax.fori_loop(0, tiles, layer_one_back, 0)
+    lax.fori_loop(0, steps, layer_one_back, 0)
 
     for comp in range(3):
         grid = box_acc[comp * 32 : comp * 32 + 16, :] + box_acc[comp * 32 + 16 : comp * 32 + 32, :]
@@ -576,11 +635,13 @@
 
 def pair_program(own, low, high, weights):
     vm = pltpu.VMEM
-    pair_rows = (MAX_TILES * 2 + 8) * 8
+    pair_rows = (MAX_TILES * 2 + 6) * 8
     scratch = [
         vm((5, 9, 8, 128), F32),
         vm((256, 128), F32),
+        vm((32, 8, 128), F32),
         vm((5, 256, 128), F32),
+        vm((256, 128), F32),
         vm((2048, 128), F32),
         vm((pair_rows, 128), F32),
         vm((pair_rows, 128), F32),
@@ -597,7 +658,7 @@
         vm((512, 512), F32),
         vm((128, 128), F32),
         vm((4, 512, 256), BF16),
-        vm((512, TILE), F32),
+        vm((UNROLL, 512, TILE), F32),
         vm((MAX_TILES, 128, TILE), F32),
         vm((MAX_TILES, 64, TILE), F32),
         vm((MAX_CORE_TILES, 512, TILE), F32),

time: 115 us -> 94.8 us (0.82)
  the two profiles are of different devices: /device:TPU:25 before, /device:TPU:13 now
where the time goes in v2:
time: 94.8 us; the launch traced here: 94.2 us
  starting transfers between devices  41.2 us (43%)
  Pallas kernels  33.3 us (35%)
  waiting for transfers between devices  16.1 us (17%)
  other arithmetic  2.03 us (2%)
    pallas_call x1, Pallas kernels, pair_program(): pl.pallas_call(main_kernel, out_shape=(jax.ShapeDtypeStruct((1, 64), F32)...  31.8 us
    ppermute x1, starting transfers between devices, shards(): high = lax.ppermute(layer, 'gz', ring('gz', -1))  11.1 us
    ppermute x1, starting transfers between devices, shards(): total = folded[1] + lax.ppermute(folded[2], 'gy', ring('gy', 1))  9.41 us
    ppermute x1, waiting for transfers between devices, shards(): low = lax.ppermute(layer, 'gz', ring('gz', 1))  4.65 us
    ppermute x1, starting transfers between devices, shards(): lax.ppermute(down, 'gz', ring('gz', -1))  4.57 us
    ppermute x1, starting transfers between devices, shards(): below = lax.ppermute(both, 'gy', ring('gy', 1))  4.54 us
    ppermute x1, waiting for transfers between devices, shards(): above = lax.ppermute(both, 'gy', ring('gy', -1))  4.22 us
    ppermute x1, starting transfers between devices, shards(): partner = lax.ppermute(packed, 'gx', ring('gx', 1))  3.91 us
  transfers between devices with their start and end apart: 9, of which 5 were waited for; matrix products, arithmetic and copies ran while one was open for 0% of the time, Pallas kernels for 0%

profile of v2, /device:TPU:13, one launch (start us, length us, event | category | flops | bytes accessed | tf_op | source)
XLA Modules:
  0.0 94.2 jit_solution(3248440213942106640)
XLA Ops:
  0.6 1.5 %shard_map.158 = f32[5,8,128]{2,1,0:T(8,128)} custom-call(f32[3,64]{1,0:T(4,128)} %pos_ref.1, s32[1,64]{1,0:T(1,128)} %bitcast.15, s32[1,64]{1,0:T(1,128)} %bitcast.16, s32[64,64]{1,0:T(8,128)} %neighbors_ref.1), custom_call_target="tpu_custom_call" | custom-call | tf_op jit(solution)/shard_map/pallas_call | solution.py:684
  2.1 3.9 %collective-permute-start = (f32[5,8,128]{2,1,0:T(8,128)}, f32[5,8,128]{2,1,0:T(8,128)S(1)}, u32[]{:S(2)}, u32[]{:S(2)}) collective-permute-start(f32[5,8,128]{2,1,0:T(8,128)} %shard_map.158), channel_id=1, source_target_pairs={{0,256},{256,0},{1,257},{257,1},{2,258},{258,2},{3,259},{259,3},{4... | collective-permute-start | bytes 61448 | tf_op jit(solution)/shard_map/ppermute | solution.py:722
  6.0 2.3 %collective-permute-done = f32[5,8,128]{2,1,0:T(8,128)S(1)} collective-permute-done((f32[5,8,128]{2,1,0:T(8,128)}, f32[5,8,128]{2,1,0:T(8,128)S(1)}, u32[]{:S(2)}, u32[]{:S(2)}) %collective-permute-start) | collective-permute-done | bytes 20512 | tf_op jit(solution)/shard_map/ppermute | solution.py:722
  8.4 0.7 pad_maximum_fusion
  9.1 0.0 copy-start
  9.1 4.5 %collective-permute-start.1 = (f32[10,8,128]{2,1,0:T(8,128)S(1)}, f32[10,8,128]{2,1,0:T(8,128)S(1)}, u32[]{:S(2)}, u32[]{:S(2)}) collective-permute-start(f32[10,8,128]{2,1,0:T(8,128)S(1)} %pad_maximum_fusion), channel_id=1, source_target_pairs={{0,16},{16,32},{32,48},{48,64},{64,80},{80,96},{96,112},{112,128},... | collective-permute-start | bytes 122888 | tf_op jit(solution)/shard_map/ppermute | solution.py:724
  13.6 1.9 %collective-permute-start.2 = (f32[10,8,128]{2,1,0:T(8,128)S(1)}, f32[10,8,128]{2,1,0:T(8,128)S(1)}, u32[]{:S(2)}, u32[]{:S(2)}) collective-permute-start(f32[10,8,128]{2,1,0:T(8,128)S(1)} %pad_maximum_fusion), channel_id=1, source_target_pairs={{0,240},{16,0},{32,16},{48,32},{64,48},{80,64},{96,80},{112,96},{1... | collective-permute-start | bytes 122888 | tf_op jit(solution)/shard_map/ppermute | solution.py:725
  15.6 0.0 collective-permute-done.1
  15.6 0.0 copy-done
  15.6 4.2 %collective-permute-done.2 = f32[10,8,128]{2,1,0:T(8,128)S(1)} collective-permute-done((f32[10,8,128]{2,1,0:T(8,128)S(1)}, f32[10,8,128]{2,1,0:T(8,128)S(1)}, u32[]{:S(2)}, u32[]{:S(2)}) %collective-permute-start.2) | collective-permute-done | bytes 40992 | tf_op jit(solution)/shard_map/ppermute | solution.py:725
  19.9 0.0 copy-start.1
  19.9 11.1 %collective-permute-start.4 = (f32[22,8,128]{2,1,0:T(8,128)S(1)}, f32[22,8,128]{2,1,0:T(8,128)S(1)}, u32[]{:S(2)}, u32[]{:S(2)}) collective-permute-start(f32[22,8,128]{2,1,0:T(8,128)S(1)} %constant_dynamic-update-slice_fusion.own_ref), channel_id=1, source_target_pairs={{0,15},{1,0},{2,1},{3,2},{4,3},{5,4},{6,5},{7,6},{8,7},{9,8},{10,9... | collective-permute-start | bytes 270344 | tf_op jit(solution)/shard_map/ppermute | solution.py:728
  31.0 1.9 %collective-permute-start.3 = (f32[22,8,128]{2,1,0:T(8,128)S(1)}, f32[22,8,128]{2,1,0:T(8,128)S(1)}, u32[]{:S(2)}, u32[]{:S(2)}) collective-permute-start(f32[22,8,128]{2,1,0:T(8,128)S(1)} %constant_dynamic-update-slice_fusion.own_ref), channel_id=1, source_target_pairs={{0,1},{1,2},{2,3},{3,4},{4,5},{5,6},{6,7},{7,8},{8,9},{9,10},{10,1... | collective-permute-start | bytes 270344 | tf_op jit(solution)/shard_map/ppermute | solution.py:727
  32.9 0.0 collective-permute-done.4.high_ref
  32.9 0.0 copy-start.2
  32.9 4.6 %collective-permute-done.3.low_ref = f32[22,8,128]{2,1,0:T(8,128)S(1)} collective-permute-done((f32[22,8,128]{2,1,0:T(8,128)S(1)}, f32[22,8,128]{2,1,0:T(8,128)S(1)}, u32[]{:S(2)}, u32[]{:S(2)}) %collective-permute-start.3) | collective-permute-done | bytes 90144 | tf_op jit(solution)/shard_map/ppermute | solution.py:727
  37.6 0.0 copy-start.3
  37.6 0.0 copy-done.1
  37.6 0.0 copy-done.2
  37.6 0.6 copy-done.3
  38.2 31.8 %shard_map.159 = (f32[1,64]{1,0:T(1,128)}, f32[3,8,128]{2,1,0:T(8,128)}, f32[3,8,128]{2,1,0:T(8,128)}, f32[3,8,128]{2,1,0:T(8,128)}) custom-call(f32[22,8,128]{2,1,0:T(8,128)} %copy-done.1, f32[22,8,128]{2,1,0:T(8,128)} %copy-done.3, f32[22,8,128]{2,1,0:T(8,128)} %copy-done.2, f32[89,128]{1,0:T(8,128)} %emb_ref.1, f32[8,64]{1,0:T(8,128)} %fi_ref.1, ...), custom_call_target="tpu_custom_call" | custom-call | tf_op jit(solution)/shard_map/pallas_call | solution.py:671
  70.1 1.9 %collective-permute-start.5 = (f32[3,8,128]{2,1,0:T(8,128)}, f32[3,8,128]{2,1,0:T(8,128)S(1)}, u32[]{:S(2)}, u32[]{:S(2)}) collective-permute-start(f32[3,8,128]{2,1,0:T(8,128)} %get-tuple-element.8), channel_id=1, source_target_pairs={{0,1},{1,2},{2,3},{3,4},{4,5},{5,6},{6,7},{7,8},{8,9},{9,10},{10,1... | collective-permute-start | bytes 36872 | tf_op jit(solution)/shard_map/ppermute | solution.py:743
  72.0 4.6 %collective-permute-start.6 = (f32[3,8,128]{2,1,0:T(8,128)}, f32[3,8,128]{2,1,0:T(8,128)S(1)}, u32[]{:S(2)}, u32[]{:S(2)}) collective-permute-start(f32[3,8,128]{2,1,0:T(8,128)} %get-tuple-element.9), channel_id=1, source_target_pairs={{0,15},{1,0},{2,1},{3,2},{4,3},{5,4},{6,5},{7,6},{8,7},{9,8},{10,9... | collective-permute-start | bytes 36872 | tf_op jit(solution)/shard_map/ppermute | solution.py:743
  76.6 0.0 collective-permute-done.5
  76.6 1.0 %collective-permute-done.6 = f32[3,8,128]{2,1,0:T(8,128)S(1)} collective-permute-done((f32[3,8,128]{2,1,0:T(8,128)}, f32[3,8,128]{2,1,0:T(8,128)S(1)}, u32[]{:S(2)}, u32[]{:S(2)}) %collective-permute-start.6) | collective-permute-done | bytes 12320 | tf_op jit(solution)/shard_map/ppermute | solution.py:743
  77.6 0.7 add_add_fusion
  78.3 9.4 %collective-permute-start.7 = (f32[8,128]{1,0:T(8,128)S(1)}, f32[8,128]{1,0:T(8,128)S(1)}, u32[]{:S(2)}, u32[]{:S(2)}) collective-permute-start(f32[8,128]{1,0:T(8,128)S(1)} %get-tuple-element.10), channel_id=1, source_target_pairs={{0,16},{16,32},{32,48},{48,64},{64,80},{80,96},{96,112},{112,128},... | collective-permute-start | bytes 12296 | tf_op jit(solution)/shard_map/ppermute | solution.py:744
  87.8 1.9 %collective-permute-start.8 = (f32[8,128]{1,0:T(8,128)S(1)}, f32[8,128]{1,0:T(8,128)S(1)}, u32[]{:S(2)}, u32[]{:S(2)}) collective-permute-start(f32[8,128]{1,0:T(8,128)S(1)} %get-tuple-element.11), channel_id=1, source_target_pairs={{0,240},{16,0},{32,16},{48,32},{64,48},{80,64},{96,80},{112,96},{1... | collective-permute-start | bytes 12296 | tf_op jit(solution)/shard_map/ppermute | solution.py:745
  89.7 0.0 collective-permute-done.7
  89.7 3.9 %collective-permute-done.8 = f32[8,128]{1,0:T(8,128)S(1)} collective-permute-done((f32[8,128]{1,0:T(8,128)S(1)}, f32[8,128]{1,0:T(8,128)S(1)}, u32[]{:S(2)}, u32[]{:S(2)}) %collective-permute-start.8) | collective-permute-done | bytes 4128 | tf_op jit(solution)/shard_map/ppermute | solution.py:745
  93.6 0.6 slice_negate_fusion
  (9 shorter events, 0.0 us)
Async XLA Ops:
  2.1 6.2 %collective-permute-start = (f32[5,8,128]{2,1,0:T(8,128)}, f32[5,8,128]{2,1,0:T(8,128)S(1)}, u32[]{:S(2)}, u32[]{:S(2)}) collective-permute-start(f32[5,8,128]{2,1,0:T(8,128)} %shard_map.158), channel_id=1, source_target_pairs={{0,256},{256,0},{1,257},{257,1},{2,258},{258,2},{3,259},{259,3},{4... | collective-permute-start | bytes 61448 | tf_op jit(solution)/shard_map/ppermute | solution.py:722
  9.1 6.5 %copy-start = (f32[5,8,128]{2,1,0:T(8,128)S(1)}, f32[5,8,128]{2,1,0:T(8,128)}, u32[]{:S(2)}) copy-start(f32[5,8,128]{2,1,0:T(8,128)} %shard_map.158) | copy-start | bytes 61444
  9.1 6.5 %collective-permute-start.1 = (f32[10,8,128]{2,1,0:T(8,128)S(1)}, f32[10,8,128]{2,1,0:T(8,128)S(1)}, u32[]{:S(2)}, u32[]{:S(2)}) collective-permute-start(f32[10,8,128]{2,1,0:T(8,128)S(1)} %pad_maximum_fusion), channel_id=1, source_target_pairs={{0,16},{16,32},{32,48},{48,64},{64,80},{80,96},{96,112},{112,128},... | collective-permute-start | bytes 122888 | tf_op jit(solution)/shard_map/ppermute | solution.py:724
  13.6 6.2 %collective-permute-start.2 = (f32[10,8,128]{2,1,0:T(8,128)S(1)}, f32[10,8,128]{2,1,0:T(8,128)S(1)}, u32[]{:S(2)}, u32[]{:S(2)}) collective-permute-start(f32[10,8,128]{2,1,0:T(8,128)S(1)} %pad_maximum_fusion), channel_id=1, source_target_pairs={{0,240},{16,0},{32,16},{48,32},{64,48},{80,64},{96,80},{112,96},{1... | collective-permute-start | bytes 122888 | tf_op jit(solution)/shard_map/ppermute | solution.py:725
  19.9 17.7 %copy-start.1 = (f32[22,8,128]{2,1,0:T(8,128)}, f32[22,8,128]{2,1,0:T(8,128)S(1)}, u32[]{:S(2)}) copy-start(f32[22,8,128]{2,1,0:T(8,128)S(1)} %constant_dynamic-update-slice_fusion.own_ref) | copy-start | bytes 270340
  19.9 13.1 %collective-permute-start.4 = (f32[22,8,128]{2,1,0:T(8,128)S(1)}, f32[22,8,128]{2,1,0:T(8,128)S(1)}, u32[]{:S(2)}, u32[]{:S(2)}) collective-permute-start(f32[22,8,128]{2,1,0:T(8,128)S(1)} %constant_dynamic-update-slice_fusion.own_ref), channel_id=1, source_target_pairs={{0,15},{1,0},{2,1},{3,2},{4,3},{5,4},{6,5},{7,6},{8,7},{9,8},{10,9... | collective-permute-start | bytes 270344 | tf_op jit(solution)/shard_map/ppermute | solution.py:728
  31.0 6.6 %collective-permute-start.3 = (f32[22,8,128]{2,1,0:T(8,128)S(1)}, f32[22,8,128]{2,1,0:T(8,128)S(1)}, u32[]{:S(2)}, u32[]{:S(2)}) collective-permute-start(f32[22,8,128]{2,1,0:T(8,128)S(1)} %constant_dynamic-update-slice_fusion.own_ref), channel_id=1, source_target_pairs={{0,1},{1,2},{2,3},{3,4},{4,5},{5,6},{6,7},{7,8},{8,9},{9,10},{10,1... | collective-permute-start | bytes 270344 | tf_op jit(solution)/shard_map/ppermute | solution.py:727
  32.9 4.7 %copy-start.2 = (f32[22,8,128]{2,1,0:T(8,128)}, f32[22,8,128]{2,1,0:T(8,128)S(1)}, u32[]{:S(2)}) copy-start(f32[22,8,128]{2,1,0:T(8,128)S(1)} %collective-permute-done.4.high_ref) | copy-start | bytes 270340
  37.6 0.6 copy-start.3
  70.1 6.5 %collective-permute-start.5 = (f32[3,8,128]{2,1,0:T(8,128)}, f32[3,8,128]{2,1,0:T(8,128)S(1)}, u32[]{:S(2)}, u32[]{:S(2)}) collective-permute-start(f32[3,8,128]{2,1,0:T(8,128)} %get-tuple-element.8), channel_id=1, source_target_pairs={{0,1},{1,2},{2,3},{3,4},{4,5},{5,6},{6,7},{7,8},{8,9},{9,10},{10,1... | collective-permute-start | bytes 36872 | tf_op jit(solution)/shard_map/ppermute | solution.py:743
  72.0 5.6 %collective-permute-start.6 = (f32[3,8,128]{2,1,0:T(8,128)}, f32[3,8,128]{2,1,0:T(8,128)S(1)}, u32[]{:S(2)}, u32[]{:S(2)}) collective-permute-start(f32[3,8,128]{2,1,0:T(8,128)} %get-tuple-element.9), channel_id=1, source_target_pairs={{0,15},{1,0},{2,1},{3,2},{4,3},{5,4},{6,5},{7,6},{8,7},{9,8},{10,9... | collective-permute-start | bytes 36872 | tf_op jit(solution)/shard_map/ppermute | solution.py:743
  78.3 11.4 %collective-permute-start.7 = (f32[8,128]{1,0:T(8,128)S(1)}, f32[8,128]{1,0:T(8,128)S(1)}, u32[]{:S(2)}, u32[]{:S(2)}) collective-permute-start(f32[8,128]{1,0:T(8,128)S(1)} %get-tuple-element.10), channel_id=1, source_target_pairs={{0,16},{16,32},{32,48},{48,64},{64,80},{80,96},{96,112},{112,128},... | collective-permute-start | bytes 12296 | tf_op jit(solution)/shard_map/ppermute | solution.py:744
  87.8 5.8 %collective-permute-start.8 = (f32[8,128]{1,0:T(8,128)S(1)}, f32[8,128]{1,0:T(8,128)S(1)}, u32[]{:S(2)}, u32[]{:S(2)}) collective-permute-start(f32[8,128]{1,0:T(8,128)S(1)} %get-tuple-element.11), channel_id=1, source_target_pairs={{0,240},{16,0},{32,16},{48,32},{64,48},{80,64},{96,80},{112,96},{1... | collective-permute-start | bytes 12296 | tf_op jit(solution)/shard_map/ppermute | solution.py:745

commit v3 on v2

--- a/solution.py
+++ b/solution.py
@@ -1,3 +1,5 @@
+import functools
+
 import jax
 import jax.numpy as jnp
 from jax import lax
@@ -13,6 +15,7 @@
 MAX_CORE_TILES = 32
 WINDOW = 64
 UNROLL = 3
+KEPT_TILES = 30
 INTERPRET = False
 
 COLUMNS = [
@@ -120,9 +123,8 @@
     w_acc,
     grad_lhs,
     expand,
-    saved_rg,
-    saved_slope,
-    saved_feat,
+    saved,
+    saved_core,
     saved_pair_grad,
     box_acc,
     emb_pad,
@@ -349,18 +351,10 @@
         low = w - high
         return jnp.concatenate([high, high, low, jnp.zeros((64, 8), F32)], axis=1).astype(BF16)
 
-    def inner_back(ref):
-        w = jnp.concatenate([ref[...], jnp.zeros((8, 64), F32)], axis=0)
-        return three_weights(w, 1)
-
     fi_t3 = inner_weights(fi3)
     si_t3 = inner_weights(si3)
-    fi_b3 = inner_back(fi_ref)
-    si_b3 = inner_back(si_ref)
     fo_t3 = three_weights(fo_ref[...].T, 1)
     so_t3 = three_weights(so_ref[...].T, 1)
-    fo_b3 = jnp.concatenate(split(fo_ref[...]), axis=0)
-    so_b3 = jnp.concatenate(split(so_ref[...]), axis=0)
     emb_pad[...] = jnp.zeros((128, 128), F32)
     emb_pad[0:89, :] = emb_ref[...]
     emb_t2 = jnp.concatenate(split(emb_pad[...].T), axis=1)
@@ -369,11 +363,16 @@
         at = t * 16
         return jnp.concatenate([ref[pl.ds(at, 8), :], ref[pl.ds(at + 8, 8), :]], axis=1)
 
-    def hidden_of(t, weights):
-        bes = tile_rows(bes_buf, t)
-        high = bes.astype(BF16).astype(F32)
-        stack = jnp.concatenate([high, bes - high, high, jnp.zeros((8, TILE), F32)], axis=0)
-        return silu_pair(dot(weights, stack.astype(BF16)))
+    def stacked(ref, t):
+        rows = tile_rows(ref, t)
+        high = rows.astype(BF16).astype(F32)
+        stack = jnp.concatenate([high, rows - high, high, jnp.zeros((8, TILE), F32)], axis=0)
+        return stack.astype(BF16)
+
+    def radial_of(t, inner, outer):
+        hidden, slope = silu_pair(dot(inner, stacked(bes_buf, t)))
+        rate = dot(inner, stacked(dbes_buf, t)) * slope
+        return dot(outer, three(hidden, 0)), dot(outer, three(rate, 0))
 
     def onehot(index_row, rows):
         hit = iota((rows, index_row.shape[1]), 0) == index_row.astype(I32)
@@ -388,21 +387,26 @@
         return jnp.where(t == 0, 0, last_row[before]) * 2
 
     acc[...] = jnp.zeros(acc.shape, F32)
+
+    def first_terms(t):
+        weights, rates = radial_of(t, fi_t3, fo_t3)
+        pair = tile_rows(pair_buf, t)
+        sender = sender_of(pair[4:5])
+        message = weights[0:128] * sender
+        rg = weights[128:256] * sender
+        return pair, message, rg, rates[0:128] * sender, rates[128:256] * sender
 
     def layer_one(step, carry):
         done = []
         for part in range(UNROLL):
             t = step * UNROLL + part
-            hidden, slope = hidden_of(t, fi_t3)
-            saved_slope[t] = slope
-            weights = dot(fo_t3, three(hidden, 0))
-            pair = tile_rows(pair_buf, t)
-            sender = sender_of(pair[4:5])
-            message = split(weights[0:128] * sender)
-            rg = weights[128:256] * sender
-            saved_rg[t] = rg
+            pair, message, rg, rate_0, rate_1 = first_terms(t)
+            kept = jnp.minimum(t, KEPT_TILES)
+            saved[kept, 0:128, :] = rg
+            saved[kept, 128:256, :] = rate_0
+            saved[kept, 256:384, :] = rate_1
             saved_pair_grad[t] = jnp.zeros((8, TILE), F32)
-            done.append((t, first_of(t) & -8, pair, message, split(rg)))
+            done.append((t, first_of(t) & -8, pair, split(message), split(rg)))
 
         def window(entry, w):
             _, base, pair, (m_high, m_low), (v_high, v_low) = entry
@@ -482,13 +486,14 @@
     w_acc[...] = jnp.zeros((128, 128), F32)
 
     def layer_two(t, carry):
-        hidden, _ = hidden_of(t, si_t3)
-        weights = dot(so_t3, three(hidden, 0))
+        weights, rates = radial_of(t, si_t3, so_t3)
         pair = tile_rows(pair_buf, t)
         hot = onehot(pair[5:6], 512)
         feat = dot(feat_t[0], hot) + dot(feat_t[1], hot)
-        saved_feat[t] = feat
         proj = pair[0:1] * feat[128:256] + pair[1:2] * feat[256:384] + pair[2:3] * feat[384:512]
+        saved_core[t, 0:384, :] = feat[128:512]
+        saved_core[t, 384:640, :] = weights
+        saved_core[t, 640:768, :] = rates[0:128] * feat[0:128] + rates[128:256] * proj
         high, low = split(weights[0:128] * feat[0:128] + weights[128:256] * proj)
         member = onehot(pair[6:7], 128)
         w_acc[...] += dot_t(high, member) + dot_t(low, member)
@@ -510,28 +515,15 @@
     feat_grad[...] = jnp.zeros((512, 512), F32)
     feat_grad[0:128, 0:128] = mixed_grad + rf_col
 
-    def radial_back(t, slope, grad, outer3, inner3):
-        high, low = split(grad)
-        both = dot(outer3, high)
-        hidden_grad = (both[0:64] + both[64:128] + dot(outer3[0:64], low)) * slope
-        bes_grad = dot(inner3, three(hidden_grad, 0))[0:8]
-        return jnp.sum(bes_grad * tile_rows(dbes_buf, t), axis=0, keepdims=True)
-
     def layer_two_back(t, carry):
-        hidden, slope = hidden_of(t, si_t3)
-        weights = dot(so_t3, three(hidden, 0))
         pair = tile_rows(pair_buf, t)
-        feat = saved_feat[t]
         member = onehot(pair[6:7], 128)
         w_grad = dot(w_grad2, jnp.concatenate([member, member], axis=0))
-        proj = pair[0:1] * feat[128:256] + pair[1:2] * feat[256:384] + pair[2:3] * feat[384:512]
-        radial_grad = jnp.concatenate([w_grad * feat[0:128], w_grad * proj], axis=0)
-        rho_grad = radial_back(t, slope, radial_grad, so_b3, si_b3)
-        proj_grad = w_grad * weights[128:256]
-        grads = [rho_grad]
-        sends = [w_grad * weights[0:128]]
+        proj_grad = w_grad * saved_core[t, 512:640, :]
+        grads = [jnp.sum(w_grad * saved_core[t, 640:768, :], axis=0, keepdims=True)]
+        sends = [w_grad * saved_core[t, 384:512, :]]
         for x in range(3):
-            part = feat[128 + x * 128 : 256 + x * 128]
+            part = saved_core[t, x * 128 : 128 + x * 128, :]
             grads.append(jnp.sum(proj_grad * part, axis=0, keepdims=True))
             sends.append(proj_grad * pair[x : x + 1])
         saved_pair_grad[t] = jnp.concatenate(grads + [jnp.zeros((4, TILE), F32)], axis=0)
@@ -558,7 +550,7 @@
 
     box_acc[...] = jnp.zeros((96, 128), F32)
 
-    def layer_one_back(step, carry):
+    def layer_one_back(step, carry, again):
         group = []
         for part in range(UNROLL):
             t = step * UNROLL + part
@@ -590,19 +582,19 @@
 
         spreads = []
         for part, t, pair, first in group:
-            sender = sender_of(pair[4:5])
-            rg = saved_rg[t]
-            v_grad = [expand[part, 128 + x * 128 : 256 + x * 128, :] for x in range(3)]
-            along = pair[0:1] * v_grad[0] + pair[1:2] * v_grad[1] + pair[2:3] * v_grad[2]
-            radial_grad = jnp.concatenate(
-                [expand[part, 0:128, :] * sender, along * sender], axis=0
-            )
+            if again:
+                _, _, rg, rate_0, rate_1 = first_terms(t)
+            else:
+                rg, rate_0, rate_1 = (saved[t, k * 128 : k * 128 + 128, :] for k in range(3))
             earlier = saved_pair_grad[t]
-            rho_grad = radial_back(t, saved_slope[t], radial_grad, fo_b3, fi_b3) + earlier[0:1]
-            unit_grad = [
-                jnp.sum(rg * v_grad[x], axis=0, keepdims=True) + earlier[1 + x : 2 + x]
-                for x in range(3)
-            ]
+            rho_grad = earlier[0:1] + jnp.sum(expand[part, 0:128, :] * rate_0, axis=0, keepdims=True)
+            unit_grad = []
+            for x in range(3):
+                v_grad = expand[part, 128 + x * 128 : 256 + x * 128, :]
+                along = jnp.sum(v_grad * rate_1, axis=0, keepdims=True)
+                rho_grad = rho_grad + pair[x : x + 1] * along
+                across = jnp.sum(v_grad * rg, axis=0, keepdims=True)
+                unit_grad.append(across + earlier[1 + x : 2 + x])
             unit = [pair[x : x + 1] for x in range(3)]
             inner = unit[0] * unit_grad[0] + unit[1] * unit_grad[1] + unit[2] * unit_grad[2]
             inv = pair[3:4]
@@ -615,12 +607,14 @@
             for code, sign in ((both >> 11, 1.0), (both & 2047, -1.0)):
                 row = jnp.broadcast_to(code >> 7, (16, TILE)) == iota((16, TILE), 0)
                 stack = [jnp.where(row, sign * value, 0.0) for value in values]
-                lane = jnp.where(iota((128, TILE), 0) == (code & 127), 1.0, 0.0).astype(BF16)
+                lane = onehot(code & 127, 128)
                 spreads.append(dot_t(jnp.concatenate(stack, axis=0).astype(BF16), lane))
         box_acc[...] += sum(spreads[1:], spreads[0])
         return carry
 
-    lax.fori_loop(0, steps, layer_one_back, 0)
+    kept_steps = jnp.minimum(steps, KEPT_TILES // UNROLL)
+    lax.fori_loop(0, kept_steps, functools.partial(layer_one_back, again=False), 0)
+    lax.fori_loop(kept_steps, steps, functools.partial(layer_one_back, again=True), 0)
 
     for comp in range(3):
         grid = box_acc[comp * 32 : comp * 32 + 16, :] + box_acc[comp * 32 + 16 : comp * 32 + 32, :]
@@ -659,9 +653,8 @@
         vm((128, 128), F32),
         vm((4, 512, 256), BF16),
         vm((UNROLL, 512, TILE), F32),
-        vm((MAX_TILES, 128, TILE), F32),
-        vm((MAX_TILES, 64, TILE), F32),
-        vm((MAX_CORE_TILES, 512, TILE), F32),
+        vm((KEPT_TILES + 1, 384, TILE), F32),
+        vm((MAX_CORE_TILES, 768, TILE), F32),
         vm((MAX_TILES, 8, TILE), F32),
         vm((96, 128), F32),
         vm((128, 128), F32),

time: 94.8 us -> 92.2 us (0.973)
  the two profiles are of different devices: /device:TPU:13 before, /device:TPU:31 now
where the time goes in v3:
time: 92.2 us; the launch traced here: 91.6 us
  starting transfers between devices  36.3 us (39%)
  Pallas kernels  32.3 us (35%)
  waiting for transfers between devices  19.5 us (21%)
  other arithmetic  2.03 us (2%)
    pallas_call x1, Pallas kernels, pair_program(): pl.pallas_call(main_kernel, out_shape=(jax.ShapeDtypeStruct((1, 64), F32)...  30.8 us
    ppermute x1, starting transfers between devices, shards(): high = lax.ppermute(layer, 'gz', ring('gz', -1))  8.93 us
    ppermute x1, starting transfers between devices, shards(): below = lax.ppermute(both, 'gy', ring('gy', 1))  6.31 us
    ppermute x1, starting transfers between devices, shards(): total = folded[1] + lax.ppermute(folded[2], 'gy', ring('gy', 1))  5.96 us
    ppermute x1, waiting for transfers between devices, shards(): above = lax.ppermute(both, 'gy', ring('gy', -1))  5.43 us
    ppermute x1, waiting for transfers between devices, shards(): total = total + lax.ppermute(folded[0], 'gy', ring('gy', -1))  5.1 us
    ppermute x1, starting transfers between devices, shards(): lax.ppermute(down, 'gz', ring('gz', -1))  4.57 us
    ppermute x1, waiting for transfers between devices, shards(): low = lax.ppermute(layer, 'gz', ring('gz', 1))  4.53 us
  transfers between devices with their start and end apart: 9, of which 5 were waited for; matrix products, arithmetic and copies ran while one was open for 0% of the time, Pallas kernels for 0%

profile of v3, /device:TPU:31, one launch (start us, length us, event | category | flops | bytes accessed | tf_op | source)
XLA Modules:
  0.0 91.6 jit_solution(18415092200884637213)
XLA Ops:
  0.6 1.5 %shard_map.158 = f32[5,8,128]{2,1,0:T(8,128)} custom-call(f32[3,64]{1,0:T(4,128)} %pos_ref.1, s32[1,64]{1,0:T(1,128)} %bitcast.15, s32[1,64]{1,0:T(1,128)} %bitcast.16, s32[64,64]{1,0:T(8,128)} %neighbors_ref.1), custom_call_target="tpu_custom_call" | custom-call | tf_op jit(solution)/shard_map/pallas_call | solution.py:677
  2.1 2.9 %collective-permute-start = (f32[5,8,128]{2,1,0:T(8,128)}, f32[5,8,128]{2,1,0:T(8,128)S(1)}, u32[]{:S(2)}, u32[]{:S(2)}) collective-permute-start(f32[5,8,128]{2,1,0:T(8,128)} %shard_map.158), channel_id=1, source_target_pairs={{0,256},{256,0},{1,257},{257,1},{2,258},{258,2},{3,259},{259,3},{4... | collective-permute-start | bytes 61448 | tf_op jit(solution)/shard_map/ppermute | solution.py:715
  5.0 3.4 %collective-permute-done = f32[5,8,128]{2,1,0:T(8,128)S(1)} collective-permute-done((f32[5,8,128]{2,1,0:T(8,128)}, f32[5,8,128]{2,1,0:T(8,128)S(1)}, u32[]{:S(2)}, u32[]{:S(2)}) %collective-permute-start) | collective-permute-done | bytes 20512 | tf_op jit(solution)/shard_map/ppermute | solution.py:715
  8.4 0.7 pad_maximum_fusion
  9.1 0.0 copy-start
  9.1 6.3 %collective-permute-start.1 = (f32[10,8,128]{2,1,0:T(8,128)S(1)}, f32[10,8,128]{2,1,0:T(8,128)S(1)}, u32[]{:S(2)}, u32[]{:S(2)}) collective-permute-start(f32[10,8,128]{2,1,0:T(8,128)S(1)} %pad_maximum_fusion), channel_id=1, source_target_pairs={{0,16},{16,32},{32,48},{48,64},{64,80},{80,96},{96,112},{112,128},... | collective-permute-start | bytes 122888 | tf_op jit(solution)/shard_map/ppermute | solution.py:717
  15.4 1.9 %collective-permute-start.2 = (f32[10,8,128]{2,1,0:T(8,128)S(1)}, f32[10,8,128]{2,1,0:T(8,128)S(1)}, u32[]{:S(2)}, u32[]{:S(2)}) collective-permute-start(f32[10,8,128]{2,1,0:T(8,128)S(1)} %pad_maximum_fusion), channel_id=1, source_target_pairs={{0,240},{16,0},{32,16},{48,32},{64,48},{80,64},{96,80},{112,96},{1... | collective-permute-start | bytes 122888 | tf_op jit(solution)/shard_map/ppermute | solution.py:718
  17.3 0.0 collective-permute-done.1
  17.4 0.0 copy-done
  17.4 5.4 %collective-permute-done.2 = f32[10,8,128]{2,1,0:T(8,128)S(1)} collective-permute-done((f32[10,8,128]{2,1,0:T(8,128)S(1)}, f32[10,8,128]{2,1,0:T(8,128)S(1)}, u32[]{:S(2)}, u32[]{:S(2)}) %collective-permute-start.2) | collective-permute-done | bytes 40992 | tf_op jit(solution)/shard_map/ppermute | solution.py:718
  22.8 0.0 copy-start.1
  22.8 8.9 %collective-permute-start.4 = (f32[22,8,128]{2,1,0:T(8,128)S(1)}, f32[22,8,128]{2,1,0:T(8,128)S(1)}, u32[]{:S(2)}, u32[]{:S(2)}) collective-permute-start(f32[22,8,128]{2,1,0:T(8,128)S(1)} %constant_dynamic-update-slice_fusion.own_ref), channel_id=1, source_target_pairs={{0,15},{1,0},{2,1},{3,2},{4,3},{5,4},{6,5},{7,6},{8,7},{9,8},{10,9... | collective-permute-start | bytes 270344 | tf_op jit(solution)/shard_map/ppermute | solution.py:721
  31.8 1.9 %collective-permute-start.3 = (f32[22,8,128]{2,1,0:T(8,128)S(1)}, f32[22,8,128]{2,1,0:T(8,128)S(1)}, u32[]{:S(2)}, u32[]{:S(2)}) collective-permute-start(f32[22,8,128]{2,1,0:T(8,128)S(1)} %constant_dynamic-update-slice_fusion.own_ref), channel_id=1, source_target_pairs={{0,1},{1,2},{2,3},{3,4},{4,5},{5,6},{6,7},{7,8},{8,9},{9,10},{10,1... | collective-permute-start | bytes 270344 | tf_op jit(solution)/shard_map/ppermute | solution.py:720
  33.7 0.0 collective-permute-done.4.high_ref
  33.7 0.0 copy-start.2
  33.7 4.5 %collective-permute-done.3.low_ref = f32[22,8,128]{2,1,0:T(8,128)S(1)} collective-permute-done((f32[22,8,128]{2,1,0:T(8,128)S(1)}, f32[22,8,128]{2,1,0:T(8,128)S(1)}, u32[]{:S(2)}, u32[]{:S(2)}) %collective-permute-start.3) | collective-permute-done | bytes 90144 | tf_op jit(solution)/shard_map/ppermute | solution.py:720
  38.3 0.0 copy-start.3
  38.3 0.0 copy-done.1
  38.3 0.0 copy-done.2
  38.3 0.6 copy-done.3
  38.9 30.8 %shard_map.159 = (f32[1,64]{1,0:T(1,128)}, f32[3,8,128]{2,1,0:T(8,128)}, f32[3,8,128]{2,1,0:T(8,128)}, f32[3,8,128]{2,1,0:T(8,128)}) custom-call(f32[22,8,128]{2,1,0:T(8,128)} %copy-done.1, f32[22,8,128]{2,1,0:T(8,128)} %copy-done.3, f32[22,8,128]{2,1,0:T(8,128)} %copy-done.2, f32[89,128]{1,0:T(8,128)} %emb_ref.1, f32[8,64]{1,0:T(8,128)} %fi_ref.1, ...), custom_call_target="tpu_custom_call" | custom-call | tf_op jit(solution)/shard_map/pallas_call | solution.py:664
  69.8 1.9 %collective-permute-start.5 = (f32[3,8,128]{2,1,0:T(8,128)}, f32[3,8,128]{2,1,0:T(8,128)S(1)}, u32[]{:S(2)}, u32[]{:S(2)}) collective-permute-start(f32[3,8,128]{2,1,0:T(8,128)} %get-tuple-element.8), channel_id=1, source_target_pairs={{0,1},{1,2},{2,3},{3,4},{4,5},{5,6},{6,7},{7,8},{8,9},{9,10},{10,1... | collective-permute-start | bytes 36872 | tf_op jit(solution)/shard_map/ppermute | solution.py:736
  71.7 4.6 %collective-permute-start.6 = (f32[3,8,128]{2,1,0:T(8,128)}, f32[3,8,128]{2,1,0:T(8,128)S(1)}, u32[]{:S(2)}, u32[]{:S(2)}) collective-permute-start(f32[3,8,128]{2,1,0:T(8,128)} %get-tuple-element.9), channel_id=1, source_target_pairs={{0,15},{1,0},{2,1},{3,2},{4,3},{5,4},{6,5},{7,6},{8,7},{9,8},{10,9... | collective-permute-start | bytes 36872 | tf_op jit(solution)/shard_map/ppermute | solution.py:736
  76.3 0.0 collective-permute-done.5
  76.3 1.0 %collective-permute-done.6 = f32[3,8,128]{2,1,0:T(8,128)S(1)} collective-permute-done((f32[3,8,128]{2,1,0:T(8,128)}, f32[3,8,128]{2,1,0:T(8,128)S(1)}, u32[]{:S(2)}, u32[]{:S(2)}) %collective-permute-start.6) | collective-permute-done | bytes 12320 | tf_op jit(solution)/shard_map/ppermute | solution.py:736
  77.3 0.7 add_add_fusion
  78.0 6.0 %collective-permute-start.7 = (f32[8,128]{1,0:T(8,128)S(1)}, f32[8,128]{1,0:T(8,128)S(1)}, u32[]{:S(2)}, u32[]{:S(2)}) collective-permute-start(f32[8,128]{1,0:T(8,128)S(1)} %get-tuple-element.10), channel_id=1, source_target_pairs={{0,16},{16,32},{32,48},{48,64},{64,80},{80,96},{96,112},{112,128},... | collective-permute-start | bytes 12296 | tf_op jit(solution)/shard_map/ppermute | solution.py:737
  84.0 1.9 %collective-permute-start.8 = (f32[8,128]{1,0:T(8,128)S(1)}, f32[8,128]{1,0:T(8,128)S(1)}, u32[]{:S(2)}, u32[]{:S(2)}) collective-permute-start(f32[8,128]{1,0:T(8,128)S(1)} %get-tuple-element.11), channel_id=1, source_target_pairs={{0,240},{16,0},{32,16},{48,32},{64,48},{80,64},{96,80},{112,96},{1... | collective-permute-start | bytes 12296 | tf_op jit(solution)/shard_map/ppermute | solution.py:738
  85.9 0.0 collective-permute-done.7
  85.9 5.1 %collective-permute-done.8 = f32[8,128]{1,0:T(8,128)S(1)} collective-permute-done((f32[8,128]{1,0:T(8,128)S(1)}, f32[8,128]{1,0:T(8,128)S(1)}, u32[]{:S(2)}, u32[]{:S(2)}) %collective-permute-start.8) | collective-permute-done | bytes 4128 | tf_op jit(solution)/shard_map/ppermute | solution.py:738
  91.0 0.6 slice_negate_fusion
  (9 shorter events, 0.0 us)
Async XLA Ops:
  2.1 6.2 %collective-permute-start = (f32[5,8,128]{2,1,0:T(8,128)}, f32[5,8,128]{2,1,0:T(8,128)S(1)}, u32[]{:S(2)}, u32[]{:S(2)}) collective-permute-start(f32[5,8,128]{2,1,0:T(8,128)} %shard_map.158), channel_id=1, source_target_pairs={{0,256},{256,0},{1,257},{257,1},{2,258},{258,2},{3,259},{259,3},{4... | collective-permute-start | bytes 61448 | tf_op jit(solution)/shard_map/ppermute | solution.py:715
  9.1 8.3 %copy-start = (f32[5,8,128]{2,1,0:T(8,128)S(1)}, f32[5,8,128]{2,1,0:T(8,128)}, u32[]{:S(2)}) copy-start(f32[5,8,128]{2,1,0:T(8,128)} %shard_map.158) | copy-start | bytes 61444
  9.1 8.2 %collective-permute-start.1 = (f32[10,8,128]{2,1,0:T(8,128)S(1)}, f32[10,8,128]{2,1,0:T(8,128)S(1)}, u32[]{:S(2)}, u32[]{:S(2)}) collective-permute-start(f32[10,8,128]{2,1,0:T(8,128)S(1)} %pad_maximum_fusion), channel_id=1, source_target_pairs={{0,16},{16,32},{32,48},{48,64},{64,80},{80,96},{96,112},{112,128},... | collective-permute-start | bytes 122888 | tf_op jit(solution)/shard_map/ppermute | solution.py:717
  15.4 7.4 %collective-permute-start.2 = (f32[10,8,128]{2,1,0:T(8,128)S(1)}, f32[10,8,128]{2,1,0:T(8,128)S(1)}, u32[]{:S(2)}, u32[]{:S(2)}) collective-permute-start(f32[10,8,128]{2,1,0:T(8,128)S(1)} %pad_maximum_fusion), channel_id=1, source_target_pairs={{0,240},{16,0},{32,16},{48,32},{64,48},{80,64},{96,80},{112,96},{1... | collective-permute-start | bytes 122888 | tf_op jit(solution)/shard_map/ppermute | solution.py:718
  22.8 15.4 %copy-start.1 = (f32[22,8,128]{2,1,0:T(8,128)}, f32[22,8,128]{2,1,0:T(8,128)S(1)}, u32[]{:S(2)}) copy-start(f32[22,8,128]{2,1,0:T(8,128)S(1)} %constant_dynamic-update-slice_fusion.own_ref) | copy-start | bytes 270340
  22.8 10.9 %collective-permute-start.4 = (f32[22,8,128]{2,1,0:T(8,128)S(1)}, f32[22,8,128]{2,1,0:T(8,128)S(1)}, u32[]{:S(2)}, u32[]{:S(2)}) collective-permute-start(f32[22,8,128]{2,1,0:T(8,128)S(1)} %constant_dynamic-update-slice_fusion.own_ref), channel_id=1, source_target_pairs={{0,15},{1,0},{2,1},{3,2},{4,3},{5,4},{6,5},{7,6},{8,7},{9,8},{10,9... | collective-permute-start | bytes 270344 | tf_op jit(solution)/shard_map/ppermute | solution.py:721
  31.8 6.5 %collective-permute-start.3 = (f32[22,8,128]{2,1,0:T(8,128)S(1)}, f32[22,8,128]{2,1,0:T(8,128)S(1)}, u32[]{:S(2)}, u32[]{:S(2)}) collective-permute-start(f32[22,8,128]{2,1,0:T(8,128)S(1)} %constant_dynamic-update-slice_fusion.own_ref), channel_id=1, source_target_pairs={{0,1},{1,2},{2,3},{3,4},{4,5},{5,6},{6,7},{7,8},{8,9},{9,10},{10,1... | collective-permute-start | bytes 270344 | tf_op jit(solution)/shard_map/ppermute | solution.py:720
  33.7 4.6 %copy-start.2 = (f32[22,8,128]{2,1,0:T(8,128)}, f32[22,8,128]{2,1,0:T(8,128)S(1)}, u32[]{:S(2)}) copy-start(f32[22,8,128]{2,1,0:T(8,128)S(1)} %collective-permute-done.4.high_ref) | copy-start | bytes 270340
  38.3 0.6 copy-start.3
  69.8 6.5 %collective-permute-start.5 = (f32[3,8,128]{2,1,0:T(8,128)}, f32[3,8,128]{2,1,0:T(8,128)S(1)}, u32[]{:S(2)}, u32[]{:S(2)}) collective-permute-start(f32[3,8,128]{2,1,0:T(8,128)} %get-tuple-element.8), channel_id=1, source_target_pairs={{0,1},{1,2},{2,3},{3,4},{4,5},{5,6},{6,7},{7,8},{8,9},{9,10},{10,1... | collective-permute-start | bytes 36872 | tf_op jit(solution)/shard_map/ppermute | solution.py:736
  71.7 5.6 %collective-permute-start.6 = (f32[3,8,128]{2,1,0:T(8,128)}, f32[3,8,128]{2,1,0:T(8,128)S(1)}, u32[]{:S(2)}, u32[]{:S(2)}) collective-permute-start(f32[3,8,128]{2,1,0:T(8,128)} %get-tuple-element.9), channel_id=1, source_target_pairs={{0,15},{1,0},{2,1},{3,2},{4,3},{5,4},{6,5},{7,6},{8,7},{9,8},{10,9... | collective-permute-start | bytes 36872 | tf_op jit(solution)/shard_map/ppermute | solution.py:736
  78.0 7.9 %collective-permute-start.7 = (f32[8,128]{1,0:T(8,128)S(1)}, f32[8,128]{1,0:T(8,128)S(1)}, u32[]{:S(2)}, u32[]{:S(2)}) collective-permute-start(f32[8,128]{1,0:T(8,128)S(1)} %get-tuple-element.10), channel_id=1, source_target_pairs={{0,16},{16,32},{32,48},{48,64},{64,80},{80,96},{96,112},{112,128},... | collective-permute-start | bytes 12296 | tf_op jit(solution)/shard_map/ppermute | solution.py:737
  84.0 7.0 %collective-permute-start.8 = (f32[8,128]{1,0:T(8,128)S(1)}, f32[8,128]{1,0:T(8,128)S(1)}, u32[]{:S(2)}, u32[]{:S(2)}) collective-permute-start(f32[8,128]{1,0:T(8,128)S(1)} %get-tuple-element.11), channel_id=1, source_target_pairs={{0,240},{16,0},{32,16},{48,32},{64,48},{80,64},{96,80},{112,96},{1... | collective-permute-start | bytes 12296 | tf_op jit(solution)/shard_map/ppermute | solution.py:738

commit v4 on v3

--- a/solution.py
+++ b/solution.py
@@ -11,11 +11,12 @@
 BF16 = jnp.bfloat16
 I32 = jnp.int32
 TILE = 256
-MAX_TILES = 129
-MAX_CORE_TILES = 32
+MAX_TILES = 132
 WINDOW = 64
 UNROLL = 3
+SCATTER = 6
 KEPT_TILES = 30
+KEPT_CORE_TILES = 8
 INTERPRET = False
 
 COLUMNS = [
@@ -261,6 +262,7 @@
     tiles = (total + (TILE - 1)) // TILE
     core_tiles = (core_total + (TILE - 1)) // TILE
     steps = (tiles + UNROLL - 1) // UNROLL
+    scatters = (tiles + SCATTER - 1) // SCATTER
 
     def basis(chunk, carry):
         at = chunk * 64
@@ -340,7 +342,7 @@
             pair_buf[pl.ds(at + k, 8, stride=8), :] = value
         return carry
 
-    lax.fori_loop(0, (steps * UNROLL * TILE + 1023) // 1024, basis, 0)
+    lax.fori_loop(0, (scatters * SCATTER * TILE + 1023) // 1024, basis, 0)
 
     fi3 = jnp.concatenate([fi_ref[...], jnp.zeros((24, 64), F32)], axis=0)
     si3 = jnp.concatenate([si_ref[...], jnp.zeros((24, 64), F32)], axis=0)
@@ -406,17 +408,20 @@
             saved[kept, 128:256, :] = rate_0
             saved[kept, 256:384, :] = rate_1
             saved_pair_grad[t] = jnp.zeros((8, TILE), F32)
-            done.append((t, first_of(t) & -8, pair, split(message), split(rg)))
+            both = jnp.concatenate(split(message), axis=0), jnp.concatenate(split(rg), axis=0)
+            done.append((t, first_of(t) & -8, pair, both))
 
         def window(entry, w):
-            _, base, pair, (m_high, m_low), (v_high, v_low) = entry
+            _, base, pair, (m_parts, v_parts) = entry
             at = base + w * WINDOW
             unit = [split(pair[k : k + 1]) for k in range(3)]
             hot = onehot(pair[6:7] - at.astype(F32), WINDOW)
             u_high = jnp.concatenate([hot * high for high, _ in unit], axis=0)
             u_low = jnp.concatenate([hot * low for _, low in unit], axis=0)
-            m = dot_t(hot, m_high) + dot_t(hot, m_low)
-            v = dot_t(u_high, v_high) + dot_t(u_high, v_low) + dot_t(u_low, v_high)
+            m = dot_t(hot, m_parts)
+            v = dot_t(u_high, v_parts)
+            m = m[:, 0:128] + m[:, 128:256]
+            v = v[:, 0:128] + v[:, 128:256] + dot_t(u_low, v_parts[0:128])
             return pl.ds(pl.multiple_of(at, 8), WINDOW), m, v
 
         def add(rows, m, v):
@@ -428,7 +433,7 @@
             add(*sums)
         counts = [
             jnp.where(t < tiles, (last_row[t] * 2 + 1 - base) // WINDOW + 1, 1)
-            for t, base, _, _, _ in done
+            for t, base, _, _ in done
         ]
         most = counts[0]
         for count in counts[1:]:
@@ -485,16 +490,24 @@
 
     w_acc[...] = jnp.zeros((128, 128), F32)
 
-    def layer_two(t, carry):
+    def second_terms(t):
         weights, rates = radial_of(t, si_t3, so_t3)
         pair = tile_rows(pair_buf, t)
         hot = onehot(pair[5:6], 512)
-        feat = dot(feat_t[0], hot) + dot(feat_t[1], hot)
+        feat = dot(feat_t[...].reshape(1024, 512), hot)
+        feat = feat[0:512] + feat[512:1024]
         proj = pair[0:1] * feat[128:256] + pair[1:2] * feat[256:384] + pair[2:3] * feat[384:512]
-        saved_core[t, 0:384, :] = feat[128:512]
-        saved_core[t, 384:640, :] = weights
-        saved_core[t, 640:768, :] = rates[0:128] * feat[0:128] + rates[128:256] * proj
-        high, low = split(weights[0:128] * feat[0:128] + weights[128:256] * proj)
+        rate = rates[0:128] * feat[0:128] + rates[128:256] * proj
+        message = weights[0:128] * feat[0:128] + weights[128:256] * proj
+        return pair, message, feat[128:512], weights, rate
+
+    def layer_two(t, carry):
+        pair, message, vectors, weights, rate = second_terms(t)
+        kept = jnp.minimum(t, KEPT_CORE_TILES)
+        saved_core[kept, 0:384, :] = vectors
+        saved_core[kept, 384:640, :] = weights
+        saved_core[kept, 640:768, :] = rate
+        high, low = split(message)
         member = onehot(pair[6:7], 128)
         w_acc[...] += dot_t(high, member) + dot_t(low, member)
         return carry
@@ -515,15 +528,20 @@
     feat_grad[...] = jnp.zeros((512, 512), F32)
     feat_grad[0:128, 0:128] = mixed_grad + rf_col
 
-    def layer_two_back(t, carry):
+    def layer_two_back(t, carry, again):
         pair = tile_rows(pair_buf, t)
         member = onehot(pair[6:7], 128)
         w_grad = dot(w_grad2, jnp.concatenate([member, member], axis=0))
-        proj_grad = w_grad * saved_core[t, 512:640, :]
-        grads = [jnp.sum(w_grad * saved_core[t, 640:768, :], axis=0, keepdims=True)]
-        sends = [w_grad * saved_core[t, 384:512, :]]
+        if again:
+            _, _, vectors, weights, rate = second_terms(t)
+        else:
+            vectors, weights = saved_core[t, 0:384, :], saved_core[t, 384:640, :]
+            rate = saved_core[t, 640:768, :]
+        proj_grad = w_grad * weights[128:256]
+        grads = [jnp.sum(w_grad * rate, axis=0, keepdims=True)]
+        sends = [w_grad * weights[0:128]]
         for x in range(3):
-            part = saved_core[t, x * 128 : 128 + x * 128, :]
+            part = vectors[x * 128 : 128 + x * 128]
             grads.append(jnp.sum(proj_grad * part, axis=0, keepdims=True))
             sends.append(proj_grad * pair[x : x + 1])
         saved_pair_grad[t] = jnp.concatenate(grads + [jnp.zeros((4, TILE), F32)], axis=0)
@@ -532,7 +550,9 @@
         feat_grad[...] += dot_t(high, hot) + dot_t(low, hot)
         return carry
 
-    lax.fori_loop(0, core_tiles, layer_two_back, 0)
+    kept_core = jnp.minimum(core_tiles, KEPT_CORE_TILES)
+    lax.fori_loop(0, kept_core, functools.partial(layer_two_back, again=False), 0)
+    lax.fori_loop(kept_core, core_tiles, functools.partial(layer_two_back, again=True), 0)
 
     pre_grad3 = three(feat_grad[0:128, :] * slope_t[...], 0)
     m_grad = dot(three_weights(fs_ref[...], 1), pre_grad3)
@@ -543,54 +563,45 @@
         part = feat_grad[128 + x * 128 : 256 + x * 128, :] + 2.0 * vec_t[x] * square_grad
         message_grads.append(dot(fv_b3, three(part, 0)))
     for kind in range(4):
-        high, low = split(message_grads[kind] * 0.25)
-        for w in range(4):
-            grad_lhs[w, kind * 128 : (kind + 1) * 128, 0:128] = high[:, w * 128 : (w + 1) * 128]
-            grad_lhs[w, kind * 128 : (kind + 1) * 128, 128:256] = low[:, w * 128 : (w + 1) * 128]
+        wide = jnp.concatenate([message_grads[kind] * 0.25, jnp.zeros((128, 128), F32)], axis=1)
+        for odd, part in enumerate((wide, pltpu.roll(wide, 576, 1))):
+            high, low = split(part)
+            for w in range(4):
+                rows = pl.ds(kind * 128, 128)
+                grad_lhs[2 * w + odd, rows, 0:128] = high[:, w * 128 : (w + 1) * 128]
+                grad_lhs[2 * w + odd, rows, 128:256] = low[:, w * 128 : (w + 1) * 128]
 
     box_acc[...] = jnp.zeros((96, 128), F32)
 
-    def layer_one_back(step, carry, again):
-        group = []
+    def expanded(pair, w):
+        member = onehot(pair[6:7] - (w * 64).astype(F32), 128)
+        return dot(grad_lhs[w], jnp.concatenate([member, member], axis=0))
+
+    def back_tiles(step, again, many):
         for part in range(UNROLL):
             t = step * UNROLL + part
-            group.append((part, t, tile_rows(pair_buf, t), first_of(t) >> 7))
-
-        def expanded(pair, w):
-            member = onehot(pair[6:7] - (w * 128).astype(F32), 128)
-            return dot(grad_lhs[w], jnp.concatenate([member, member], axis=0))
-
-        for part, t, pair, first in group:
-            expand[part] = expanded(pair, first)
-        lasts = [
-            jnp.where(t < tiles, (last_row[t] * 2 + 1) >> 7, 0)
-            for _, t, _, _ in group
-        ]
-        crossing = lasts[0] > group[0][3]
-        for last, entry in zip(lasts[1:], group[1:]):
-            crossing = crossing | (last > entry[3])
-
-        @pl.when(crossing)
-        def _():
-            for last, (part, t, pair, first) in zip(lasts, group):
-
-                def more(w, carry, part=part, pair=pair):
-                    expand[part] += expanded(pair, w)
+            pair = tile_rows(pair_buf, t)
+            first = first_of(t) >> 6
+            moved = expanded(pair, first)
+            if many:
+                expand[...] = moved
+                last = jnp.where(t < tiles, (last_row[t] * 2 + 1) >> 6, 0)
+
+                def more(w, carry, pair=pair, first=first):
+                    expand[...] += expanded(pair, first + 2 * w)
                     return carry
 
-                lax.fori_loop(first + 1, last + 1, more, 0)
-
-        spreads = []
-        for part, t, pair, first in group:
+                lax.fori_loop(1, ((last - first) >> 1) + 1, more, 0)
+                moved = expand[...]
             if again:
                 _, _, rg, rate_0, rate_1 = first_terms(t)
             else:
                 rg, rate_0, rate_1 = (saved[t, k * 128 : k * 128 + 128, :] for k in range(3))
             earlier = saved_pair_grad[t]
-            rho_grad = earlier[0:1] + jnp.sum(expand[part, 0:128, :] * rate_0, axis=0, keepdims=True)
+            rho_grad = earlier[0:1] + jnp.sum(moved[0:128] * rate_0, axis=0, keepdims=True)
             unit_grad = []
             for x in range(3):
-                v_grad = expand[part, 128 + x * 128 : 256 + x * 128, :]
+                v_grad = moved[128 + x * 128 : 256 + x * 128]
                 along = jnp.sum(v_grad * rate_1, axis=0, keepdims=True)
                 rho_grad = rho_grad + pair[x : x + 1] * along
                 across = jnp.sum(v_grad * rg, axis=0, keepdims=True)
@@ -600,21 +611,58 @@
             inv = pair[3:4]
             values = []
             for x in range(3):
-                value = (unit_grad[x] - unit[x] * inner) * inv + rho_grad * unit[x]
+                values.append((unit_grad[x] - unit[x] * inner) * inv + rho_grad * unit[x])
+            for x in range(3):
+                saved_pair_grad[t, x : x + 1, :] = values[x]
+
+    def layer_one_back(step, carry):
+        crossing = False
+        for part in range(UNROLL):
+            t = step * UNROLL + part
+            last = jnp.where(t < tiles, (last_row[t] * 2 + 1) >> 6, 0)
+            crossing = crossing | (last > (first_of(t) >> 6) + 1)
+
+        @pl.when(crossing)
+        def _():
+            back_tiles(step, False, True)
+
+        @pl.when(jnp.logical_not(crossing))
+        def _():
+            back_tiles(step, False, False)
+
+        return carry
+
+    def layer_one_again(step, carry):
+        back_tiles(step, True, True)
+        return carry
+
+    kept_steps = jnp.minimum(steps, KEPT_TILES // UNROLL)
+    lax.fori_loop(0, kept_steps, layer_one_back, 0)
+    lax.fori_loop(kept_steps, steps, layer_one_again, 0)
+
+    def scatter(group, carry):
+        total_grad = None
+        for part in range(SCATTER):
+            t = group * SCATTER + part
+            pair = tile_rows(pair_buf, t)
+            values = []
+            for x in range(3):
+                value = jnp.where(pair[6:7] >= 0.0, saved_pair_grad[t, x : x + 1, :], 0.0)
                 high = value.astype(BF16).astype(F32)
                 values += [high, value - high]
             both = pair[7:8].astype(I32)
+            rows, lanes = [], []
             for code, sign in ((both >> 11, 1.0), (both & 2047, -1.0)):
                 row = jnp.broadcast_to(code >> 7, (16, TILE)) == iota((16, TILE), 0)
                 stack = [jnp.where(row, sign * value, 0.0) for value in values]
-                lane = onehot(code & 127, 128)
-                spreads.append(dot_t(jnp.concatenate(stack, axis=0).astype(BF16), lane))
-        box_acc[...] += sum(spreads[1:], spreads[0])
-        return carry
-
-    kept_steps = jnp.minimum(steps, KEPT_TILES // UNROLL)
-    lax.fori_loop(0, kept_steps, functools.partial(layer_one_back, again=False), 0)
-    lax.fori_loop(kept_steps, steps, functools.partial(layer_one_back, again=True), 0)
+                rows.append(jnp.concatenate(stack, axis=0).astype(BF16))
+                lanes.append(onehot(code & 127, 128))
+            moved = dot_t(jnp.concatenate(rows, axis=1), jnp.concatenate(lanes, axis=1))
+            total_grad = moved if total_grad is None else total_grad + moved
+        box_acc[...] += total_grad
+        return carry
+
+    lax.fori_loop(0, scatters, scatter, 0)
 
     for comp in range(3):
         grid = box_acc[comp * 32 : comp * 32 + 16, :] + box_acc[comp * 32 + 16 : comp * 32 + 32, :]
@@ -651,10 +699,10 @@
         vm((2, 512, 512), BF16),
         vm((512, 512), F32),
         vm((128, 128), F32),
-        vm((4, 512, 256), BF16),
-        vm((UNROLL, 512, TILE), F32),
+        vm((8, 512, 256), BF16),
+        vm((512, TILE), F32),
         vm((KEPT_TILES + 1, 384, TILE), F32),
-        vm((MAX_CORE_TILES, 768, TILE), F32),
+        vm((KEPT_CORE_TILES + 1, 768, TILE), F32),
         vm((MAX_TILES, 8, TILE), F32),
         vm((96, 128), F32),
         vm((128, 128), F32),
@@ -667,7 +715,7 @@
         in_specs=[whole] * (3 + len(weights)),
         out_specs=(whole,) * 4,
         scratch_shapes=scratch,
-        compiler_params=pltpu.CompilerParams(vmem_limit_bytes=60 * 1024 * 1024),
+        compiler_params=pltpu.CompilerParams(vmem_limit_bytes=42 * 1024 * 1024),
         interpret=INTERPRET,
     )(own, low, high, *weights)
 

time: 92.2 us -> 88.1 us (0.956)
  starting transfers between devices: 36.3 us -> 33.1 us
  local copies, waits for them, and re-layouts: 0.67 us -> 3.11 us
  Pallas kernels: 32.3 us -> 30.3 us
  waiting for transfers between devices: 19.5 us -> 18.5 us
    ppermute x1, starting transfers between devices: 5.96 us -> 2.93 us  [shards(): total = folded[1] + lax.ppermute(folded[2], 'gy', ring('gy', 1))]
    unnamed x14 -> x28, local copies, waits for them, and re-layouts: 0.67 us -> 3.1 us
    pallas_call x1, Pallas kernels: 30.8 us -> 28.8 us  [pair_program(): pl.pallas_call(main_kernel, out_shape=(jax.ShapeDtypeStruct((1, 64), F32)...]
  transfers between devices with their start and end apart: 9 -> 9, of which waited for: 5 -> 5; matrix products, arithmetic and copies ran while one was open for 0% -> 1% of each run, Pallas kernels for 0% -> 0%
where the time goes in v4:
time: 88.1 us; the launch traced here: 87.2 us
  starting transfers between devices  33.1 us (38%)
  Pallas kernels  30.3 us (34%)
  waiting for transfers between devices  18.5 us (21%)
  local copies, waits for them, and re-layouts  3.11 us (4%)
  other arithmetic  1.36 us (2%)
    pallas_call x1, Pallas kernels, pair_program(): pl.pallas_call(main_kernel, out_shape=(jax.ShapeDtypeStruct((1, 64), F32)...  28.8 us
    ppermute x1, starting transfers between devices, shards(): high = lax.ppermute(layer, 'gz', ring('gz', -1))  8.92 us
    ppermute x1, starting transfers between devices, shards(): below = lax.ppermute(both, 'gy', ring('gy', 1))  6.18 us
    ppermute x1, waiting for transfers between devices, shards(): total = total + lax.ppermute(folded[0], 'gy', ring('gy', -1))  5.1 us
    ppermute x1, waiting for transfers between devices, shards(): above = lax.ppermute(both, 'gy', ring('gy', -1))  4.68 us
    ppermute x1, starting transfers between devices, shards(): lax.ppermute(down, 'gz', ring('gz', -1))  4.57 us
    ppermute x1, waiting for transfers between devices, shards(): low = lax.ppermute(layer, 'gz', ring('gz', 1))  4.54 us
    ppermute x1, waiting for transfers between devices, shards(): partner = lax.ppermute(packed, 'gx', ring('gx', 1))  3.37 us
  transfers between devices with their start and end apart: 9, of which 5 were waited for; matrix products, arithmetic and copies ran while one was open for 1% of the time, Pallas kernels for 0%

profile of v4, /device:TPU:31, one launch (start us, length us, event | category | flops | bytes accessed | tf_op | source)
XLA Modules:
  0.0 87.2 jit_solution(5444816740389562879)
XLA Ops:
  0.6 0.0 copy-start.6
  0.6 0.0 copy-start.7
  0.7 0.0 copy-start.8
  0.7 1.5 %shard_map.158 = f32[5,8,128]{2,1,0:T(8,128)} custom-call(f32[3,64]{1,0:T(4,128)} %pos_ref.1, s32[1,64]{1,0:T(1,128)} %bitcast.17, s32[1,64]{1,0:T(1,128)} %bitcast.18, s32[64,64]{1,0:T(8,128)} %neighbors_ref.1), custom_call_target="tpu_custom_call" | custom-call | tf_op jit(solution)/shard_map/pallas_call | solution.py:725
  2.2 2.9 %collective-permute-start = (f32[5,8,128]{2,1,0:T(8,128)}, f32[5,8,128]{2,1,0:T(8,128)S(1)}, u32[]{:S(2)}, u32[]{:S(2)}) collective-permute-start(f32[5,8,128]{2,1,0:T(8,128)} %shard_map.158), channel_id=1, source_target_pairs={{0,256},{256,0},{1,257},{257,1},{2,258},{258,2},{3,259},{259,3},{4... | collective-permute-start | bytes 61448 | tf_op jit(solution)/shard_map/ppermute | solution.py:763
  5.0 3.4 %collective-permute-done = f32[5,8,128]{2,1,0:T(8,128)S(1)} collective-permute-done((f32[5,8,128]{2,1,0:T(8,128)}, f32[5,8,128]{2,1,0:T(8,128)S(1)}, u32[]{:S(2)}, u32[]{:S(2)}) %collective-permute-start) | collective-permute-done | bytes 20512 | tf_op jit(solution)/shard_map/ppermute | solution.py:763
  8.4 0.0 copy-start.2
  8.4 0.0 copy-start.3
  8.4 0.8 pad_maximum_fusion
  9.2 6.2 %collective-permute-start.1 = (f32[10,8,128]{2,1,0:T(8,128)S(1)}, f32[10,8,128]{2,1,0:T(8,128)S(1)}, u32[]{:S(2)}, u32[]{:S(2)}) collective-permute-start(f32[10,8,128]{2,1,0:T(8,128)S(1)} %pad_maximum_fusion), channel_id=1, source_target_pairs={{0,16},{16,32},{32,48},{48,64},{64,80},{80,96},{96,112},{112,128},... | collective-permute-start | bytes 122888 | tf_op jit(solution)/shard_map/ppermute | solution.py:765
  15.4 1.9 %collective-permute-start.2 = (f32[10,8,128]{2,1,0:T(8,128)S(1)}, f32[10,8,128]{2,1,0:T(8,128)S(1)}, u32[]{:S(2)}, u32[]{:S(2)}) collective-permute-start(f32[10,8,128]{2,1,0:T(8,128)S(1)} %pad_maximum_fusion), channel_id=1, source_target_pairs={{0,240},{16,0},{32,16},{48,32},{64,48},{80,64},{96,80},{112,96},{1... | collective-permute-start | bytes 122888 | tf_op jit(solution)/shard_map/ppermute | solution.py:766
  17.3 0.0 collective-permute-done.1
  17.3 0.0 copy-start
  17.3 0.0 copy-start.1
  17.3 0.8 constant_dynamic-update-slice_fusion.4
  18.1 4.7 %collective-permute-done.2 = f32[10,8,128]{2,1,0:T(8,128)S(1)} collective-permute-done((f32[10,8,128]{2,1,0:T(8,128)S(1)}, f32[10,8,128]{2,1,0:T(8,128)S(1)}, u32[]{:S(2)}, u32[]{:S(2)}) %collective-permute-start.2) | collective-permute-done | bytes 40992 | tf_op jit(solution)/shard_map/ppermute | solution.py:766
  22.8 8.9 %collective-permute-start.4 = (f32[22,8,128]{2,1,0:T(8,128)S(1)}, f32[22,8,128]{2,1,0:T(8,128)S(1)}, u32[]{:S(2)}, u32[]{:S(2)}) collective-permute-start(f32[22,8,128]{2,1,0:T(8,128)S(1)} %constant_dynamic-update-slice_fusion.own_ref), channel_id=1, source_target_pairs={{0,15},{1,0},{2,1},{3,2},{4,3},{5,4},{6,5},{7,6},{8,7},{9,8},{10,9... | collective-permute-start | bytes 270344 | tf_op jit(solution)/shard_map/ppermute | solution.py:769
  31.7 1.9 %collective-permute-start.3 = (f32[22,8,128]{2,1,0:T(8,128)S(1)}, f32[22,8,128]{2,1,0:T(8,128)S(1)}, u32[]{:S(2)}, u32[]{:S(2)}) collective-permute-start(f32[22,8,128]{2,1,0:T(8,128)S(1)} %constant_dynamic-update-slice_fusion.own_ref), channel_id=1, source_target_pairs={{0,1},{1,2},{2,3},{3,4},{4,5},{5,6},{6,7},{7,8},{8,9},{9,10},{10,1... | collective-permute-start | bytes 270344 | tf_op jit(solution)/shard_map/ppermute | solution.py:768
  33.6 0.0 collective-permute-done.4.high_ref
  33.7 4.5 %collective-permute-done.3.low_ref = f32[22,8,128]{2,1,0:T(8,128)S(1)} collective-permute-done((f32[22,8,128]{2,1,0:T(8,128)S(1)}, f32[22,8,128]{2,1,0:T(8,128)S(1)}, u32[]{:S(2)}, u32[]{:S(2)}) %collective-permute-start.3) | collective-permute-done | bytes 90144 | tf_op jit(solution)/shard_map/ppermute | solution.py:768
  38.2 0.0 copy-start.9
  38.2 0.0 copy-start.10
  38.2 0.0 copy-done.6
  38.2 0.0 copy-done.7
  38.2 0.0 copy-done.8
  38.2 0.0 copy-done.2
  38.2 0.0 copy-done.3
  38.2 0.0 copy-done
  38.3 0.0 copy-done.1
  38.3 0.6 copy-done.9
  38.9 0.0 copy-done.10
  38.9 0.0 copy-start.4
  38.9 0.8 copy-done.4
  39.7 0.0 copy-start.5
  39.7 0.8 copy-done.5
  40.6 28.8 %shard_map.159 = (f32[1,64]{1,0:T(1,128)}, f32[3,8,128]{2,1,0:T(8,128)S(1)}, f32[3,8,128]{2,1,0:T(8,128)S(1)}, f32[3,8,128]{2,1,0:T(8,128)S(1)}) custom-call(f32[22,8,128]{2,1,0:T(8,128)S(1)} %constant_dynamic-update-slice_fusion.own_ref, f32[22,8,128]{2,1,0:T(8,128)S(1)} %collective-permute-done.3.low_ref, ...), custom_call_target="tpu_custom_call" | custom-call | tf_op jit(solution)/shard_map/pallas_call | solution.py:712
  69.3 1.9 %collective-permute-start.5 = (f32[3,8,128]{2,1,0:T(8,128)S(1)}, f32[3,8,128]{2,1,0:T(8,128)S(1)}, u32[]{:S(2)}, u32[]{:S(2)}) collective-permute-start(f32[3,8,128]{2,1,0:T(8,128)S(1)} %get-tuple-element.8), channel_id=1, source_target_pairs={{0,1},{1,2},{2,3},{3,4},{4,5},{5,6},{6,7},{7,8},{8,9},{9,10},{10,1... | collective-permute-start | bytes 36872 | tf_op jit(solution)/shard_map/ppermute | solution.py:784
  71.3 4.6 %collective-permute-start.6 = (f32[3,8,128]{2,1,0:T(8,128)S(1)}, f32[3,8,128]{2,1,0:T(8,128)S(1)}, u32[]{:S(2)}, u32[]{:S(2)}) collective-permute-start(f32[3,8,128]{2,1,0:T(8,128)S(1)} %get-tuple-element.9), channel_id=1, source_target_pairs={{0,15},{1,0},{2,1},{3,2},{4,3},{5,4},{6,5},{7,6},{8,7},{9,8},{10,9... | collective-permute-start | bytes 36872 | tf_op jit(solution)/shard_map/ppermute | solution.py:784
  75.8 0.0 collective-permute-done.5
  75.8 0.8 collective-permute-done.6
  76.7 2.9 %collective-permute-start.7 = (f32[8,128]{1,0:T(8,128)S(1)}, f32[8,128]{1,0:T(8,128)S(1)}, u32[]{:S(2)}, u32[]{:S(2)}) collective-permute-start(f32[8,128]{1,0:T(8,128)S(1)} %get-tuple-element.10), channel_id=1, source_target_pairs={{0,16},{16,32},{32,48},{48,64},{64,80},{80,96},{96,112},{112,128},... | collective-permute-start | bytes 12296 | tf_op jit(solution)/shard_map/ppermute | solution.py:785
  79.6 1.9 %collective-permute-start.8 = (f32[8,128]{1,0:T(8,128)S(1)}, f32[8,128]{1,0:T(8,128)S(1)}, u32[]{:S(2)}, u32[]{:S(2)}) collective-permute-start(f32[8,128]{1,0:T(8,128)S(1)} %get-tuple-element.11), channel_id=1, source_target_pairs={{0,240},{16,0},{32,16},{48,32},{64,48},{80,64},{96,80},{112,96},{1... | collective-permute-start | bytes 12296 | tf_op jit(solution)/shard_map/ppermute | solution.py:786
  81.5 0.0 collective-permute-done.7
  81.5 5.1 %collective-permute-done.8 = f32[8,128]{1,0:T(8,128)S(1)} collective-permute-done((f32[8,128]{1,0:T(8,128)S(1)}, f32[8,128]{1,0:T(8,128)S(1)}, u32[]{:S(2)}, u32[]{:S(2)}) %collective-permute-start.8) | collective-permute-done | bytes 4128 | tf_op jit(solution)/shard_map/ppermute | solution.py:786
  86.6 0.6 slice_negate_fusion
  (9 shorter events, 0.0 us)
Async XLA Ops:
  0.6 37.6 %copy-start.6 = (f32[89,128]{1,0:T(8,128)S(1)}, f32[89,128]{1,0:T(8,128)}, u32[]{:S(2)}) copy-start(f32[89,128]{1,0:T(8,128)} %emb_ref.1) | copy-start | bytes 136708
  0.6 37.6 %copy-start.7 = (f32[8,64]{1,0:T(8,128)S(1)}, f32[8,64]{1,0:T(8,128)}, u32[]{:S(2)}) copy-start(f32[8,64]{1,0:T(8,128)} %fi_ref.1) | copy-start | bytes 6148
  0.7 37.6 %copy-start.8 = (f32[8,64]{1,0:T(8,128)S(1)}, f32[8,64]{1,0:T(8,128)}, u32[]{:S(2)}) copy-start(f32[8,64]{1,0:T(8,128)} %si_ref.1) | copy-start | bytes 6148
  2.2 6.2 %collective-permute-start = (f32[5,8,128]{2,1,0:T(8,128)}, f32[5,8,128]{2,1,0:T(8,128)S(1)}, u32[]{:S(2)}, u32[]{:S(2)}) collective-permute-start(f32[5,8,128]{2,1,0:T(8,128)} %shard_map.158), channel_id=1, source_target_pairs={{0,256},{256,0},{1,257},{257,1},{2,258},{258,2},{3,259},{259,3},{4... | collective-permute-start | bytes 61448 | tf_op jit(solution)/shard_map/ppermute | solution.py:763
  8.4 29.8 %copy-start.2 = (f32[128,128]{1,0:T(8,128)S(1)}, f32[128,128]{1,0:T(8,128)}, u32[]{:S(2)}) copy-start(f32[128,128]{1,0:T(8,128)} %fv_ref.1) | copy-start | bytes 196612
  8.4 29.8 %copy-start.3 = (f32[128,128]{1,0:T(8,128)S(1)}, f32[128,128]{1,0:T(8,128)}, u32[]{:S(2)}) copy-start(f32[128,128]{1,0:T(8,128)} %fq_ref.1) | copy-start | bytes 196612
  9.2 8.1 %collective-permute-start.1 = (f32[10,8,128]{2,1,0:T(8,128)S(1)}, f32[10,8,128]{2,1,0:T(8,128)S(1)}, u32[]{:S(2)}, u32[]{:S(2)}) collective-permute-start(f32[10,8,128]{2,1,0:T(8,128)S(1)} %pad_maximum_fusion), channel_id=1, source_target_pairs={{0,16},{16,32},{32,48},{48,64},{64,80},{80,96},{96,112},{112,128},... | collective-permute-start | bytes 122888 | tf_op jit(solution)/shard_map/ppermute | solution.py:765
  15.4 7.4 %collective-permute-start.2 = (f32[10,8,128]{2,1,0:T(8,128)S(1)}, f32[10,8,128]{2,1,0:T(8,128)S(1)}, u32[]{:S(2)}, u32[]{:S(2)}) collective-permute-start(f32[10,8,128]{2,1,0:T(8,128)S(1)} %pad_maximum_fusion), channel_id=1, source_target_pairs={{0,240},{16,0},{32,16},{48,32},{64,48},{80,64},{96,80},{112,96},{1... | collective-permute-start | bytes 122888 | tf_op jit(solution)/shard_map/ppermute | solution.py:766
  17.3 20.9 %copy-start = (f32[64,256]{1,0:T(8,128)S(1)}, f32[64,256]{1,0:T(8,128)}, u32[]{:S(2)}) copy-start(f32[64,256]{1,0:T(8,128)} %fo_ref.1) | copy-start | bytes 196612
  17.3 20.9 %copy-start.1 = (f32[128,128]{1,0:T(8,128)S(1)}, f32[128,128]{1,0:T(8,128)}, u32[]{:S(2)}) copy-start(f32[128,128]{1,0:T(8,128)} %fs_ref.1) | copy-start | bytes 196612
  22.8 10.9 %collective-permute-start.4 = (f32[22,8,128]{2,1,0:T(8,128)S(1)}, f32[22,8,128]{2,1,0:T(8,128)S(1)}, u32[]{:S(2)}, u32[]{:S(2)}) collective-permute-start(f32[22,8,128]{2,1,0:T(8,128)S(1)} %constant_dynamic-update-slice_fusion.own_ref), channel_id=1, source_target_pairs={{0,15},{1,0},{2,1},{3,2},{4,3},{5,4},{6,5},{7,6},{8,7},{9,8},{10,9... | collective-permute-start | bytes 270344 | tf_op jit(solution)/shard_map/ppermute | solution.py:769
  31.7 6.5 %collective-permute-start.3 = (f32[22,8,128]{2,1,0:T(8,128)S(1)}, f32[22,8,128]{2,1,0:T(8,128)S(1)}, u32[]{:S(2)}, u32[]{:S(2)}) collective-permute-start(f32[22,8,128]{2,1,0:T(8,128)S(1)} %constant_dynamic-update-slice_fusion.own_ref), channel_id=1, source_target_pairs={{0,1},{1,2},{2,3},{3,4},{4,5},{5,6},{6,7},{7,8},{8,9},{9,10},{10,1... | collective-permute-start | bytes 270344 | tf_op jit(solution)/shard_map/ppermute | solution.py:768
  38.2 0.7 copy-start.9
  38.2 0.7 copy-start.10
  38.9 0.8 copy-start.4
  39.7 0.8 copy-start.5
  69.3 6.5 %collective-permute-start.5 = (f32[3,8,128]{2,1,0:T(8,128)S(1)}, f32[3,8,128]{2,1,0:T(8,128)S(1)}, u32[]{:S(2)}, u32[]{:S(2)}) collective-permute-start(f32[3,8,128]{2,1,0:T(8,128)S(1)} %get-tuple-element.8), channel_id=1, source_target_pairs={{0,1},{1,2},{2,3},{3,4},{4,5},{5,6},{6,7},{7,8},{8,9},{9,10},{10,1... | collective-permute-start | bytes 36872 | tf_op jit(solution)/shard_map/ppermute | solution.py:784
  71.3 5.4 %collective-permute-start.6 = (f32[3,8,128]{2,1,0:T(8,128)S(1)}, f32[3,8,128]{2,1,0:T(8,128)S(1)}, u32[]{:S(2)}, u32[]{:S(2)}) collective-permute-start(f32[3,8,128]{2,1,0:T(8,128)S(1)} %get-tuple-element.9), channel_id=1, source_target_pairs={{0,15},{1,0},{2,1},{3,2},{4,3},{5,4},{6,5},{7,6},{8,7},{9,8},{10,9... | collective-permute-start | bytes 36872 | tf_op jit(solution)/shard_map/ppermute | solution.py:784
  76.7 4.9 %collective-permute-start.7 = (f32[8,128]{1,0:T(8,128)S(1)}, f32[8,128]{1,0:T(8,128)S(1)}, u32[]{:S(2)}, u32[]{:S(2)}) collective-permute-start(f32[8,128]{1,0:T(8,128)S(1)} %get-tuple-element.10), channel_id=1, source_target_pairs={{0,16},{16,32},{32,48},{48,64},{64,80},{80,96},{96,112},{112,128},... | collective-permute-start | bytes 12296 | tf_op jit(solution)/shard_map/ppermute | solution.py:785
  79.6 7.0 %collective-permute-start.8 = (f32[8,128]{1,0:T(8,128)S(1)}, f32[8,128]{1,0:T(8,128)S(1)}, u32[]{:S(2)}, u32[]{:S(2)}) collective-permute-start(f32[8,128]{1,0:T(8,128)S(1)} %get-tuple-element.11), channel_id=1, source_target_pairs={{0,240},{16,0},{32,16},{48,32},{64,48},{80,64},{96,80},{112,96},{1... | collective-permute-start | bytes 12296 | tf_op jit(solution)/shard_map/ppermute | solution.py:786

commit v5 on v4

--- a/solution.py
+++ b/solution.py
@@ -87,17 +87,17 @@
     own_ref,
     low_ref,
     high_ref,
-    emb_ref,
-    fi_ref,
-    fo_ref,
-    fs_ref,
-    fv_ref,
-    fq_ref,
-    si_ref,
-    so_ref,
-    sm_ref,
-    rf_ref,
-    rs_ref,
+    emb_hbm,
+    fi_hbm,
+    fo_hbm,
+    fs_hbm,
+    fv_hbm,
+    fq_hbm,
+    si_hbm,
+    so_hbm,
+    sm_hbm,
+    rf_hbm,
+    rs_hbm,
     energy_ref,
     up_ref,
     mid_ref,
@@ -129,7 +129,27 @@
     saved_pair_grad,
     box_acc,
     emb_pad,
+    emb_ref,
+    fi_ref,
+    fo_ref,
+    fs_ref,
+    fv_ref,
+    fq_ref,
+    si_ref,
+    so_ref,
+    sm_ref,
+    rf_ref,
+    rs_ref,
+    weight_sem,
 ):
+    sources = [emb_hbm, fi_hbm, fo_hbm, fs_hbm, fv_hbm, fq_hbm, si_hbm, so_hbm, sm_hbm, rf_hbm, rs_hbm]
+    targets = [emb_ref, fi_ref, fo_ref, fs_ref, fv_ref, fq_ref, si_ref, so_ref, sm_ref, rf_ref, rs_ref]
+    fetches = [
+        pltpu.make_async_copy(source, target, weight_sem.at[k])
+        for k, (source, target) in enumerate(zip(sources, targets))
+    ]
+    for fetch in fetches:
+        fetch.start()
     lane8 = iota((8, 128), 1)
     sub8 = iota((8, 128), 0)
     upper = lane8 >= 64
@@ -178,7 +198,7 @@
         y_zero = y_index == 0
         z_zero = z_index == 0
 
-        def fetch(comp):
+        def pick(comp):
             low = jnp.where(
                 z_zero, lanes_of(table[comp, row0], lane), lanes_of(table[comp, row0 + 1], lane)
             )
@@ -187,9 +207,9 @@
             )
             return jnp.where(y_zero, low, top)
 
-        d = [fetch(comp) - lanes_of(table[comp, row_l], lane_l) for comp in range(3)]
+        d = [pick(comp) - lanes_of(table[comp, row_l], lane_l) for comp in range(3)]
         d[0] = jnp.where(d[0] > 12.0, d[0] - 24.0, jnp.where(d[0] < -12.0, d[0] + 24.0, d[0]))
-        species = fetch(3)
+        species = pick(3)
         count = lanes_of(table[4, row_l], lane_l)
         square = d[0] * d[0] + d[1] * d[1] + d[2] * d[2] + 0.25
         slot = (lane8 & 63).astype(F32)
@@ -344,6 +364,8 @@
 
     lax.fori_loop(0, (scatters * SCATTER * TILE + 1023) // 1024, basis, 0)
 
+    for fetch in fetches:
+        fetch.wait()
     fi3 = jnp.concatenate([fi_ref[...], jnp.zeros((24, 64), F32)], axis=0)
     si3 = jnp.concatenate([si_ref[...], jnp.zeros((24, 64), F32)], axis=0)
 
@@ -707,15 +729,17 @@
         vm((96, 128), F32),
         vm((128, 128), F32),
     ]
+    scratch += [vm(w.shape, F32) for w in weights]
+    scratch.append(pltpu.SemaphoreType.DMA((len(weights),)))
     whole = pl.BlockSpec(memory_space=pltpu.VMEM)
     piece = jax.ShapeDtypeStruct((3, 8, 128), F32)
     return pl.pallas_call(
         main_kernel,
         out_shape=(jax.ShapeDtypeStruct((1, 64), F32), piece, piece, piece),
-        in_specs=[whole] * (3 + len(weights)),
+        in_specs=[whole] * 3 + [pl.BlockSpec(memory_space=pltpu.HBM)] * len(weights),
         out_specs=(whole,) * 4,
         scratch_shapes=scratch,
-        compiler_params=pltpu.CompilerParams(vmem_limit_bytes=42 * 1024 * 1024),
+        compiler_params=pltpu.CompilerParams(vmem_limit_bytes=58 * 1024 * 1024),
         interpret=INTERPRET,
     )(own, low, high, *weights)
 

time: 88.1 us -> 89.2 us (1.012)
  local copies, waits for them, and re-layouts: 3.11 us -> 0.67 us
  starting transfers between devices: 33.1 us -> 34.8 us
  waiting for transfers between devices: 18.5 us -> 19.5 us
    unnamed x28 -> x14, local copies, waits for them, and re-layouts: 3.1 us -> 0.67 us
    ppermute x1, starting transfers between devices: 2.93 us -> 4.46 us  [shards(): total = folded[1] + lax.ppermute(folded[2], 'gy', ring('gy', 1))]
  transfers between devices with their start and end apart: 9 -> 9, of which waited for: 5 -> 5; matrix products, arithmetic and copies ran while one was open for 1% -> 0% of each run, Pallas kernels for 0% -> 0%
where the time goes in v5:
time: 89.2 us; the launch traced here: 87.7 us
  starting transfers between devices  34.8 us (39%)
  Pallas kernels  29.9 us (34%)
  waiting for transfers between devices  19.5 us (22%)
  other arithmetic  2.03 us (2%)
    pallas_call x1, Pallas kernels, pair_program(): pl.pallas_call(main_kernel, out_shape=(jax.ShapeDtypeStruct((1, 64), F32)...  28.4 us
    ppermute x1, starting transfers between devices, shards(): high = lax.ppermute(layer, 'gz', ring('gz', -1))  8.93 us
    ppermute x1, starting transfers between devices, shards(): below = lax.ppermute(both, 'gy', ring('gy', 1))  6.31 us
    ppermute x1, waiting for transfers between devices, shards(): above = lax.ppermute(both, 'gy', ring('gy', -1))  5.43 us
    ppermute x1, waiting for transfers between devices, shards(): total = total + lax.ppermute(folded[0], 'gy', ring('gy', -1))  5.1 us
    ppermute x1, starting transfers between devices, shards(): lax.ppermute(down, 'gz', ring('gz', -1))  4.57 us
    ppermute x1, waiting for transfers between devices, shards(): low = lax.ppermute(layer, 'gz', ring('gz', 1))  4.53 us
    ppermute x1, starting transfers between devices, shards(): total = folded[1] + lax.ppermute(folded[2], 'gy', ring('gy', 1))  4.46 us
  transfers between devices with their start and end apart: 9, of which 5 were waited for; matrix products, arithmetic and copies ran while one was open for 0% of the time, Pallas kernels for 0%

profile of v5, /device:TPU:31, one launch (start us, length us, event | category | flops | bytes accessed | tf_op | source)
XLA Modules:
  0.0 87.7 jit_solution(2504948238502034112)
XLA Ops:
  0.6 1.5 %shard_map.158 = f32[5,8,128]{2,1,0:T(8,128)} custom-call(f32[3,64]{1,0:T(4,128)} %pos_ref.1, s32[1,64]{1,0:T(1,128)} %bitcast.15, s32[1,64]{1,0:T(1,128)} %bitcast.16, s32[64,64]{1,0:T(8,128)} %neighbors_ref.1), custom_call_target="tpu_custom_call" | custom-call | tf_op jit(solution)/shard_map/pallas_call | solution.py:749
  2.1 2.9 %collective-permute-start = (f32[5,8,128]{2,1,0:T(8,128)}, f32[5,8,128]{2,1,0:T(8,128)S(1)}, u32[]{:S(2)}, u32[]{:S(2)}) collective-permute-start(f32[5,8,128]{2,1,0:T(8,128)} %shard_map.158), channel_id=1, source_target_pairs={{0,256},{256,0},{1,257},{257,1},{2,258},{258,2},{3,259},{259,3},{4... | collective-permute-start | bytes 61448 | tf_op jit(solution)/shard_map/ppermute | solution.py:787
  5.0 3.4 %collective-permute-done = f32[5,8,128]{2,1,0:T(8,128)S(1)} collective-permute-done((f32[5,8,128]{2,1,0:T(8,128)}, f32[5,8,128]{2,1,0:T(8,128)S(1)}, u32[]{:S(2)}, u32[]{:S(2)}) %collective-permute-start) | collective-permute-done | bytes 20512 | tf_op jit(solution)/shard_map/ppermute | solution.py:787
  8.4 0.7 pad_maximum_fusion
  9.1 0.0 copy-start
  9.1 6.3 %collective-permute-start.1 = (f32[10,8,128]{2,1,0:T(8,128)S(1)}, f32[10,8,128]{2,1,0:T(8,128)S(1)}, u32[]{:S(2)}, u32[]{:S(2)}) collective-permute-start(f32[10,8,128]{2,1,0:T(8,128)S(1)} %pad_maximum_fusion), channel_id=1, source_target_pairs={{0,16},{16,32},{32,48},{48,64},{64,80},{80,96},{96,112},{112,128},... | collective-permute-start | bytes 122888 | tf_op jit(solution)/shard_map/ppermute | solution.py:789
  15.4 1.9 %collective-permute-start.2 = (f32[10,8,128]{2,1,0:T(8,128)S(1)}, f32[10,8,128]{2,1,0:T(8,128)S(1)}, u32[]{:S(2)}, u32[]{:S(2)}) collective-permute-start(f32[10,8,128]{2,1,0:T(8,128)S(1)} %pad_maximum_fusion), channel_id=1, source_target_pairs={{0,240},{16,0},{32,16},{48,32},{64,48},{80,64},{96,80},{112,96},{1... | collective-permute-start | bytes 122888 | tf_op jit(solution)/shard_map/ppermute | solution.py:790
  17.3 0.0 collective-permute-done.1
  17.4 0.0 copy-done
  17.4 5.4 %collective-permute-done.2 = f32[10,8,128]{2,1,0:T(8,128)S(1)} collective-permute-done((f32[10,8,128]{2,1,0:T(8,128)S(1)}, f32[10,8,128]{2,1,0:T(8,128)S(1)}, u32[]{:S(2)}, u32[]{:S(2)}) %collective-permute-start.2) | collective-permute-done | bytes 40992 | tf_op jit(solution)/shard_map/ppermute | solution.py:790
  22.8 0.0 copy-start.1
  22.8 8.9 %collective-permute-start.4 = (f32[22,8,128]{2,1,0:T(8,128)S(1)}, f32[22,8,128]{2,1,0:T(8,128)S(1)}, u32[]{:S(2)}, u32[]{:S(2)}) collective-permute-start(f32[22,8,128]{2,1,0:T(8,128)S(1)} %constant_dynamic-update-slice_fusion.own_ref), channel_id=1, source_target_pairs={{0,15},{1,0},{2,1},{3,2},{4,3},{5,4},{6,5},{7,6},{8,7},{9,8},{10,9... | collective-permute-start | bytes 270344 | tf_op jit(solution)/shard_map/ppermute | solution.py:793
  31.8 1.9 %collective-permute-start.3 = (f32[22,8,128]{2,1,0:T(8,128)S(1)}, f32[22,8,128]{2,1,0:T(8,128)S(1)}, u32[]{:S(2)}, u32[]{:S(2)}) collective-permute-start(f32[22,8,128]{2,1,0:T(8,128)S(1)} %constant_dynamic-update-slice_fusion.own_ref), channel_id=1, source_target_pairs={{0,1},{1,2},{2,3},{3,4},{4,5},{5,6},{6,7},{7,8},{8,9},{9,10},{10,1... | collective-permute-start | bytes 270344 | tf_op jit(solution)/shard_map/ppermute | solution.py:792
  33.7 0.0 collective-permute-done.4.high_ref
  33.7 0.0 copy-start.2
  33.7 4.5 %collective-permute-done.3.low_ref = f32[22,8,128]{2,1,0:T(8,128)S(1)} collective-permute-done((f32[22,8,128]{2,1,0:T(8,128)S(1)}, f32[22,8,128]{2,1,0:T(8,128)S(1)}, u32[]{:S(2)}, u32[]{:S(2)}) %collective-permute-start.3) | collective-permute-done | bytes 90144 | tf_op jit(solution)/shard_map/ppermute | solution.py:792
  38.3 0.0 copy-start.3
  38.3 0.0 copy-done.1
  38.3 0.0 copy-done.2
  38.3 0.6 copy-done.3
  38.9 28.4 %shard_map.159 = (f32[1,64]{1,0:T(1,128)}, f32[3,8,128]{2,1,0:T(8,128)}, f32[3,8,128]{2,1,0:T(8,128)}, f32[3,8,128]{2,1,0:T(8,128)}) custom-call(f32[22,8,128]{2,1,0:T(8,128)} %copy-done.1, f32[22,8,128]{2,1,0:T(8,128)} %copy-done.3, f32[22,8,128]{2,1,0:T(8,128)} %copy-done.2, f32[89,128]{1,0:T(8,128)} %emb_hbm.1, f32[8,64]{1,0:T(8,128)} %fi_hbm.1, ...), custom_call_target="tpu_custom_call" | custom-call | tf_op jit(solution)/shard_map/pallas_call | solution.py:736
  67.3 1.9 %collective-permute-start.5 = (f32[3,8,128]{2,1,0:T(8,128)}, f32[3,8,128]{2,1,0:T(8,128)S(1)}, u32[]{:S(2)}, u32[]{:S(2)}) collective-permute-start(f32[3,8,128]{2,1,0:T(8,128)} %get-tuple-element.8), channel_id=1, source_target_pairs={{0,1},{1,2},{2,3},{3,4},{4,5},{5,6},{6,7},{7,8},{8,9},{9,10},{10,1... | collective-permute-start | bytes 36872 | tf_op jit(solution)/shard_map/ppermute | solution.py:808
  69.2 4.6 %collective-permute-start.6 = (f32[3,8,128]{2,1,0:T(8,128)}, f32[3,8,128]{2,1,0:T(8,128)S(1)}, u32[]{:S(2)}, u32[]{:S(2)}) collective-permute-start(f32[3,8,128]{2,1,0:T(8,128)} %get-tuple-element.9), channel_id=1, source_target_pairs={{0,15},{1,0},{2,1},{3,2},{4,3},{5,4},{6,5},{7,6},{8,7},{9,8},{10,9... | collective-permute-start | bytes 36872 | tf_op jit(solution)/shard_map/ppermute | solution.py:808
  73.8 0.0 collective-permute-done.5
  73.8 1.0 %collective-permute-done.6 = f32[3,8,128]{2,1,0:T(8,128)S(1)} collective-permute-done((f32[3,8,128]{2,1,0:T(8,128)}, f32[3,8,128]{2,1,0:T(8,128)S(1)}, u32[]{:S(2)}, u32[]{:S(2)}) %collective-permute-start.6) | collective-permute-done | bytes 12320 | tf_op jit(solution)/shard_map/ppermute | solution.py:808
  74.8 0.7 add_add_fusion
  75.6 4.5 %collective-permute-start.7 = (f32[8,128]{1,0:T(8,128)S(1)}, f32[8,128]{1,0:T(8,128)S(1)}, u32[]{:S(2)}, u32[]{:S(2)}) collective-permute-start(f32[8,128]{1,0:T(8,128)S(1)} %get-tuple-element.10), channel_id=1, source_target_pairs={{0,16},{16,32},{32,48},{48,64},{64,80},{80,96},{96,112},{112,128},... | collective-permute-start | bytes 12296 | tf_op jit(solution)/shard_map/ppermute | solution.py:809
  80.0 1.9 %collective-permute-start.8 = (f32[8,128]{1,0:T(8,128)S(1)}, f32[8,128]{1,0:T(8,128)S(1)}, u32[]{:S(2)}, u32[]{:S(2)}) collective-permute-start(f32[8,128]{1,0:T(8,128)S(1)} %get-tuple-element.11), channel_id=1, source_target_pairs={{0,240},{16,0},{32,16},{48,32},{64,48},{80,64},{96,80},{112,96},{1... | collective-permute-start | bytes 12296 | tf_op jit(solution)/shard_map/ppermute | solution.py:810
  82.0 0.0 collective-permute-done.7
  82.0 5.1 %collective-permute-done.8 = f32[8,128]{1,0:T(8,128)S(1)} collective-permute-done((f32[8,128]{1,0:T(8,128)S(1)}, f32[8,128]{1,0:T(8,128)S(1)}, u32[]{:S(2)}, u32[]{:S(2)}) %collective-permute-start.8) | collective-permute-done | bytes 4128 | tf_op jit(solution)/shard_map/ppermute | solution.py:810
  87.1 0.6 slice_negate_fusion
  (9 shorter events, 0.0 us)
Async XLA Ops:
  2.1 6.2 %collective-permute-start = (f32[5,8,128]{2,1,0:T(8,128)}, f32[5,8,128]{2,1,0:T(8,128)S(1)}, u32[]{:S(2)}, u32[]{:S(2)}) collective-permute-start(f32[5,8,128]{2,1,0:T(8,128)} %shard_map.158), channel_id=1, source_target_pairs={{0,256},{256,0},{1,257},{257,1},{2,258},{258,2},{3,259},{259,3},{4... | collective-permute-start | bytes 61448 | tf_op jit(solution)/shard_map/ppermute | solution.py:787
  9.1 8.3 %copy-start = (f32[5,8,128]{2,1,0:T(8,128)S(1)}, f32[5,8,128]{2,1,0:T(8,128)}, u32[]{:S(2)}) copy-start(f32[5,8,128]{2,1,0:T(8,128)} %shard_map.158) | copy-start | bytes 61444
  9.1 8.2 %collective-permute-start.1 = (f32[10,8,128]{2,1,0:T(8,128)S(1)}, f32[10,8,128]{2,1,0:T(8,128)S(1)}, u32[]{:S(2)}, u32[]{:S(2)}) collective-permute-start(f32[10,8,128]{2,1,0:T(8,128)S(1)} %pad_maximum_fusion), channel_id=1, source_target_pairs={{0,16},{16,32},{32,48},{48,64},{64,80},{80,96},{96,112},{112,128},... | collective-permute-start | bytes 122888 | tf_op jit(solution)/shard_map/ppermute | solution.py:789
  15.4 7.4 %collective-permute-start.2 = (f32[10,8,128]{2,1,0:T(8,128)S(1)}, f32[10,8,128]{2,1,0:T(8,128)S(1)}, u32[]{:S(2)}, u32[]{:S(2)}) collective-permute-start(f32[10,8,128]{2,1,0:T(8,128)S(1)} %pad_maximum_fusion), channel_id=1, source_target_pairs={{0,240},{16,0},{32,16},{48,32},{64,48},{80,64},{96,80},{112,96},{1... | collective-permute-start | bytes 122888 | tf_op jit(solution)/shard_map/ppermute | solution.py:790
  22.8 15.4 %copy-start.1 = (f32[22,8,128]{2,1,0:T(8,128)}, f32[22,8,128]{2,1,0:T(8,128)S(1)}, u32[]{:S(2)}) copy-start(f32[22,8,128]{2,1,0:T(8,128)S(1)} %constant_dynamic-update-slice_fusion.own_ref) | copy-start | bytes 270340
  22.8 10.9 %collective-permute-start.4 = (f32[22,8,128]{2,1,0:T(8,128)S(1)}, f32[22,8,128]{2,1,0:T(8,128)S(1)}, u32[]{:S(2)}, u32[]{:S(2)}) collective-permute-start(f32[22,8,128]{2,1,0:T(8,128)S(1)} %constant_dynamic-update-slice_fusion.own_ref), channel_id=1, source_target_pairs={{0,15},{1,0},{2,1},{3,2},{4,3},{5,4},{6,5},{7,6},{8,7},{9,8},{10,9... | collective-permute-start | bytes 270344 | tf_op jit(solution)/shard_map/ppermute | solution.py:793
  31.8 6.5 %collective-permute-start.3 = (f32[22,8,128]{2,1,0:T(8,128)S(1)}, f32[22,8,128]{2,1,0:T(8,128)S(1)}, u32[]{:S(2)}, u32[]{:S(2)}) collective-permute-start(f32[22,8,128]{2,1,0:T(8,128)S(1)} %constant_dynamic-update-slice_fusion.own_ref), channel_id=1, source_target_pairs={{0,1},{1,2},{2,3},{3,4},{4,5},{5,6},{6,7},{7,8},{8,9},{9,10},{10,1... | collective-permute-start | bytes 270344 | tf_op jit(solution)/shard_map/ppermute | solution.py:792
  33.7 4.6 %copy-start.2 = (f32[22,8,128]{2,1,0:T(8,128)}, f32[22,8,128]{2,1,0:T(8,128)S(1)}, u32[]{:S(2)}) copy-start(f32[22,8,128]{2,1,0:T(8,128)S(1)} %collective-permute-done.4.high_ref) | copy-start | bytes 270340
  38.3 0.6 copy-start.3
  67.3 6.5 %collective-permute-start.5 = (f32[3,8,128]{2,1,0:T(8,128)}, f32[3,8,128]{2,1,0:T(8,128)S(1)}, u32[]{:S(2)}, u32[]{:S(2)}) collective-permute-start(f32[3,8,128]{2,1,0:T(8,128)} %get-tuple-element.8), channel_id=1, source_target_pairs={{0,1},{1,2},{2,3},{3,4},{4,5},{5,6},{6,7},{7,8},{8,9},{9,10},{10,1... | collective-permute-start | bytes 36872 | tf_op jit(solution)/shard_map/ppermute | solution.py:808
  69.2 5.6 %collective-permute-start.6 = (f32[3,8,128]{2,1,0:T(8,128)}, f32[3,8,128]{2,1,0:T(8,128)S(1)}, u32[]{:S(2)}, u32[]{:S(2)}) collective-permute-start(f32[3,8,128]{2,1,0:T(8,128)} %get-tuple-element.9), channel_id=1, source_target_pairs={{0,15},{1,0},{2,1},{3,2},{4,3},{5,4},{6,5},{7,6},{8,7},{9,8},{10,9... | collective-permute-start | bytes 36872 | tf_op jit(solution)/shard_map/ppermute | solution.py:808
  75.6 6.4 %collective-permute-start.7 = (f32[8,128]{1,0:T(8,128)S(1)}, f32[8,128]{1,0:T(8,128)S(1)}, u32[]{:S(2)}, u32[]{:S(2)}) collective-permute-start(f32[8,128]{1,0:T(8,128)S(1)} %get-tuple-element.10), channel_id=1, source_target_pairs={{0,16},{16,32},{32,48},{48,64},{64,80},{80,96},{96,112},{112,128},... | collective-permute-start | bytes 12296 | tf_op jit(solution)/shard_map/ppermute | solution.py:809
  80.0 7.0 %collective-permute-start.8 = (f32[8,128]{1,0:T(8,128)S(1)}, f32[8,128]{1,0:T(8,128)S(1)}, u32[]{:S(2)}, u32[]{:S(2)}) collective-permute-start(f32[8,128]{1,0:T(8,128)S(1)} %get-tuple-element.11), channel_id=1, source_target_pairs={{0,240},{16,0},{32,16},{48,32},{64,48},{80,64},{96,80},{112,96},{1... | collective-permute-start | bytes 12296 | tf_op jit(solution)/shard_map/ppermute | solution.py:810
